TPU v7x, 128 devices: a whole 4x4x4 slice. The times are simulated.
128 devices in a mesh: dp: 32 (over y, x, z_hi), mp: 4 (over z_lo, core).
Axes of the slice: x: 4, y: 4, z: 4 (z_hi: 2, z_lo: 2; z = z_hi * 2 + z_lo), core: 2. Of those that a mesh axis runs over, the one named last changes fastest.
Arguments:
- image_in: bfloat16 [8192, 1408], P('dp'), may hold values from -8 to 8
- text_in: bfloat16 [8192, 1408], P('dp'), may hold values from -8 to 8
- image_gain: float32 [1408], replicated, may hold values from 0.25 to 1.75
- image_up: bfloat16 [1408, 6144], P(None, 'mp'), may hold values from -0.15625 to 0.15625
- image_down: bfloat16 [6144, 1408], P('mp'), may hold values from -0.078125 to 0.078125
- image_final: float32 [1408], replicated, may hold values from 0.25 to 1.75
- text_gain: float32 [1408], replicated, may hold values from 0.25 to 1.75
- text_up: bfloat16 [1408, 6144], P(None, 'mp'), may hold values from -0.15625 to 0.15625
- text_down: bfloat16 [6144, 1408], P('mp'), may hold values from -0.078125 to 0.078125
- text_final: float32 [1408], replicated, may hold values from 0.25 to 1.75
Outputs:
- image_grad: float32 [8192, 1408], P('dp')
- text_grad: float32 [8192, 1408], P('dp')
- row_loss: float32 [8192], P('dp')
All inputs are finite; a program needn't handle non-finite values.
Results may differ from a plain program's by a relative error of at most 0.015.
Values may be sent and summed in bfloat16 or wider, within the bound.
No kernel may reach another device: no remote copies, remote signals or barrier semaphores. Data moves between devices by JAX's collectives and lax.ppermute only.
A program may use at most 128 MiB of HBM per device.

v0:
```python
import functools

import jax
import jax.numpy as jnp
import numpy as np
from jax import lax
from jax.experimental import pallas as pl
from jax.experimental.pallas import tpu as pltpu
from jax.sharding import PartitionSpec as P

epsilon = 1e-06
logit_scale = 10.0
logit_bias = -1.0
loss_scale = 32768.0
total_rows = 8192.0

WIDTH = 1408
HIDDEN = 1536
PACKED = 1536
BLOCK = 64
FF_STEP = 256
AXES = ("dp", "mp")
DIMS = (4, 4, 2, 2, 2)
bf16 = jnp.bfloat16
f32 = jnp.float32


def routes(move):
    pairs = []
    for source in range(128):
        y, x, z_hi, z_lo, core = (int(v) for v in np.unravel_index(source, DIMS))
        y, x, z, core = move(y, x, 2 * z_hi + z_lo, core)
        y, x, z = y % 4, x % 4, z % 4
        target = np.ravel_multi_index((y, x, z // 2, z % 2, core), DIMS)
        pairs.append((source, int(target)))
    return pairs


def first_ring(steps):
    return routes(lambda y, x, z, c: (y, x + steps, z, c) if c == 0 else (y + steps, x, z, c))


def second_ring(steps):
    return routes(lambda y, x, z, c: (y + steps, x, z, c) if c == 0 else (y, x + steps, z, c))


SIBLING = routes(lambda y, x, z, c: (y, x, z, 1 - c))
Z_PAIR = routes(lambda y, x, z, c: (y, x, z ^ 1, c))
Z_OUT = routes(lambda y, x, z, c: (y, x, z + 1 - 2 * c, c))
Z_BACK = routes(lambda y, x, z, c: (y, x, z - 1 + 2 * c, c))


def send(value, pairs):
    return lax.ppermute(value, AXES, pairs)


def contract(a, b, left, right):
    return lax.dot_general(a, b, (((left,), (right,)), ((), ())), preferred_element_type=f32)


def call(body, outs, args, scalar=None, flops=1 << 20, **options):
    specs = [pl.BlockSpec(memory_space=pltpu.VMEM) for _ in args]
    if scalar is not None:
        specs = [pl.BlockSpec(memory_space=pltpu.SMEM)] + specs
        args = [scalar] + list(args)
    moved = sum(int(np.prod(o.shape)) * o.dtype.itemsize for o in outs)
    moved += sum(int(np.prod(a.shape)) * a.dtype.itemsize for a in args)
    return pl.pallas_call(
        body,
        out_shape=outs,
        in_specs=specs,
        out_specs=[pl.BlockSpec(memory_space=pltpu.VMEM) for _ in outs],
        compiler_params=pltpu.CompilerParams(vmem_limit_bytes=30 << 20),
        cost_estimate=pl.CostEstimate(flops=flops, bytes_accessed=moved, transcendentals=0),
        **options,
    )(*args)


def shape(rows, columns, kind):
    return jax.ShapeDtypeStruct((rows, columns), kind)


def centred(values):
    center = jnp.mean(values, axis=-1, keepdims=True)
    shifted = values - center
    variance = jnp.mean(shifted * shifted, axis=-1, keepdims=True)
    inverse = lax.rsqrt(variance + epsilon)
    return shifted * inverse, inverse


def centred_back(unit, inverse, d_unit):
    along = jnp.mean(d_unit * unit, axis=-1, keepdims=True)
    return inverse * (d_unit - jnp.mean(d_unit, axis=-1, keepdims=True) - unit * along)


def pack(out_ref, start, values, loss):
    rows = values.shape[0]
    column = lax.broadcasted_iota(jnp.int32, (rows, 128), 1)
    high = loss.astype(bf16).astype(f32)
    tail = jnp.where(column == 0, high, jnp.where(column == 1, loss - high, 0.0))
    out_ref[pl.ds(start, rows), 0:WIDTH] = values.astype(out_ref.dtype)
    out_ref[pl.ds(start, rows), WIDTH:PACKED] = tail.astype(out_ref.dtype)


def loss_of(tail):
    return jnp.sum(tail.astype(f32), axis=-1, keepdims=True)


SLOPE = 0.7978845608028654
CUBIC = 0.044715


def forward_body(mine, x_ref, gain_ref, up_ref, down_ref, pre_ref, keep_ref, send_ref, norm, total):
    step = pl.program_id(0)

    @pl.when(step == 0)
    def _():
        for place in range(4):
            start = pl.multiple_of((place ^ mine[0]) * BLOCK, BLOCK)
            unit, _ = centred(x_ref[pl.ds(start, BLOCK), :].astype(f32))
            norm[place * BLOCK : (place + 1) * BLOCK, :] = (unit * gain_ref[...]).astype(bf16)

    pre = contract(norm[...], up_ref[...], 1, 0)
    pre_ref[...] = pre
    act = 0.5 * pre * (1.0 + jnp.tanh(SLOPE * (pre + CUBIC * pre * pre * pre)))
    part = contract(act.astype(bf16), down_ref[...], 1, 0)

    @pl.when(step == 0)
    def _():
        total[...] = part

    @pl.when(step > 0)
    def _():
        total[...] += part

    @pl.when(step == pl.num_programs(0) - 1)
    def _():
        keep_ref[...] = total[0:128, :]
        send_ref[...] = total[128:256, :].astype(bf16)


def tower_forward(mine, tokens, gain, up, down):
    steps = HIDDEN // FF_STEP
    fixed = lambda i, m: (0, 0)
    return pl.pallas_call(
        forward_body,
        grid_spec=pltpu.PrefetchScalarGridSpec(
            num_scalar_prefetch=1,
            grid=(steps,),
            in_specs=[
                pl.BlockSpec((256, WIDTH), fixed),
                pl.BlockSpec((1, WIDTH), fixed),
                pl.BlockSpec((WIDTH, FF_STEP), lambda i, m: (0, i)),
                pl.BlockSpec((FF_STEP, WIDTH), lambda i, m: (i, 0)),
            ],
            out_specs=[
                pl.BlockSpec((256, FF_STEP), lambda i, m: (0, i)),
                pl.BlockSpec((128, WIDTH), fixed),
                pl.BlockSpec((128, WIDTH), fixed),
            ],
            scratch_shapes=[pltpu.VMEM((256, WIDTH), bf16), pltpu.VMEM((256, WIDTH), f32)],
        ),
        out_shape=[shape(256, HIDDEN, f32), shape(128, WIDTH, f32), shape(128, WIDTH, bf16)],
        compiler_params=pltpu.CompilerParams(vmem_limit_bytes=30 << 20),
        cost_estimate=pl.CostEstimate(
            flops=4 * 256 * WIDTH * HIDDEN, bytes_accessed=12 << 20, transcendentals=256 * HIDDEN
        ),
    )(mine, tokens, gain.reshape(1, WIDTH), up, down)


def backward_body(r0, r1, r2, r3, pre_ref, up_ref, down_ref, keep_ref, send_ref, given, total):
    step = pl.program_id(0)

    @pl.when(step == 0)
    def _():
        for place, ref in enumerate((r0, r1, r2, r3)):
            given[place * BLOCK : (place + 1) * BLOCK, :] = ref[:, 0:WIDTH]

    d_act = contract(given[...], down_ref[...], 1, 1)
    pre = pre_ref[...]
    square = pre * pre
    curve = jnp.tanh(SLOPE * pre * (1.0 + CUBIC * square))
    slope = 0.5 * (1.0 + curve) + 0.5 * pre * (1.0 - curve * curve) * (
        SLOPE * (1.0 + 3.0 * CUBIC * square)
    )
    part = contract((d_act * slope).astype(bf16), up_ref[...], 1, 1)

    @pl.when(step == 0)
    def _():
        total[...] = part

    @pl.when(step > 0)
    def _():
        total[...] += part

    @pl.when(step == pl.num_programs(0) - 1)
    def _():
        keep_ref[...] = total[0:128, :]
        send_ref[...] = total[128:256, :].astype(bf16)


def tower_backward(blocks, pre, up, down):
    steps = HIDDEN // FF_STEP
    fixed = lambda i: (0, 0)
    return pl.pallas_call(
        backward_body,
        grid=(steps,),
        in_specs=[pl.BlockSpec(block.shape, fixed) for block in blocks]
        + [
            pl.BlockSpec((256, FF_STEP), lambda i: (0, i)),
            pl.BlockSpec((WIDTH, FF_STEP), lambda i: (0, i)),
            pl.BlockSpec((FF_STEP, WIDTH), lambda i: (i, 0)),
        ],
        out_specs=[pl.BlockSpec((128, WIDTH), fixed), pl.BlockSpec((128, WIDTH), fixed)],
        scratch_shapes=[pltpu.VMEM((256, WIDTH), bf16), pltpu.VMEM((256, WIDTH), f32)],
        out_shape=[shape(128, WIDTH, f32), shape(128, WIDTH, bf16)],
        compiler_params=pltpu.CompilerParams(vmem_limit_bytes=30 << 20),
        cost_estimate=pl.CostEstimate(
            flops=4 * 256 * WIDTH * HIDDEN, bytes_accessed=12 << 20, transcendentals=256 * HIDDEN
        ),
    )(*blocks, pre, up, down)


def halve_body(keep_ref, got_ref, own_ref, send_ref):
    own_ref[...] = keep_ref[0:BLOCK, :] + got_ref[0:BLOCK, :].astype(f32)
    send_ref[...] = (keep_ref[BLOCK:128, :] + got_ref[BLOCK:128, :].astype(f32)).astype(bf16)


def embed_body(mine, own_ref, got_ref, x_ref, gain_ref, resid_ref, z_ref):
    start = pl.multiple_of(mine[0] * BLOCK, BLOCK)
    resid = own_ref[...] + got_ref[...].astype(f32) + x_ref[pl.ds(start, BLOCK), :].astype(f32)
    resid_ref[...] = resid
    normed = centred(resid)[0] * gain_ref[...]
    scale = lax.rsqrt(jnp.sum(normed * normed, axis=-1, keepdims=True) + epsilon)
    z_ref[...] = (normed * scale).astype(bf16)


def scattered_embed(mine, keep, sent, tokens, final_gain):
    got = send(sent, SIBLING)
    own, sent = call(halve_body, [shape(BLOCK, WIDTH, f32), shape(BLOCK, WIDTH, bf16)], [keep, got])
    got = send(sent, Z_PAIR)
    return call(
        embed_body,
        [shape(BLOCK, WIDTH, f32), shape(BLOCK, WIDTH, bf16)],
        [own, got, tokens, final_gain.reshape(1, WIDTH)],
        scalar=mine,
    )


def stack_body(first_ref, second_ref, out_ref):
    out_ref[0:BLOCK, :] = first_ref[...]
    out_ref[BLOCK:128, :] = second_ref[...]


def stacked(first, second):
    return call(stack_body, [shape(128, WIDTH, bf16)], [first, second])[0]


def gather_plane(own):
    before = send(own, first_ring(1))
    across = send(own, first_ring(2))
    after = send(own, first_ring(-1))
    near = (stacked(own, before), stacked(after, across))
    left = [send(near[0], second_ring(1)), None]
    right = [None, send(near[1], second_ring(-1))]
    left[1] = send(near[1], second_ring(1))
    right[0] = send(near[0], second_ring(-1))
    far = (send(left[0], second_ring(1)), send(right[1], second_ring(-1)))
    return near, left, right, far


def gather_column(own):
    ahead = send(own, Z_OUT)
    behind = send(own, Z_BACK)
    across = send(ahead, Z_OUT)
    blocks = [own, ahead, behind, across]
    return blocks + [send(block, SIBLING) for block in blocks]


def pair_chunk(images, texts, has_own):
    logits = logit_scale * contract(images, texts, 1, 1) + logit_bias
    grown = jnp.exp(logits)
    softplus = jnp.log1p(grown)
    share = grown / (1.0 + grown)
    if has_own:
        row = lax.broadcasted_iota(jnp.int32, logits.shape, 0)
        column = lax.broadcasted_iota(jnp.int32, logits.shape, 1)
        matched = (row == column) & (row < BLOCK)
        softplus = jnp.where(matched, softplus - logits, softplus)
        share = jnp.where(matched, share - 1.0, share)
    loss = jnp.sum(softplus, axis=1, keepdims=True) / total_rows
    pair_grad = (loss_scale / total_rows * share).astype(bf16)
    to_image = logit_scale * contract(pair_grad, texts, 1, 0)
    to_text = logit_scale * contract(pair_grad, images, 0, 0)
    return loss, to_image, to_text


def early_body(*refs):
    image_refs, refs = refs[:8], refs[8:]
    near0, near1, left0, left1, right0, right1 = refs[:6]
    image_ref, total_ref, loss_ref, near_ref, left_keep, left_send, right_send, right_keep = refs[6:14]
    texts = refs[14]
    for place, ref in enumerate(image_refs):
        image_ref[place * BLOCK : (place + 1) * BLOCK, :] = ref[...]
    losses = 0.0
    for chunk, parts in enumerate(((near0, near1), (left0, left1), (right0, right1))):
        texts[0:128, :] = parts[0][...]
        texts[128:256, :] = parts[1][...]
        loss, to_image, to_text = pair_chunk(image_ref[...], texts[...], chunk == 0)
        losses = losses + loss
        if chunk == 0:
            total_ref[...] = to_image
            near_ref[...] = to_text
        else:
            total_ref[...] += to_image
            halves = (left_keep, left_send) if chunk == 1 else (right_send, right_keep)
            halves[0][...] = to_text[0:128, :].astype(halves[0].dtype)
            halves[1][...] = to_text[128:256, :].astype(halves[1].dtype)
    loss_ref[...] = jnp.broadcast_to(losses, (512, 128))


def late_body(image_ref, total_ref, loss_ref, far0, far1, far0_ref, far1_ref, keep_ref, send_ref, texts):
    texts[0:128, :] = far0[...]
    texts[128:256, :] = far1[...]
    loss, to_image, to_text = pair_chunk(image_ref[...], texts[...], False)
    far0_ref[...] = to_text[0:128, :].astype(bf16)
    far1_ref[...] = to_text[128:256, :].astype(bf16)
    loss = loss + loss_ref[:, 0:1]
    to_image = to_image + total_ref[...]
    pack(keep_ref, 0, to_image[0:256, :], loss[0:256, :])
    pack(send_ref, 0, to_image[256:512, :], loss[256:512, :])


def pair_tile(images, near, left, right, far):
    half32, half16 = shape(128, WIDTH, f32), shape(128, WIDTH, bf16)
    image, total, loss, near_grad, left_keep, left_send, right_send, right_keep = call(
        early_body,
        [shape(512, WIDTH, bf16), shape(512, WIDTH, f32), shape(512, 128, f32)]
        + [shape(256, WIDTH, f32), half32, half16, half16, half32],
        [*images, *near, *left, *right],
        flops=6 * 512 * 768 * WIDTH,
        scratch_shapes=[pltpu.VMEM((256, WIDTH), bf16)],
    )
    far0, far1, image_keep, image_send = call(
        late_body,
        [half16, half16, shape(256, PACKED, f32), shape(256, PACKED, bf16)],
        [image, total, loss, *far],
        flops=6 * 512 * 256 * WIDTH,
        scratch_shapes=[pltpu.VMEM((256, WIDTH), bf16)],
    )
    return near_grad, left_keep, left_send, right_send, right_keep, far0, far1, image_keep, image_send


def joined_body(keep_ref, got_ref, out_ref):
    out_ref[...] = (keep_ref[...] + got_ref[...].astype(f32)).astype(out_ref.dtype)


def near_body(near_ref, l0, l1, r0, r1, own_ref, before_ref, after_ref, across_ref):
    first = near_ref[0:128, :] + l0[...].astype(f32) + r0[...].astype(f32)
    second = near_ref[128:256, :] + l1[...].astype(f32) + r1[...].astype(f32)
    own_ref[...] = first[0:BLOCK, :]
    before_ref[...] = first[BLOCK:128, :].astype(bf16)
    after_ref[...] = second[0:BLOCK, :].astype(bf16)
    across_ref[...] = second[BLOCK:128, :].astype(bf16)


def head_back(resid, gain, d_embed):
    unit, inverse = centred(resid)
    normed = unit * gain
    scale = lax.rsqrt(jnp.sum(normed * normed, axis=-1, keepdims=True) + epsilon)
    along = jnp.sum(d_embed * normed, axis=-1, keepdims=True)
    d_normed = scale * d_embed - normed * (scale * scale * scale * along)
    return centred_back(unit, inverse, d_normed * gain)


def text_head_body(own_ref, before_ref, after_ref, across_ref, resid_ref, gain_ref, out_ref):
    d_embed = own_ref[...] + before_ref[...].astype(f32)
    d_embed = d_embed + after_ref[...].astype(f32) + across_ref[...].astype(f32)
    out_ref[...] = head_back(resid_ref[...], gain_ref[...], d_embed).astype(bf16)


def scatter_plane(grads, resid, gain):
    near, left_keep, left_send, right_send, right_keep, far0, far1 = grads
    half16, block16 = shape(128, WIDTH, bf16), shape(BLOCK, WIDTH, bf16)
    l1 = send(left_send, second_ring(-1))
    r0 = send(right_send, second_ring(1))
    got0 = send(far0, second_ring(-1))
    got1 = send(far1, second_ring(1))
    l0 = send(call(joined_body, [half16], [left_keep, got0])[0], second_ring(-1))
    r1 = send(call(joined_body, [half16], [right_keep, got1])[0], second_ring(1))
    own, before, after, across = call(
        near_body, [shape(BLOCK, WIDTH, f32), block16, block16, block16], [near, l0, l1, r0, r1]
    )
    across = send(across, first_ring(2))
    before = send(before, first_ring(-1))
    after = send(after, first_ring(1))
    return call(text_head_body, [block16], [own, before, after, across, resid, gain.reshape(1, WIDTH)])[0]


def add_packed(values, loss, ref, start):
    rows = values.shape[0]
    return (
        values + ref[start : start + rows, 0:WIDTH].astype(f32),
        loss + loss_of(ref[start : start + rows, WIDTH:PACKED]),
    )


def packed_rows(ref, start, rows):
    return ref[start : start + rows, 0:WIDTH], loss_of(ref[start : start + rows, WIDTH:PACKED])


def column_first_body(keep_ref, got_ref, near_ref, across_ref):
    for place in range(3):
        values, loss = packed_rows(keep_ref, place * BLOCK, BLOCK)
        pack(near_ref, place * BLOCK, *add_packed(values, loss, got_ref, place * BLOCK))
    values, loss = packed_rows(keep_ref, 3 * BLOCK, BLOCK)
    pack(across_ref, 0, *add_packed(values, loss, got_ref, 3 * BLOCK))


def column_second_body(near_ref, got_ref, ahead_ref, behind_ref):
    values, loss = packed_rows(near_ref, BLOCK, BLOCK)
    pack(ahead_ref, 0, *add_packed(values, loss, got_ref, 0))
    pack(behind_ref, 0, *packed_rows(near_ref, 2 * BLOCK, BLOCK))


def image_head_body(near_ref, ahead_ref, behind_ref, resid_ref, gain_ref, out_ref):
    values, loss = packed_rows(near_ref, 0, BLOCK)
    values, loss = add_packed(values, loss, ahead_ref, 0)
    values, loss = add_packed(values, loss, behind_ref, 0)
    pack(out_ref, 0, head_back(resid_ref[...], gain_ref[...], values), loss)


def scatter_column(keep, sent, resid, gain):
    block16 = shape(BLOCK, PACKED, bf16)
    got = send(sent, SIBLING)
    near, across = call(column_first_body, [shape(3 * BLOCK, PACKED, f32), block16], [keep, got])
    got = send(across, Z_BACK)
    ahead, behind = call(column_second_body, [block16, block16], [near, got])
    ahead = send(ahead, Z_BACK)
    behind = send(behind, Z_OUT)
    return call(image_head_body, [block16], [near, ahead, behind, resid, gain.reshape(1, WIDTH)])[0]


def gather_rows(own):
    other = send(own, Z_PAIR)
    return own, other, send(own, SIBLING), send(other, SIBLING)


def swapped_body(own_ref, got_ref, out_ref):
    own, got = own_ref[...].astype(f32), got_ref[...].astype(f32)
    out_ref[0:BLOCK, :] = (own[0:BLOCK, :] + got[BLOCK:128, :]).astype(bf16)
    out_ref[BLOCK:128, :] = (own[BLOCK:128, :] + got[0:BLOCK, :]).astype(bf16)


def grad_body(has_loss, mine, x_ref, gain_ref, r0, r1, r2, r3, own_ref, got_ref, out_ref, *loss_ref):
    losses = jnp.zeros((1, 256), f32)
    for place, ref in enumerate((r0, r1, r2, r3)):
        target = place ^ mine[0]
        start = pl.multiple_of(target * BLOCK, BLOCK)
        unit, inverse = centred(x_ref[pl.ds(start, BLOCK), :].astype(f32))
        half = own_ref if place < 2 else got_ref
        first = (place % 2) * BLOCK
        d_norm = half[first : first + BLOCK, :].astype(f32)
        back = centred_back(unit, inverse, d_norm * gain_ref[...])
        out_ref[pl.ds(start, BLOCK), :] = ref[:, 0:WIDTH].astype(f32) + back
        if has_loss:
            row = lax.broadcasted_iota(jnp.int32, (BLOCK, 256), 0)
            column = lax.broadcasted_iota(jnp.int32, (BLOCK, 256), 1)
            spread = jnp.where(column == target * BLOCK + row, loss_of(ref[:, WIDTH:PACKED]), 0.0)
            losses = losses + jnp.sum(spread, axis=0, keepdims=True)
    if has_loss:
        loss_ref[0][...] = losses


def input_grad(mine, tokens, gain, blocks, keep, sent, has_loss):
    half16 = shape(128, WIDTH, bf16)
    got = send(sent, SIBLING)
    half = call(joined_body, [half16], [keep, got])[0]
    got = send(half, Z_PAIR)
    own = call(swapped_body, [half16], [half, got])[0]
    got = send(own, SIBLING)
    outs = [shape(256, WIDTH, f32)] + ([shape(1, 256, f32)] if has_loss else [])
    return call(
        functools.partial(grad_body, has_loss),
        outs,
        [tokens, gain.reshape(1, WIDTH), *blocks, own, got],
        scalar=mine,
    )


def on_device(
    image_in,
    text_in,
    image_gain,
    image_up,
    image_down,
    image_final,
    text_gain,
    text_up,
    text_down,
    text_final,
):
    mp = lax.axis_index("mp")
    mine = (2 * (mp % 2) + mp // 2).astype(jnp.int32).reshape(1)

    text_pre, keep, sent = tower_forward(mine, text_in, text_gain, text_up, text_down)
    text_resid, z_text = scattered_embed(mine, keep, sent, text_in, text_final)
    near, left, right, far = gather_plane(z_text)
    image_pre, keep, sent = tower_forward(mine, image_in, image_gain, image_up, image_down)
    image_resid, z_image = scattered_embed(mine, keep, sent, image_in, image_final)
    images = gather_column(z_image)

    *text_grads, keep, sent = pair_tile(images, near, left, right, far)
    image_dres = gather_rows(scatter_column(keep, sent, image_resid, image_final))
    keep, sent = tower_backward(image_dres, image_pre, image_up, image_down)
    image_grad, losses = input_grad(mine, image_in, image_gain, image_dres, keep, sent, True)

    text_dres = gather_rows(scatter_plane(text_grads, text_resid, text_final))
    keep, sent = tower_backward(text_dres, text_pre, text_up, text_down)
    text_grad = input_grad(mine, text_in, text_gain, text_dres, keep, sent, False)[0]
    return (image_grad, text_grad, losses.reshape(256))


def solution(mesh):
    placed = (
        P("dp", None),
        P("dp", None),
        P(),
        P(None, "mp"),
        P("mp", None),
        P(),
        P(),
        P(None, "mp"),
        P("mp", None),
        P(),
    )
    return jax.shard_map(
        on_device,
        mesh=mesh,
        in_specs=placed,
        out_specs=(P("dp", None), P("dp", None), P("dp")),
        check_vma=False,
    )
```

profile of v0, /device:TPU:1, one launch (start us, length us, event | category | flops | bytes accessed | tf_op | source)
XLA Modules:
  0.0 148.8 jit_solution(13935896658148907880)
XLA Ops:
  1.4 2.2 %copy-done = bf16[1408,1536]{1,0:T(8,128)(2,1)S(1)} copy-done((bf16[1408,1536]{1,0:T(8,128)(2,1)S(1)}, bf16[1408,1536]{1,0:T(8,128)(2,1)}, u32[]{:S(2)}) %copy-start) | copy-done | bytes 4325400
  3.6 2.2 %copy-done.1 = bf16[1536,1408]{1,0:T(8,128)(2,1)S(1)} copy-done((bf16[1536,1408]{1,0:T(8,128)(2,1)S(1)}, bf16[1536,1408]{1,0:T(8,128)(2,1)}, u32[]{:S(2)}) %copy-start.1) | copy-done | bytes 4325400
  5.8 1.1 copy-done.5
  6.9 8.1 %shard_map.124 = (f32[256,1536]{1,0:T(8,128)S(1)}, f32[128,1408]{1,0:T(8,128)S(1)}, bf16[128,1408]{1,0:T(8,128)(2,1)S(1)}) custom-call(s32[1]{0:T(128)} %bitcast.mine, bf16[256,1408]{1,0:T(8,128)(2,1)S(1)} %copy-done.5, f32[1,1408]{1,0:T(1,128)S(1)} %reshape.31.gain_ref, bf16[1408,1536]{1,0:T(8,128)(2,1)S(1)} %copy-done, bf16[1536,1408]{1,0:T(8,128)(2,1)S(1)} %copy-done.1), custom_call_target="tpu_custom_call" | custom-call | flops 2214592512 | bytes 12582912 | tf_op jit(solution)/shard_map/pallas_call | solution.py:145
  15.0 1.5 %collective-permute-start.9 = (bf16[128,1408]{1,0:T(8,128)(2,1)S(1)}, bf16[128,1408]{1,0:T(8,128)(2,1)S(1)}, u32[]{:S(2)}, u32[]{:S(2)}) collective-permute-start(bf16[128,1408]{1,0:T(8,128)(2,1)S(1)} %get-tuple-element.49), channel_id=1, source_target_pairs={{0,1},{1,0},{2,3},{3,2},{4,5},{5,4},{6,7},{7,6},{8,9},{9,8},{10,11... | collective-permute-start | bytes 1081352 | tf_op jit(solution)/shard_map/ppermute | solution.py:54
  17.2 8.1 %shard_map.121 = (f32[256,1536]{1,0:T(8,128)S(1)}, f32[128,1408]{1,0:T(8,128)S(1)}, bf16[128,1408]{1,0:T(8,128)(2,1)S(1)}) custom-call(s32[1]{0:T(128)} %bitcast.mine, bf16[256,1408]{1,0:T(8,128)(2,1)S(1)} %copy-done.4, f32[1,1408]{1,0:T(1,128)S(1)} %reshape.29.gain_ref, bf16[1408,1536]{1,0:T(8,128)(2,1)S(1)} %copy-done.2, bf16[1536,1408]{1,0:T(8,128)(2,1)S(1)} %copy-done.3), custom_call_target="tpu_custom_call" | custom-call | flops 2214592512 | bytes 12582912 | tf_op jit(solution)/shard_map/pallas_call | solution.py:145
  25.5 1.8 %collective-permute-start.10 = (bf16[64,1408]{1,0:T(8,128)(2,1)S(1)}, bf16[64,1408]{1,0:T(8,128)(2,1)S(1)}, u32[]{:S(2)}, u32[]{:S(2)}) collective-permute-start(bf16[64,1408]{1,0:T(8,128)(2,1)S(1)} %get-tuple-element.51), channel_id=1, source_target_pairs={{0,2},{1,3},{2,0},{3,1},{4,6},{5,7},{6,4},{7,5},{8,10},{9,11},{10,... | collective-permute-start | bytes 540680 | tf_op jit(solution)/shard_map/ppermute | solution.py:54
  27.4 1.6 %collective-permute-start.1 = (bf16[64,1408]{1,0:T(8,128)(2,1)S(1)}, bf16[64,1408]{1,0:T(8,128)(2,1)S(1)}, u32[]{:S(2)}, u32[]{:S(2)}) collective-permute-start(bf16[64,1408]{1,0:T(8,128)(2,1)S(1)} %get-tuple-element.46), channel_id=1, source_target_pairs={{0,2},{1,3},{2,0},{3,1},{4,6},{5,7},{6,4},{7,5},{8,10},{9,11},{10,... | collective-permute-start | bytes 540680 | tf_op jit(solution)/shard_map/ppermute | solution.py:54
  29.0 2.8 %collective-permute-done.10.got_ref = bf16[64,1408]{1,0:T(8,128)(2,1)S(1)} collective-permute-done((bf16[64,1408]{1,0:T(8,128)(2,1)S(1)}, bf16[64,1408]{1,0:T(8,128)(2,1)S(1)}, u32[]{:S(2)}, u32[]{:S(2)}) %collective-permute-start.10) | collective-permute-done | bytes 180256 | tf_op jit(solution)/shard_map/ppermute | solution.py:54
  32.2 2.7 %collective-permute-start.12 = (bf16[64,1408]{1,0:T(8,128)(2,1)S(1)}, bf16[64,1408]{1,0:T(8,128)(2,1)S(1)}, u32[]{:S(2)}, u32[]{:S(2)}) collective-permute-start(bf16[64,1408]{1,0:T(8,128)(2,1)S(1)} %get-tuple-element.52.first_ref), channel_id=1, source_target_pairs={{0,24},{1,97},{2,26},{3,99},{4,28},{5,101},{6,30},{7,103},{8,0},{9... | collective-permute-start | bytes 540680 | tf_op jit(solution)/shard_map/ppermute | solution.py:54
  34.9 0.8 collective-permute-done.1.got_ref
  36.0 3.4 %collective-permute-start.2 = (bf16[64,1408]{1,0:T(8,128)(2,1)S(1)}, bf16[64,1408]{1,0:T(8,128)(2,1)S(1)}, u32[]{:S(2)}, u32[]{:S(2)}) collective-permute-start(bf16[64,1408]{1,0:T(8,128)(2,1)S(1)} %get-tuple-element.47.refs_0_), channel_id=1, source_target_pairs={{0,2},{1,7},{2,4},{3,1},{4,6},{5,3},{6,0},{7,5},{8,10},{9,15},{10,... | collective-permute-start | bytes 540680 | tf_op jit(solution)/shard_map/ppermute | solution.py:54
  39.4 2.9 %collective-permute-start.13 = (bf16[64,1408]{1,0:T(8,128)(2,1)S(1)}, bf16[64,1408]{1,0:T(8,128)(2,1)S(1)}, u32[]{:S(2)}, u32[]{:S(2)}) collective-permute-start(bf16[64,1408]{1,0:T(8,128)(2,1)S(1)} %get-tuple-element.52.first_ref), channel_id=1, source_target_pairs={{0,16},{1,65},{2,18},{3,67},{4,20},{5,69},{6,22},{7,71},{8,24},{9,... | collective-permute-start | bytes 540680 | tf_op jit(solution)/shard_map/ppermute | solution.py:54
  42.7 2.0 %collective-permute-start.5 = (bf16[64,1408]{1,0:T(8,128)(2,1)S(1)}, bf16[64,1408]{1,0:T(8,128)(2,1)S(1)}, u32[]{:S(2)}, u32[]{:S(2)}) collective-permute-start(bf16[64,1408]{1,0:T(8,128)(2,1)S(1)} %get-tuple-element.47.refs_0_), channel_id=1, source_target_pairs={{0,1},{1,0},{2,3},{3,2},{4,5},{5,4},{6,7},{7,6},{8,9},{9,8},{10,11... | collective-permute-start | bytes 540680 | tf_op jit(solution)/shard_map/ppermute | solution.py:54
  44.7 1.7 %collective-permute-start.4 = (bf16[64,1408]{1,0:T(8,128)(2,1)S(1)}, bf16[64,1408]{1,0:T(8,128)(2,1)S(1)}, u32[]{:S(2)}, u32[]{:S(2)}) collective-permute-start(bf16[64,1408]{1,0:T(8,128)(2,1)S(1)} %collective-permute-done.2.refs_1_), channel_id=1, source_target_pairs={{0,2},{1,7},{2,4},{3,1},{4,6},{5,3},{6,0},{7,5},{8,10},{9,15},{10,... | collective-permute-start | bytes 540680 | tf_op jit(solution)/shard_map/ppermute | solution.py:54
  46.4 1.7 %collective-permute-done.11.second_ref = bf16[64,1408]{1,0:T(8,128)(2,1)S(1)} collective-permute-done((bf16[64,1408]{1,0:T(8,128)(2,1)S(1)}, bf16[64,1408]{1,0:T(8,128)(2,1)S(1)}, u32[]{:S(2)}, u32[]{:S(2)}) %collective-permute-start.11) | collective-permute-done | bytes 180256 | tf_op jit(solution)/shard_map/ppermute | solution.py:54
  48.1 2.2 %collective-permute-start.17 = (bf16[128,1408]{1,0:T(8,128)(2,1)S(1)}, bf16[128,1408]{1,0:T(8,128)(2,1)S(1)}, u32[]{:S(2)}, u32[]{:S(2)}) collective-permute-start(bf16[128,1408]{1,0:T(8,128)(2,1)S(1)} %shard_map.128.refs_9_), channel_id=1, source_target_pairs={{0,96},{1,25},{2,98},{3,27},{4,100},{5,29},{6,102},{7,31},{8,104},... | collective-permute-start | bytes 1081352 | tf_op jit(solution)/shard_map/ppermute | solution.py:54
  50.7 2.5 %collective-permute-start.16 = (bf16[128,1408]{1,0:T(8,128)(2,1)S(1)}, bf16[128,1408]{1,0:T(8,128)(2,1)S(1)}, u32[]{:S(2)}, u32[]{:S(2)}) collective-permute-start(bf16[128,1408]{1,0:T(8,128)(2,1)S(1)} %shard_map.127.refs_8_), channel_id=1, source_target_pairs={{0,96},{1,25},{2,98},{3,27},{4,100},{5,29},{6,102},{7,31},{8,104},... | collective-permute-start | bytes 1081352 | tf_op jit(solution)/shard_map/ppermute | solution.py:54
  53.2 1.9 %collective-permute-start.7 = (bf16[64,1408]{1,0:T(8,128)(2,1)S(1)}, bf16[64,1408]{1,0:T(8,128)(2,1)S(1)}, u32[]{:S(2)}, u32[]{:S(2)}) collective-permute-start(bf16[64,1408]{1,0:T(8,128)(2,1)S(1)} %collective-permute-done.3.refs_2_), channel_id=1, source_target_pairs={{0,1},{1,0},{2,3},{3,2},{4,5},{5,4},{6,7},{7,6},{8,9},{9,8},{10,11... | collective-permute-start | bytes 540680 | tf_op jit(solution)/shard_map/ppermute | solution.py:54
  55.1 1.0 collective-permute-done.7.refs_6_
  56.5 1.8 %collective-permute-start.19 = (bf16[128,1408]{1,0:T(8,128)(2,1)S(1)}, bf16[128,1408]{1,0:T(8,128)(2,1)S(1)}, u32[]{:S(2)}, u32[]{:S(2)}) collective-permute-start(bf16[128,1408]{1,0:T(8,128)(2,1)S(1)} %collective-permute-done.17.refs_13_), channel_id=1, source_target_pairs={{0,96},{1,25},{2,98},{3,27},{4,100},{5,29},{6,102},{7,31},{8,104},... | collective-permute-start | bytes 1081352 | tf_op jit(solution)/shard_map/ppermute | solution.py:54
  58.3 3.8 %collective-permute-done.15.refs_11_ = bf16[128,1408]{1,0:T(8,128)(2,1)S(1)} collective-permute-done((bf16[128,1408]{1,0:T(8,128)(2,1)S(1)}, bf16[128,1408]{1,0:T(8,128)(2,1)S(1)}, u32[]{:S(2)}, u32[]{:S(2)}) %collective-permute-start.15) | collective-permute-done | bytes 360480 | tf_op jit(solution)/shard_map/ppermute | solution.py:54
  62.1 5.8 %shard_map.129 = (bf16[512,1408]{1,0:T(8,128)(2,1)S(1)}, f32[512,1408]{1,0:T(8,128)S(1)}, f32[512,128]{1,0:T(8,128)S(1)}, f32[256,1408]{1,0:T(8,128)S(1)}, f32[1...) custom-call(bf16[64,1408]{1,0:T(8,128)(2,1)S(1)} %get-tuple-element., ...), custom_call_target="tpu_custom_call" | custom-call | flops 3321888768 | bytes 11796480 | tf_op jit(solution)/shard_map/pallas_call | solution.py:68
  67.9 2.3 %shard_map.130 = (bf16[128,1408]{1,0:T(8,128)(2,1)S(1)}, bf16[128,1408]{1,0:T(8,128)(2,1)S(1)}, f32[256,1536]{1,0:T(8,128)S(1)}, bf16[256,1536]{1,0:T(8,128)(2,1)S(1)}) custom-call(bf16[512,1408]{1,0:T(8,128)(2,1)S(1)} %get-tuple-element.53.image_ref, f32[512,1408]{1,0:T(8,128)S(1)} %get-tuple-element.54.total_ref, ...), custom_call_target="tpu_custom_call" | custom-call | flops 1107296256 | bytes 8388608 | tf_op jit(solution)/shard_map/pallas_call | solution.py:68
  70.2 2.2 %collective-permute-start.20 = (bf16[256,1536]{1,0:T(8,128)(2,1)S(1)}, bf16[256,1536]{1,0:T(8,128)(2,1)S(1)}, u32[]{:S(2)}, u32[]{:S(2)}) collective-permute-start(bf16[256,1536]{1,0:T(8,128)(2,1)S(1)} %get-tuple-element.57), channel_id=1, source_target_pairs={{0,1},{1,0},{2,3},{3,2},{4,5},{5,4},{6,7},{7,6},{8,9},{9,8},{10,11... | collective-permute-start | bytes 2359304 | tf_op jit(solution)/shard_map/ppermute | solution.py:54
  72.9 2.2 %collective-permute-start.30 = (bf16[128,1408]{1,0:T(8,128)(2,1)S(1)}, bf16[128,1408]{1,0:T(8,128)(2,1)S(1)}, u32[]{:S(2)}, u32[]{:S(2)}) collective-permute-start(bf16[128,1408]{1,0:T(8,128)(2,1)S(1)} %get-tuple-element.69), channel_id=1, source_target_pairs={{0,96},{1,25},{2,98},{3,27},{4,100},{5,29},{6,102},{7,31},{8,104},... | collective-permute-start | bytes 1081352 | tf_op jit(solution)/shard_map/ppermute | solution.py:54
  75.2 1.4 collective-permute-start.33
  76.6 3.6 %collective-permute-done.34.got_ref = bf16[128,1408]{1,0:T(8,128)(2,1)S(1)} collective-permute-done((bf16[128,1408]{1,0:T(8,128)(2,1)S(1)}, bf16[128,1408]{1,0:T(8,128)(2,1)S(1)}, u32[]{:S(2)}, u32[]{:S(2)}) %collective-permute-start.34) | collective-permute-done | bytes 360480 | tf_op jit(solution)/shard_map/ppermute | solution.py:54
  80.5 2.7 %collective-permute-start.31 = (bf16[128,1408]{1,0:T(8,128)(2,1)S(1)}, bf16[128,1408]{1,0:T(8,128)(2,1)S(1)}, u32[]{:S(2)}, u32[]{:S(2)}) collective-permute-start(bf16[128,1408]{1,0:T(8,128)(2,1)S(1)} %shard_map.138), channel_id=1, source_target_pairs={{0,96},{1,25},{2,98},{3,27},{4,100},{5,29},{6,102},{7,31},{8,104},... | collective-permute-start | bytes 1081352 | tf_op jit(solution)/shard_map/ppermute | solution.py:54
  83.4 1.7 %collective-permute-start.21 = (bf16[64,1536]{1,0:T(8,128)(2,1)S(1)}, bf16[64,1536]{1,0:T(8,128)(2,1)S(1)}, u32[]{:S(2)}, u32[]{:S(2)}) collective-permute-start(bf16[64,1536]{1,0:T(8,128)(2,1)S(1)} %get-tuple-element.59), channel_id=1, source_target_pairs={{0,6},{1,3},{2,0},{3,5},{4,2},{5,7},{6,4},{7,1},{8,14},{9,11},{10,... | collective-permute-start | bytes 589832 | tf_op jit(solution)/shard_map/ppermute | solution.py:54
  85.1 3.0 %collective-permute-done.35.r1 = bf16[128,1408]{1,0:T(8,128)(2,1)S(1)} collective-permute-done((bf16[128,1408]{1,0:T(8,128)(2,1)S(1)}, bf16[128,1408]{1,0:T(8,128)(2,1)S(1)}, u32[]{:S(2)}, u32[]{:S(2)}) %collective-permute-start.35) | collective-permute-done | bytes 360480 | tf_op jit(solution)/shard_map/ppermute | solution.py:54
  88.5 1.5 collective-permute-start.37
  90.1 1.7 %collective-permute-start.22 = (bf16[64,1536]{1,0:T(8,128)(2,1)S(1)}, bf16[64,1536]{1,0:T(8,128)(2,1)S(1)}, u32[]{:S(2)}, u32[]{:S(2)}) collective-permute-start(bf16[64,1536]{1,0:T(8,128)(2,1)S(1)} %get-tuple-element.60), channel_id=1, source_target_pairs={{0,6},{1,3},{2,0},{3,5},{4,2},{5,7},{6,4},{7,1},{8,14},{9,11},{10,... | collective-permute-start | bytes 589832 | tf_op jit(solution)/shard_map/ppermute | solution.py:54
  91.8 1.0 collective-permute-start.23
  92.8 3.5 %collective-permute-done.37.after_ref = bf16[64,1408]{1,0:T(8,128)(2,1)S(1)} collective-permute-done((bf16[64,1408]{1,0:T(8,128)(2,1)S(1)}, bf16[64,1408]{1,0:T(8,128)(2,1)S(1)}, u32[]{:S(2)}, u32[]{:S(2)}) %collective-permute-start.37) | collective-permute-done | bytes 180256 | tf_op jit(solution)/shard_map/ppermute | solution.py:54
  96.8 1.7 %collective-permute-start.39 = (bf16[64,1408]{1,0:T(8,128)(2,1)S(1)}, bf16[64,1408]{1,0:T(8,128)(2,1)S(1)}, u32[]{:S(2)}, u32[]{:S(2)}) collective-permute-start(bf16[64,1408]{1,0:T(8,128)(2,1)S(1)} %shard_map.141.r0), channel_id=1, source_target_pairs={{0,2},{1,3},{2,0},{3,1},{4,6},{5,7},{6,4},{7,5},{8,10},{9,11},{10,... | collective-permute-start | bytes 540680 | tf_op jit(solution)/shard_map/ppermute | solution.py:54
  99.2 4.6 %collective-permute-start.40 = (bf16[64,1408]{1,0:T(8,128)(2,1)S(1)}, bf16[64,1408]{1,0:T(8,128)(2,1)S(1)}, u32[]{:S(2)}, u32[]{:S(2)}) collective-permute-start(bf16[64,1408]{1,0:T(8,128)(2,1)S(1)} %shard_map.141.r0), channel_id=1, source_target_pairs={{0,1},{1,0},{2,3},{3,2},{4,5},{5,4},{6,7},{7,6},{8,9},{9,8},{10,11... | collective-permute-start | bytes 540680 | tf_op jit(solution)/shard_map/ppermute | solution.py:54
  103.7 2.5 %collective-permute-start.41 = (bf16[64,1408]{1,0:T(8,128)(2,1)S(1)}, bf16[64,1408]{1,0:T(8,128)(2,1)S(1)}, u32[]{:S(2)}, u32[]{:S(2)}) collective-permute-start(bf16[64,1408]{1,0:T(8,128)(2,1)S(1)} %collective-permute-done.39.r1), channel_id=1, source_target_pairs={{0,1},{1,0},{2,3},{3,2},{4,5},{5,4},{6,7},{7,6},{8,9},{9,8},{10,11... | collective-permute-start | bytes 540680 | tf_op jit(solution)/shard_map/ppermute | solution.py:54
  106.3 3.0 %collective-permute-start.26 = (bf16[64,1536]{1,0:T(8,128)(2,1)S(1)}, bf16[64,1536]{1,0:T(8,128)(2,1)S(1)}, u32[]{:S(2)}, u32[]{:S(2)}) collective-permute-start(bf16[64,1536]{1,0:T(8,128)(2,1)S(1)} %collective-permute-done.24.r1), channel_id=1, source_target_pairs={{0,1},{1,0},{2,3},{3,2},{4,5},{5,4},{6,7},{7,6},{8,9},{9,8},{10,11... | collective-permute-start | bytes 589832 | tf_op jit(solution)/shard_map/ppermute | solution.py:54
  109.4 7.8 %shard_map.142 = (f32[128,1408]{1,0:T(8,128)S(1)}, bf16[128,1408]{1,0:T(8,128)(2,1)S(1)}) custom-call(bf16[64,1408]{1,0:T(8,128)(2,1)S(1)} %shard_map.141.r0, bf16[64,1408]{1,0:T(8,128)(2,1)S(1)} %collective-permute-done.39.r1, bf16[64,1408]{1,0:T(8,128)(2,1)S(1)} %collective-permute-done.40.r2, bf16[64,1408]{1,0:T(8,128)(2,1)S(1)} %collective-permute-done.41.r3, ...), custom_call_target="tpu_custom_call" | custom-call | flops 2214592512 | bytes 12582912 | tf_op jit(solution)/shard_map/pallas_call | solution.py:205
  117.3 7.8 %shard_map.134 = (f32[128,1408]{1,0:T(8,128)S(1)}, bf16[128,1408]{1,0:T(8,128)(2,1)S(1)}) custom-call(bf16[64,1536]{1,0:T(8,128)(2,1)S(1)} %shard_map.133.r0, bf16[64,1536]{1,0:T(8,128)(2,1)S(1)} %collective-permute-done.24.r1, bf16[64,1536]{1,0:T(8,128)(2,1)S(1)} %collective-permute-done.25.r2, bf16[64,1536]{1,0:T(8,128)(2,1)S(1)} %collective-permute-done.26.r3, ...), custom_call_target="tpu_custom_call" | custom-call | flops 2214592512 | bytes 12582912 | tf_op jit(solution)/shard_map/pallas_call | solution.py:205
  126.3 0.7 collective-permute-done.27.got_ref
  127.6 8.3 %collective-permute-done.43.got_ref = bf16[128,1408]{1,0:T(8,128)(2,1)S(1)} collective-permute-done((bf16[128,1408]{1,0:T(8,128)(2,1)S(1)}, bf16[128,1408]{1,0:T(8,128)(2,1)S(1)}, u32[]{:S(2)}, u32[]{:S(2)}) %collective-permute-start.43) | collective-permute-done | bytes 360480 | tf_op jit(solution)/shard_map/ppermute | solution.py:54
  136.0 1.3 collective-permute-start.44
  137.3 6.3 %collective-permute-done.28.got_ref = bf16[128,1408]{1,0:T(8,128)(2,1)S(1)} collective-permute-done((bf16[128,1408]{1,0:T(8,128)(2,1)S(1)}, bf16[128,1408]{1,0:T(8,128)(2,1)S(1)}, u32[]{:S(2)}, u32[]{:S(2)}) %collective-permute-start.28) | collective-permute-done | bytes 360480 | tf_op jit(solution)/shard_map/ppermute | solution.py:54
  143.7 0.9 collective-permute-start.29
  144.6 2.1 %shard_map.145 = f32[256,1408]{1,0:T(8,128)} custom-call(s32[1]{0:T(128)} %bitcast.mine, bf16[256,1408]{1,0:T(8,128)(2,1)S(1)} %copy-done.6, f32[1,1408]{1,0:T(1,128)S(1)} %reshape.31.gain_ref, bf16[64,1408]{1,0:T(8,128)(2,1)S(1)} %shard_map.141.r0, bf16[64,1408]{1,0:T(8,128)(2,1)S(1)} %collective-permute-done.39.r1, ...), custom_call_target="tpu_custom_call" | custom-call | flops 1048576 | bytes 3610116 | tf_op jit(solution)/shard_map/pallas_call | solution.py:68
  146.7 2.1 %shard_map.137 = (f32[256,1408]{1,0:T(8,128)}, f32[1,256]{1,0:T(1,128)}) custom-call(s32[1]{0:T(128)} %bitcast.mine, bf16[256,1408]{1,0:T(8,128)(2,1)S(1)} %copy-done.4, f32[1,1408]{1,0:T(1,128)S(1)} %reshape.29.gain_ref, bf16[64,1536]{1,0:T(8,128)(2,1)S(1)} %shard_map.133.r0, bf16[64,1536]{1,0:T(8,128)(2,1)S(1)} %collective-permute-done.24.r1, ...), custom_call_target="tpu_custom_call" | custom-call | flops 1048576 | bytes 3676676 | tf_op jit(solution)/shard_map/pallas_call | solution.py:68
  (99 shorter events, 8.0 us)
Async XLA Ops:
  15.0 10.5 %collective-permute-start.9 = (bf16[128,1408]{1,0:T(8,128)(2,1)S(1)}, bf16[128,1408]{1,0:T(8,128)(2,1)S(1)}, u32[]{:S(2)}, u32[]{:S(2)}) collective-permute-start(bf16[128,1408]{1,0:T(8,128)(2,1)S(1)} %get-tuple-element.49), channel_id=1, source_target_pairs={{0,1},{1,0},{2,3},{3,2},{4,5},{5,4},{6,7},{7,6},{8,9},{9,8},{10,11... | collective-permute-start | bytes 1081352 | tf_op jit(solution)/shard_map/ppermute | solution.py:54
  25.4 2.0 %collective-permute-start = (bf16[128,1408]{1,0:T(8,128)(2,1)S(1)}, bf16[128,1408]{1,0:T(8,128)(2,1)S(1)}, u32[]{:S(2)}, u32[]{:S(2)}) collective-permute-start(bf16[128,1408]{1,0:T(8,128)(2,1)S(1)} %get-tuple-element.44), channel_id=1, source_target_pairs={{0,1},{1,0},{2,3},{3,2},{4,5},{5,4},{6,7},{7,6},{8,9},{9,8},{10,11... | collective-permute-start | bytes 1081352 | tf_op jit(solution)/shard_map/ppermute | solution.py:54
  25.5 6.3 %collective-permute-start.10 = (bf16[64,1408]{1,0:T(8,128)(2,1)S(1)}, bf16[64,1408]{1,0:T(8,128)(2,1)S(1)}, u32[]{:S(2)}, u32[]{:S(2)}) collective-permute-start(bf16[64,1408]{1,0:T(8,128)(2,1)S(1)} %get-tuple-element.51), channel_id=1, source_target_pairs={{0,2},{1,3},{2,0},{3,1},{4,6},{5,7},{6,4},{7,5},{8,10},{9,11},{10,... | collective-permute-start | bytes 540680 | tf_op jit(solution)/shard_map/ppermute | solution.py:54
  27.4 8.2 %collective-permute-start.1 = (bf16[64,1408]{1,0:T(8,128)(2,1)S(1)}, bf16[64,1408]{1,0:T(8,128)(2,1)S(1)}, u32[]{:S(2)}, u32[]{:S(2)}) collective-permute-start(bf16[64,1408]{1,0:T(8,128)(2,1)S(1)} %get-tuple-element.46), channel_id=1, source_target_pairs={{0,2},{1,3},{2,0},{3,1},{4,6},{5,7},{6,4},{7,5},{8,10},{9,11},{10,... | collective-permute-start | bytes 540680 | tf_op jit(solution)/shard_map/ppermute | solution.py:54
  32.2 10.5 %collective-permute-start.12 = (bf16[64,1408]{1,0:T(8,128)(2,1)S(1)}, bf16[64,1408]{1,0:T(8,128)(2,1)S(1)}, u32[]{:S(2)}, u32[]{:S(2)}) collective-permute-start(bf16[64,1408]{1,0:T(8,128)(2,1)S(1)} %get-tuple-element.52.first_ref), channel_id=1, source_target_pairs={{0,24},{1,97},{2,26},{3,99},{4,28},{5,101},{6,30},{7,103},{8,0},{9... | collective-permute-start | bytes 540680 | tf_op jit(solution)/shard_map/ppermute | solution.py:54
  36.0 8.7 %collective-permute-start.2 = (bf16[64,1408]{1,0:T(8,128)(2,1)S(1)}, bf16[64,1408]{1,0:T(8,128)(2,1)S(1)}, u32[]{:S(2)}, u32[]{:S(2)}) collective-permute-start(bf16[64,1408]{1,0:T(8,128)(2,1)S(1)} %get-tuple-element.47.refs_0_), channel_id=1, source_target_pairs={{0,2},{1,7},{2,4},{3,1},{4,6},{5,3},{6,0},{7,5},{8,10},{9,15},{10,... | collective-permute-start | bytes 540680 | tf_op jit(solution)/shard_map/ppermute | solution.py:54
  39.4 7.0 %collective-permute-start.13 = (bf16[64,1408]{1,0:T(8,128)(2,1)S(1)}, bf16[64,1408]{1,0:T(8,128)(2,1)S(1)}, u32[]{:S(2)}, u32[]{:S(2)}) collective-permute-start(bf16[64,1408]{1,0:T(8,128)(2,1)S(1)} %get-tuple-element.52.first_ref), channel_id=1, source_target_pairs={{0,16},{1,65},{2,18},{3,67},{4,20},{5,69},{6,22},{7,71},{8,24},{9,... | collective-permute-start | bytes 540680 | tf_op jit(solution)/shard_map/ppermute | solution.py:54
  42.3 5.9 %collective-permute-start.11 = (bf16[64,1408]{1,0:T(8,128)(2,1)S(1)}, bf16[64,1408]{1,0:T(8,128)(2,1)S(1)}, u32[]{:S(2)}, u32[]{:S(2)}) collective-permute-start(bf16[64,1408]{1,0:T(8,128)(2,1)S(1)} %get-tuple-element.52.first_ref), channel_id=1, source_target_pairs={{0,8},{1,33},{2,10},{3,35},{4,12},{5,37},{6,14},{7,39},{8,16},{9,4... | collective-permute-start | bytes 540680 | tf_op jit(solution)/shard_map/ppermute | solution.py:54
  42.7 7.7 %collective-permute-start.3 = (bf16[64,1408]{1,0:T(8,128)(2,1)S(1)}, bf16[64,1408]{1,0:T(8,128)(2,1)S(1)}, u32[]{:S(2)}, u32[]{:S(2)}) collective-permute-start(bf16[64,1408]{1,0:T(8,128)(2,1)S(1)} %get-tuple-element.47.refs_0_), channel_id=1, source_target_pairs={{0,6},{1,3},{2,0},{3,5},{4,2},{5,7},{6,4},{7,1},{8,14},{9,11},{10,... | collective-permute-start | bytes 540680 | tf_op jit(solution)/shard_map/ppermute | solution.py:54
  42.7 7.8 %collective-permute-start.5 = (bf16[64,1408]{1,0:T(8,128)(2,1)S(1)}, bf16[64,1408]{1,0:T(8,128)(2,1)S(1)}, u32[]{:S(2)}, u32[]{:S(2)}) collective-permute-start(bf16[64,1408]{1,0:T(8,128)(2,1)S(1)} %get-tuple-element.47.refs_0_), channel_id=1, source_target_pairs={{0,1},{1,0},{2,3},{3,2},{4,5},{5,4},{6,7},{7,6},{8,9},{9,8},{10,11... | collective-permute-start | bytes 540680 | tf_op jit(solution)/shard_map/ppermute | solution.py:54
  44.7 6.0 %collective-permute-start.4 = (bf16[64,1408]{1,0:T(8,128)(2,1)S(1)}, bf16[64,1408]{1,0:T(8,128)(2,1)S(1)}, u32[]{:S(2)}, u32[]{:S(2)}) collective-permute-start(bf16[64,1408]{1,0:T(8,128)(2,1)S(1)} %collective-permute-done.2.refs_1_), channel_id=1, source_target_pairs={{0,2},{1,7},{2,4},{3,1},{4,6},{5,3},{6,0},{7,5},{8,10},{9,15},{10,... | collective-permute-start | bytes 540680 | tf_op jit(solution)/shard_map/ppermute | solution.py:54
  46.4 6.8 %collective-permute-start.6 = (bf16[64,1408]{1,0:T(8,128)(2,1)S(1)}, bf16[64,1408]{1,0:T(8,128)(2,1)S(1)}, u32[]{:S(2)}, u32[]{:S(2)}) collective-permute-start(bf16[64,1408]{1,0:T(8,128)(2,1)S(1)} %collective-permute-done.2.refs_1_), channel_id=1, source_target_pairs={{0,1},{1,0},{2,3},{3,2},{4,5},{5,4},{6,7},{7,6},{8,9},{9,8},{10,11... | collective-permute-start | bytes 540680 | tf_op jit(solution)/shard_map/ppermute | solution.py:54
  48.1 8.3 %collective-permute-start.17 = (bf16[128,1408]{1,0:T(8,128)(2,1)S(1)}, bf16[128,1408]{1,0:T(8,128)(2,1)S(1)}, u32[]{:S(2)}, u32[]{:S(2)}) collective-permute-start(bf16[128,1408]{1,0:T(8,128)(2,1)S(1)} %shard_map.128.refs_9_), channel_id=1, source_target_pairs={{0,96},{1,25},{2,98},{3,27},{4,100},{5,29},{6,102},{7,31},{8,104},... | collective-permute-start | bytes 1081352 | tf_op jit(solution)/shard_map/ppermute | solution.py:54
  50.4 7.9 %collective-permute-start.14 = (bf16[128,1408]{1,0:T(8,128)(2,1)S(1)}, bf16[128,1408]{1,0:T(8,128)(2,1)S(1)}, u32[]{:S(2)}, u32[]{:S(2)}) collective-permute-start(bf16[128,1408]{1,0:T(8,128)(2,1)S(1)} %shard_map.127.refs_8_), channel_id=1, source_target_pairs={{0,32},{1,9},{2,34},{3,11},{4,36},{5,13},{6,38},{7,15},{8,40},{9,1... | collective-permute-start | bytes 1081352 | tf_op jit(solution)/shard_map/ppermute | solution.py:54
  50.5 11.6 %collective-permute-start.15 = (bf16[128,1408]{1,0:T(8,128)(2,1)S(1)}, bf16[128,1408]{1,0:T(8,128)(2,1)S(1)}, u32[]{:S(2)}, u32[]{:S(2)}) collective-permute-start(bf16[128,1408]{1,0:T(8,128)(2,1)S(1)} %shard_map.128.refs_9_), channel_id=1, source_target_pairs={{0,32},{1,9},{2,34},{3,11},{4,36},{5,13},{6,38},{7,15},{8,40},{9,1... | collective-permute-start | bytes 1081352 | tf_op jit(solution)/shard_map/ppermute | solution.py:54
  50.7 11.4 %collective-permute-start.16 = (bf16[128,1408]{1,0:T(8,128)(2,1)S(1)}, bf16[128,1408]{1,0:T(8,128)(2,1)S(1)}, u32[]{:S(2)}, u32[]{:S(2)}) collective-permute-start(bf16[128,1408]{1,0:T(8,128)(2,1)S(1)} %shard_map.127.refs_8_), channel_id=1, source_target_pairs={{0,96},{1,25},{2,98},{3,27},{4,100},{5,29},{6,102},{7,31},{8,104},... | collective-permute-start | bytes 1081352 | tf_op jit(solution)/shard_map/ppermute | solution.py:54
  53.2 2.9 %collective-permute-start.7 = (bf16[64,1408]{1,0:T(8,128)(2,1)S(1)}, bf16[64,1408]{1,0:T(8,128)(2,1)S(1)}, u32[]{:S(2)}, u32[]{:S(2)}) collective-permute-start(bf16[64,1408]{1,0:T(8,128)(2,1)S(1)} %collective-permute-done.3.refs_2_), channel_id=1, source_target_pairs={{0,1},{1,0},{2,3},{3,2},{4,5},{5,4},{6,7},{7,6},{8,9},{9,8},{10,11... | collective-permute-start | bytes 540680 | tf_op jit(solution)/shard_map/ppermute | solution.py:54
  56.1 6.0 %collective-permute-start.8 = (bf16[64,1408]{1,0:T(8,128)(2,1)S(1)}, bf16[64,1408]{1,0:T(8,128)(2,1)S(1)}, u32[]{:S(2)}, u32[]{:S(2)}) collective-permute-start(bf16[64,1408]{1,0:T(8,128)(2,1)S(1)} %collective-permute-done.4.refs_3_), channel_id=1, source_target_pairs={{0,1},{1,0},{2,3},{3,2},{4,5},{5,4},{6,7},{7,6},{8,9},{9,8},{10,11... | collective-permute-start | bytes 540680 | tf_op jit(solution)/shard_map/ppermute | solution.py:54
  56.5 11.4 %collective-permute-start.19 = (bf16[128,1408]{1,0:T(8,128)(2,1)S(1)}, bf16[128,1408]{1,0:T(8,128)(2,1)S(1)}, u32[]{:S(2)}, u32[]{:S(2)}) collective-permute-start(bf16[128,1408]{1,0:T(8,128)(2,1)S(1)} %collective-permute-done.17.refs_13_), channel_id=1, source_target_pairs={{0,96},{1,25},{2,98},{3,27},{4,100},{5,29},{6,102},{7,31},{8,104},... | collective-permute-start | bytes 1081352 | tf_op jit(solution)/shard_map/ppermute | solution.py:54
  58.3 9.6 %collective-permute-start.18 = (bf16[128,1408]{1,0:T(8,128)(2,1)S(1)}, bf16[128,1408]{1,0:T(8,128)(2,1)S(1)}, u32[]{:S(2)}, u32[]{:S(2)}) collective-permute-start(bf16[128,1408]{1,0:T(8,128)(2,1)S(1)} %collective-permute-done.14.refs_10_), channel_id=1, source_target_pairs={{0,32},{1,9},{2,34},{3,11},{4,36},{5,13},{6,38},{7,15},{8,40},{9,1... | collective-permute-start | bytes 1081352 | tf_op jit(solution)/shard_map/ppermute | solution.py:54
  62.1 47.2 %slice-start.2 = ((s8[4325376]{0:T(1024)(128)(4,1)}), s8[4194304]{0:T(1024)(128)(4,1)S(1)}, s32[]{:S(2)}) async-start(s8[4325376]{0:T(1024)(128)(4,1)} %bitcast.4), calls=%async_computation.2 | async-start | bytes 8388608
  67.9 41.4 %slice-start.3 = ((s8[4325376]{0:T(1024)(128)(4,1)}), s8[131072]{0:T(1024)(128)(4,1)S(1)}, s32[]{:S(2)}) async-start(s8[4325376]{0:T(1024)(128)(4,1)} %bitcast.4), calls=%async_computation.3 | async-start | bytes 262144
  70.2 13.0 %collective-permute-start.20 = (bf16[256,1536]{1,0:T(8,128)(2,1)S(1)}, bf16[256,1536]{1,0:T(8,128)(2,1)S(1)}, u32[]{:S(2)}, u32[]{:S(2)}) collective-permute-start(bf16[256,1536]{1,0:T(8,128)(2,1)S(1)} %get-tuple-element.57), channel_id=1, source_target_pairs={{0,1},{1,0},{2,3},{3,2},{4,5},{5,4},{6,7},{7,6},{8,9},{9,8},{10,11... | collective-permute-start | bytes 2359304 | tf_op jit(solution)/shard_map/ppermute | solution.py:54
  72.5 7.8 %collective-permute-start.34 = (bf16[128,1408]{1,0:T(8,128)(2,1)S(1)}, bf16[128,1408]{1,0:T(8,128)(2,1)S(1)}, u32[]{:S(2)}, u32[]{:S(2)}) collective-permute-start(bf16[128,1408]{1,0:T(8,128)(2,1)S(1)} %get-tuple-element.73), channel_id=1, source_target_pairs={{0,32},{1,9},{2,34},{3,11},{4,36},{5,13},{6,38},{7,15},{8,40},{9,1... | collective-permute-start | bytes 1081352 | tf_op jit(solution)/shard_map/ppermute | solution.py:54
  72.9 7.4 %collective-permute-start.30 = (bf16[128,1408]{1,0:T(8,128)(2,1)S(1)}, bf16[128,1408]{1,0:T(8,128)(2,1)S(1)}, u32[]{:S(2)}, u32[]{:S(2)}) collective-permute-start(bf16[128,1408]{1,0:T(8,128)(2,1)S(1)} %get-tuple-element.69), channel_id=1, source_target_pairs={{0,96},{1,25},{2,98},{3,27},{4,100},{5,29},{6,102},{7,31},{8,104},... | collective-permute-start | bytes 1081352 | tf_op jit(solution)/shard_map/ppermute | solution.py:54
  75.1 10.0 %collective-permute-start.32 = (bf16[128,1408]{1,0:T(8,128)(2,1)S(1)}, bf16[128,1408]{1,0:T(8,128)(2,1)S(1)}, u32[]{:S(2)}, u32[]{:S(2)}) collective-permute-start(bf16[128,1408]{1,0:T(8,128)(2,1)S(1)} %get-tuple-element.70), channel_id=1, source_target_pairs={{0,96},{1,25},{2,98},{3,27},{4,100},{5,29},{6,102},{7,31},{8,104},... | collective-permute-start | bytes 1081352 | tf_op jit(solution)/shard_map/ppermute | solution.py:54
  75.2 10.0 %collective-permute-start.33 = (bf16[128,1408]{1,0:T(8,128)(2,1)S(1)}, bf16[128,1408]{1,0:T(8,128)(2,1)S(1)}, u32[]{:S(2)}, u32[]{:S(2)}) collective-permute-start(bf16[128,1408]{1,0:T(8,128)(2,1)S(1)} %get-tuple-element.71), channel_id=1, source_target_pairs={{0,32},{1,9},{2,34},{3,11},{4,36},{5,13},{6,38},{7,15},{8,40},{9,1... | collective-permute-start | bytes 1081352 | tf_op jit(solution)/shard_map/ppermute | solution.py:54
  80.3 7.9 %collective-permute-start.35 = (bf16[128,1408]{1,0:T(8,128)(2,1)S(1)}, bf16[128,1408]{1,0:T(8,128)(2,1)S(1)}, u32[]{:S(2)}, u32[]{:S(2)}) collective-permute-start(bf16[128,1408]{1,0:T(8,128)(2,1)S(1)} %shard_map.139), channel_id=1, source_target_pairs={{0,32},{1,9},{2,34},{3,11},{4,36},{5,13},{6,38},{7,15},{8,40},{9,1... | collective-permute-start | bytes 1081352 | tf_op jit(solution)/shard_map/ppermute | solution.py:54
  80.5 7.7 %collective-permute-start.31 = (bf16[128,1408]{1,0:T(8,128)(2,1)S(1)}, bf16[128,1408]{1,0:T(8,128)(2,1)S(1)}, u32[]{:S(2)}, u32[]{:S(2)}) collective-permute-start(bf16[128,1408]{1,0:T(8,128)(2,1)S(1)} %shard_map.138), channel_id=1, source_target_pairs={{0,96},{1,25},{2,98},{3,27},{4,100},{5,29},{6,102},{7,31},{8,104},... | collective-permute-start | bytes 1081352 | tf_op jit(solution)/shard_map/ppermute | solution.py:54
  83.2 26.1 %slice-start = ((s8[4325376]{0:T(1024)(128)(4,1)}), s8[4194304]{0:T(1024)(128)(4,1)S(1)}, s32[]{:S(2)}) async-start(s8[4325376]{0:T(1024)(128)(4,1)} %bitcast.2), calls=%async_computation | async-start | bytes 8388608
  83.4 6.5 %collective-permute-start.21 = (bf16[64,1536]{1,0:T(8,128)(2,1)S(1)}, bf16[64,1536]{1,0:T(8,128)(2,1)S(1)}, u32[]{:S(2)}, u32[]{:S(2)}) collective-permute-start(bf16[64,1536]{1,0:T(8,128)(2,1)S(1)} %get-tuple-element.59), channel_id=1, source_target_pairs={{0,6},{1,3},{2,0},{3,5},{4,2},{5,7},{6,4},{7,1},{8,14},{9,11},{10,... | collective-permute-start | bytes 589832 | tf_op jit(solution)/shard_map/ppermute | solution.py:54
  88.4 4.4 %collective-permute-start.36 = (bf16[64,1408]{1,0:T(8,128)(2,1)S(1)}, bf16[64,1408]{1,0:T(8,128)(2,1)S(1)}, u32[]{:S(2)}, u32[]{:S(2)}) collective-permute-start(bf16[64,1408]{1,0:T(8,128)(2,1)S(1)} %get-tuple-element.75), channel_id=1, source_target_pairs={{0,24},{1,97},{2,26},{3,99},{4,28},{5,101},{6,30},{7,103},{8,0},{9... | collective-permute-start | bytes 540680 | tf_op jit(solution)/shard_map/ppermute | solution.py:54
  88.5 7.9 %collective-permute-start.37 = (bf16[64,1408]{1,0:T(8,128)(2,1)S(1)}, bf16[64,1408]{1,0:T(8,128)(2,1)S(1)}, u32[]{:S(2)}, u32[]{:S(2)}) collective-permute-start(bf16[64,1408]{1,0:T(8,128)(2,1)S(1)} %get-tuple-element.76), channel_id=1, source_target_pairs={{0,8},{1,33},{2,10},{3,35},{4,12},{5,37},{6,14},{7,39},{8,16},{9,4... | collective-permute-start | bytes 540680 | tf_op jit(solution)/shard_map/ppermute | solution.py:54
  89.9 6.4 %collective-permute-start.38 = (bf16[64,1408]{1,0:T(8,128)(2,1)S(1)}, bf16[64,1408]{1,0:T(8,128)(2,1)S(1)}, u32[]{:S(2)}, u32[]{:S(2)}) collective-permute-start(bf16[64,1408]{1,0:T(8,128)(2,1)S(1)} %get-tuple-element.77), channel_id=1, source_target_pairs={{0,16},{1,65},{2,18},{3,67},{4,20},{5,69},{6,22},{7,71},{8,24},{9,... | collective-permute-start | bytes 540680 | tf_op jit(solution)/shard_map/ppermute | solution.py:54
  90.1 8.5 %collective-permute-start.22 = (bf16[64,1536]{1,0:T(8,128)(2,1)S(1)}, bf16[64,1536]{1,0:T(8,128)(2,1)S(1)}, u32[]{:S(2)}, u32[]{:S(2)}) collective-permute-start(bf16[64,1536]{1,0:T(8,128)(2,1)S(1)} %get-tuple-element.60), channel_id=1, source_target_pairs={{0,6},{1,3},{2,0},{3,5},{4,2},{5,7},{6,4},{7,1},{8,14},{9,11},{10,... | collective-permute-start | bytes 589832 | tf_op jit(solution)/shard_map/ppermute | solution.py:54
  91.8 6.8 %collective-permute-start.23 = (bf16[64,1536]{1,0:T(8,128)(2,1)S(1)}, bf16[64,1536]{1,0:T(8,128)(2,1)S(1)}, u32[]{:S(2)}, u32[]{:S(2)}) collective-permute-start(bf16[64,1536]{1,0:T(8,128)(2,1)S(1)} %get-tuple-element.61), channel_id=1, source_target_pairs={{0,2},{1,7},{2,4},{3,1},{4,6},{5,3},{6,0},{7,5},{8,10},{9,15},{10,... | collective-permute-start | bytes 589832 | tf_op jit(solution)/shard_map/ppermute | solution.py:54
  96.8 6.9 %collective-permute-start.39 = (bf16[64,1408]{1,0:T(8,128)(2,1)S(1)}, bf16[64,1408]{1,0:T(8,128)(2,1)S(1)}, u32[]{:S(2)}, u32[]{:S(2)}) collective-permute-start(bf16[64,1408]{1,0:T(8,128)(2,1)S(1)} %shard_map.141.r0), channel_id=1, source_target_pairs={{0,2},{1,3},{2,0},{3,1},{4,6},{5,7},{6,4},{7,5},{8,10},{9,11},{10,... | collective-permute-start | bytes 540680 | tf_op jit(solution)/shard_map/ppermute | solution.py:54
  99.1 7.2 %collective-permute-start.24 = (bf16[64,1536]{1,0:T(8,128)(2,1)S(1)}, bf16[64,1536]{1,0:T(8,128)(2,1)S(1)}, u32[]{:S(2)}, u32[]{:S(2)}) collective-permute-start(bf16[64,1536]{1,0:T(8,128)(2,1)S(1)} %shard_map.133.r0), channel_id=1, source_target_pairs={{0,2},{1,3},{2,0},{3,1},{4,6},{5,7},{6,4},{7,5},{8,10},{9,11},{10,... | collective-permute-start | bytes 589832 | tf_op jit(solution)/shard_map/ppermute | solution.py:54
  99.2 10.1 %collective-permute-start.40 = (bf16[64,1408]{1,0:T(8,128)(2,1)S(1)}, bf16[64,1408]{1,0:T(8,128)(2,1)S(1)}, u32[]{:S(2)}, u32[]{:S(2)}) collective-permute-start(bf16[64,1408]{1,0:T(8,128)(2,1)S(1)} %shard_map.141.r0), channel_id=1, source_target_pairs={{0,1},{1,0},{2,3},{3,2},{4,5},{5,4},{6,7},{7,6},{8,9},{9,8},{10,11... | collective-permute-start | bytes 540680 | tf_op jit(solution)/shard_map/ppermute | solution.py:54
  103.7 5.6 %collective-permute-start.41 = (bf16[64,1408]{1,0:T(8,128)(2,1)S(1)}, bf16[64,1408]{1,0:T(8,128)(2,1)S(1)}, u32[]{:S(2)}, u32[]{:S(2)}) collective-permute-start(bf16[64,1408]{1,0:T(8,128)(2,1)S(1)} %collective-permute-done.39.r1), channel_id=1, source_target_pairs={{0,1},{1,0},{2,3},{3,2},{4,5},{5,4},{6,7},{7,6},{8,9},{9,8},{10,11... | collective-permute-start | bytes 540680 | tf_op jit(solution)/shard_map/ppermute | solution.py:54
  106.3 11.0 %collective-permute-start.25 = (bf16[64,1536]{1,0:T(8,128)(2,1)S(1)}, bf16[64,1536]{1,0:T(8,128)(2,1)S(1)}, u32[]{:S(2)}, u32[]{:S(2)}) collective-permute-start(bf16[64,1536]{1,0:T(8,128)(2,1)S(1)} %shard_map.133.r0), channel_id=1, source_target_pairs={{0,1},{1,0},{2,3},{3,2},{4,5},{5,4},{6,7},{7,6},{8,9},{9,8},{10,11... | collective-permute-start | bytes 589832 | tf_op jit(solution)/shard_map/ppermute | solution.py:54
  106.3 11.0 %collective-permute-start.26 = (bf16[64,1536]{1,0:T(8,128)(2,1)S(1)}, bf16[64,1536]{1,0:T(8,128)(2,1)S(1)}, u32[]{:S(2)}, u32[]{:S(2)}) collective-permute-start(bf16[64,1536]{1,0:T(8,128)(2,1)S(1)} %collective-permute-done.24.r1), channel_id=1, source_target_pairs={{0,1},{1,0},{2,3},{3,2},{4,5},{5,4},{6,7},{7,6},{8,9},{9,8},{10,11... | collective-permute-start | bytes 589832 | tf_op jit(solution)/shard_map/ppermute | solution.py:54
  117.2 8.5 %collective-permute-start.42 = (bf16[128,1408]{1,0:T(8,128)(2,1)S(1)}, bf16[128,1408]{1,0:T(8,128)(2,1)S(1)}, u32[]{:S(2)}, u32[]{:S(2)}) collective-permute-start(bf16[128,1408]{1,0:T(8,128)(2,1)S(1)} %get-tuple-element.81), channel_id=1, source_target_pairs={{0,1},{1,0},{2,3},{3,2},{4,5},{5,4},{6,7},{7,6},{8,9},{9,8},{10,11... | collective-permute-start | bytes 1081352 | tf_op jit(solution)/shard_map/ppermute | solution.py:54
  125.2 1.9 %collective-permute-start.27 = (bf16[128,1408]{1,0:T(8,128)(2,1)S(1)}, bf16[128,1408]{1,0:T(8,128)(2,1)S(1)}, u32[]{:S(2)}, u32[]{:S(2)}) collective-permute-start(bf16[128,1408]{1,0:T(8,128)(2,1)S(1)} %get-tuple-element.65), channel_id=1, source_target_pairs={{0,1},{1,0},{2,3},{3,2},{4,5},{5,4},{6,7},{7,6},{8,9},{9,8},{10,11... | collective-permute-start | bytes 1081352 | tf_op jit(solution)/shard_map/ppermute | solution.py:54
  125.8 10.1 %collective-permute-start.43 = (bf16[128,1408]{1,0:T(8,128)(2,1)S(1)}, bf16[128,1408]{1,0:T(8,128)(2,1)S(1)}, u32[]{:S(2)}, u32[]{:S(2)}) collective-permute-start(bf16[128,1408]{1,0:T(8,128)(2,1)S(1)} %shard_map.143.own_ref), channel_id=1, source_target_pairs={{0,2},{1,3},{2,0},{3,1},{4,6},{5,7},{6,4},{7,5},{8,10},{9,11},{10,... | collective-permute-start | bytes 1081352 | tf_op jit(solution)/shard_map/ppermute | solution.py:54
  127.1 16.5 %collective-permute-start.28 = (bf16[128,1408]{1,0:T(8,128)(2,1)S(1)}, bf16[128,1408]{1,0:T(8,128)(2,1)S(1)}, u32[]{:S(2)}, u32[]{:S(2)}) collective-permute-start(bf16[128,1408]{1,0:T(8,128)(2,1)S(1)} %shard_map.135.own_ref), channel_id=1, source_target_pairs={{0,2},{1,3},{2,0},{3,1},{4,6},{5,7},{6,4},{7,5},{8,10},{9,11},{10,... | collective-permute-start | bytes 1081352 | tf_op jit(solution)/shard_map/ppermute | solution.py:54
  136.0 8.6 %collective-permute-start.44 = (bf16[128,1408]{1,0:T(8,128)(2,1)S(1)}, bf16[128,1408]{1,0:T(8,128)(2,1)S(1)}, u32[]{:S(2)}, u32[]{:S(2)}) collective-permute-start(bf16[128,1408]{1,0:T(8,128)(2,1)S(1)} %shard_map.144.own_ref), channel_id=1, source_target_pairs={{0,1},{1,0},{2,3},{3,2},{4,5},{5,4},{6,7},{7,6},{8,9},{9,8},{10,11... | collective-permute-start | bytes 1081352 | tf_op jit(solution)/shard_map/ppermute | solution.py:54
  143.7 3.0 %collective-permute-start.29 = (bf16[128,1408]{1,0:T(8,128)(2,1)S(1)}, bf16[128,1408]{1,0:T(8,128)(2,1)S(1)}, u32[]{:S(2)}, u32[]{:S(2)}) collective-permute-start(bf16[128,1408]{1,0:T(8,128)(2,1)S(1)} %shard_map.136.own_ref), channel_id=1, source_target_pairs={{0,1},{1,0},{2,3},{3,2},{4,5},{5,4},{6,7},{7,6},{8,9},{9,8},{10,11... | collective-permute-start | bytes 1081352 | tf_op jit(solution)/shard_map/ppermute | solution.py:54
  (10 other events, 71.4 us)
where the time goes:
time: 149 us
  starting transfers between devices  58 us (39%)
  Pallas kernels  47.1 us (32%)
  waiting for transfers between devices  35.7 us (24%)
  local copies, waits for them, and re-layouts  7.02 us (5%)
    ppermute x45, starting transfers between devices, send(): return lax.ppermute(value, AXES, pairs)  58 us
    ppermute x45, waiting for transfers between devices, send(): return lax.ppermute(value, AXES, pairs)  35.7 us
    pallas_call x2, Pallas kernels, tower_forward(): pl.pallas_call(forward_body, grid_spec=pltpu.PrefetchScalarGridSpec(num_s...  16.2 us
    pallas_call x2, Pallas kernels, tower_backward(): pl.pallas_call(backward_body, grid=(steps,), in_specs=[pl.BlockSpec(block...  15.7 us
    pallas_call x21, Pallas kernels, call(): pl.pallas_call(body, out_shape=outs, in_specs=specs, out_specs=[pl.BlockS...  15.2 us
    unnamed x26, local copies, waits for them, and re-layouts  5.61 us
  transfers between devices with their start and end apart: 45, of which 11 were waited for; matrix products, arithmetic and copies ran while one was open for 0% of the time, Pallas kernels for 23%

commit v1 on v0

--- a/solution.py
+++ b/solution.py
@@ -58,20 +58,27 @@
     return lax.dot_general(a, b, (((left,), (right,)), ((), ())), preferred_element_type=f32)
 
 
-def call(body, outs, args, scalar=None, flops=1 << 20, **options):
+def skipping(body, first, count, *refs):
+    body(*refs[:first], *refs[first + count :])
+
+
+def call(body, outs, args, scalar=None, after=(), flops=1, **options):
     specs = [pl.BlockSpec(memory_space=pltpu.VMEM) for _ in args]
+    if after:
+        count = len(args) + (scalar is not None)
+        specs += [pl.BlockSpec(memory_space=pl.ANY) for _ in after]
+        args = list(args) + list(after)
+        body = functools.partial(skipping, body, count, len(after))
     if scalar is not None:
         specs = [pl.BlockSpec(memory_space=pltpu.SMEM)] + specs
         args = [scalar] + list(args)
-    moved = sum(int(np.prod(o.shape)) * o.dtype.itemsize for o in outs)
-    moved += sum(int(np.prod(a.shape)) * a.dtype.itemsize for a in args)
     return pl.pallas_call(
         body,
         out_shape=outs,
         in_specs=specs,
         out_specs=[pl.BlockSpec(memory_space=pltpu.VMEM) for _ in outs],
         compiler_params=pltpu.CompilerParams(vmem_limit_bytes=30 << 20),
-        cost_estimate=pl.CostEstimate(flops=flops, bytes_accessed=moved, transcendentals=0),
+        cost_estimate=pl.CostEstimate(flops=flops, bytes_accessed=1, transcendentals=0),
         **options,
     )(*args)
 
@@ -110,72 +117,99 @@
 CUBIC = 0.044715
 
 
-def forward_body(mine, x_ref, gain_ref, up_ref, down_ref, pre_ref, keep_ref, send_ref, norm, total):
-    step = pl.program_id(0)
-
-    @pl.when(step == 0)
-    def _():
-        for place in range(4):
-            start = pl.multiple_of((place ^ mine[0]) * BLOCK, BLOCK)
-            unit, _ = centred(x_ref[pl.ds(start, BLOCK), :].astype(f32))
-            norm[place * BLOCK : (place + 1) * BLOCK, :] = (unit * gain_ref[...]).astype(bf16)
-
+def normed_rows(mine, x_ref, gain_ref, norm):
+    gain = gain_ref[...].reshape(1, WIDTH)
+    for place in range(4):
+        start = pl.multiple_of((place ^ mine[0]) * BLOCK, BLOCK)
+        unit, _ = centred(x_ref[pl.ds(start, BLOCK), :].astype(f32))
+        norm[place * BLOCK : (place + 1) * BLOCK, :] = (unit * gain).astype(bf16)
+
+
+def gelu(pre):
+    return (0.5 * pre * (1.0 + jnp.tanh(SLOPE * (pre + CUBIC * pre * pre * pre)))).astype(bf16)
+
+
+def forward_body(mine, x_ref, gain_ref, up_ref, down_ref, pre_ref, keep_ref, rest_ref, norm):
+    normed_rows(mine, x_ref, gain_ref, norm)
     pre = contract(norm[...], up_ref[...], 1, 0)
     pre_ref[...] = pre
-    act = 0.5 * pre * (1.0 + jnp.tanh(SLOPE * (pre + CUBIC * pre * pre * pre)))
-    part = contract(act.astype(bf16), down_ref[...], 1, 0)
-
-    @pl.when(step == 0)
-    def _():
-        total[...] = part
-
-    @pl.when(step > 0)
-    def _():
-        total[...] += part
-
-    @pl.when(step == pl.num_programs(0) - 1)
-    def _():
-        keep_ref[...] = total[0:128, :]
-        send_ref[...] = total[128:256, :].astype(bf16)
-
-
-def tower_forward(mine, tokens, gain, up, down):
-    steps = HIDDEN // FF_STEP
-    fixed = lambda i, m: (0, 0)
+    part = contract(gelu(pre), down_ref[...], 1, 0)
+    keep_ref[...] = part[0:128, :]
+    rest_ref[...] = part[128:256, :]
+
+
+UP_CUTS = ((0, 512), (512, 1024), (1024, 1408))
+DOWN_CUTS = ((0, 768), (768, 1536))
+
+
+def streamed_body(
+    mine, x_ref, gain_ref, up_hbm, down_hbm, pre_ref, keep_ref, send_ref, norm, up_ref, down_ref, sems
+):
+    ups = [
+        pltpu.make_async_copy(up_hbm.at[a:b], up_ref.at[a:b], sems.at[i])
+        for i, (a, b) in enumerate(UP_CUTS)
+    ]
+    downs = [
+        pltpu.make_async_copy(down_hbm.at[a:b], down_ref.at[a:b], sems.at[len(ups) + i])
+        for i, (a, b) in enumerate(DOWN_CUTS)
+    ]
+    for copy in ups + downs:
+        copy.start()
+    normed_rows(mine, x_ref, gain_ref, norm)
+    for copy, (a, b) in zip(ups, UP_CUTS):
+        copy.wait()
+        part = contract(norm[:, a:b], up_ref[a:b, :], 1, 0)
+        pre_ref[...] = part if a == 0 else pre_ref[...] + part
+    for copy, (a, b) in zip(downs, DOWN_CUTS):
+        act = gelu(pre_ref[:, a:b])
+        copy.wait()
+        part = contract(act, down_ref[a:b, :], 1, 0)
+        if a == 0:
+            keep_ref[...] = part[0:128, :]
+            rest = part[128:256, :]
+        else:
+            keep_ref[...] += part[0:128, :]
+            send_ref[...] = (rest + part[128:256, :]).astype(bf16)
+
+
+TOWER = dict(flops=4 * 256 * WIDTH * HIDDEN)
+
+
+def tower_forward(mine, tokens, gain, up, down, after):
+    return call(
+        forward_body,
+        [shape(256, HIDDEN, f32), shape(128, WIDTH, f32), shape(128, WIDTH, f32)],
+        [tokens, gain, up, down],
+        scalar=mine,
+        after=after,
+        scratch_shapes=[pltpu.VMEM((256, WIDTH), bf16)],
+        **TOWER,
+    )
+
+
+def tower_streamed(mine, tokens, gain, up, down):
+    vmem, hbm = pl.BlockSpec(memory_space=pltpu.VMEM), pl.BlockSpec(memory_space=pl.ANY)
     return pl.pallas_call(
-        forward_body,
-        grid_spec=pltpu.PrefetchScalarGridSpec(
-            num_scalar_prefetch=1,
-            grid=(steps,),
-            in_specs=[
-                pl.BlockSpec((256, WIDTH), fixed),
-                pl.BlockSpec((1, WIDTH), fixed),
-                pl.BlockSpec((WIDTH, FF_STEP), lambda i, m: (0, i)),
-                pl.BlockSpec((FF_STEP, WIDTH), lambda i, m: (i, 0)),
-            ],
-            out_specs=[
-                pl.BlockSpec((256, FF_STEP), lambda i, m: (0, i)),
-                pl.BlockSpec((128, WIDTH), fixed),
-                pl.BlockSpec((128, WIDTH), fixed),
-            ],
-            scratch_shapes=[pltpu.VMEM((256, WIDTH), bf16), pltpu.VMEM((256, WIDTH), f32)],
+        streamed_body,
+        in_specs=[pl.BlockSpec(memory_space=pltpu.SMEM), vmem, vmem, hbm, hbm],
+        out_specs=[vmem, vmem, vmem],
+        out_shape=[shape(256, HIDDEN, f32), shape(128, WIDTH, f32), shape(128, WIDTH, bf16)],
+        scratch_shapes=[
+            pltpu.VMEM((256, WIDTH), bf16),
+            pltpu.VMEM((WIDTH, HIDDEN), bf16),
+            pltpu.VMEM((HIDDEN, WIDTH), bf16),
+            pltpu.SemaphoreType.DMA((len(UP_CUTS) + len(DOWN_CUTS),)),
+        ],
+        compiler_params=pltpu.CompilerParams(vmem_limit_bytes=58 << 20),
+        cost_estimate=pl.CostEstimate(
+            flops=1, bytes_accessed=1, transcendentals=0
         ),
-        out_shape=[shape(256, HIDDEN, f32), shape(128, WIDTH, f32), shape(128, WIDTH, bf16)],
-        compiler_params=pltpu.CompilerParams(vmem_limit_bytes=30 << 20),
-        cost_estimate=pl.CostEstimate(
-            flops=4 * 256 * WIDTH * HIDDEN, bytes_accessed=12 << 20, transcendentals=256 * HIDDEN
-        ),
-    )(mine, tokens, gain.reshape(1, WIDTH), up, down)
-
-
-def backward_body(r0, r1, r2, r3, pre_ref, up_ref, down_ref, keep_ref, send_ref, given, total):
-    step = pl.program_id(0)
-
-    @pl.when(step == 0)
-    def _():
-        for place, ref in enumerate((r0, r1, r2, r3)):
-            given[place * BLOCK : (place + 1) * BLOCK, :] = ref[:, 0:WIDTH]
-
+    )(mine, tokens, gain, up, down)
+
+
+def backward_body(r0, r1, r2, r3, pre_ref, up_ref, down_ref, keep_ref, send_ref, given):
+    for place, ref in enumerate((r0, r1, r2, r3)):
+        given[place * BLOCK : (place + 1) * BLOCK, :] = ref[:, 0:WIDTH]
     d_act = contract(given[...], down_ref[...], 1, 1)
     pre = pre_ref[...]
     square = pre * pre
@@ -184,41 +218,18 @@
         SLOPE * (1.0 + 3.0 * CUBIC * square)
     )
     part = contract((d_act * slope).astype(bf16), up_ref[...], 1, 1)
-
-    @pl.when(step == 0)
-    def _():
-        total[...] = part
-
-    @pl.when(step > 0)
-    def _():
-        total[...] += part
-
-    @pl.when(step == pl.num_programs(0) - 1)
-    def _():
-        keep_ref[...] = total[0:128, :]
-        send_ref[...] = total[128:256, :].astype(bf16)
-
-
-def tower_backward(blocks, pre, up, down):
-    steps = HIDDEN // FF_STEP
-    fixed = lambda i: (0, 0)
-    return pl.pallas_call(
+    keep_ref[...] = part[0:128, :]
+    send_ref[...] = part[128:256, :].astype(bf16)
+
+
+def tower_backward(blocks, pre, up, down, after=()):
+    return call(
         backward_body,
-        grid=(steps,),
-        in_specs=[pl.BlockSpec(block.shape, fixed) for block in blocks]
-        + [
-            pl.BlockSpec((256, FF_STEP), lambda i: (0, i)),
-            pl.BlockSpec((WIDTH, FF_STEP), lambda i: (0, i)),
-            pl.BlockSpec((FF_STEP, WIDTH), lambda i: (i, 0)),
-        ],
-        out_specs=[pl.BlockSpec((128, WIDTH), fixed), pl.BlockSpec((128, WIDTH), fixed)],
-        scratch_shapes=[pltpu.VMEM((256, WIDTH), bf16), pltpu.VMEM((256, WIDTH), f32)],
-        out_shape=[shape(128, WIDTH, f32), shape(128, WIDTH, bf16)],
-        compiler_params=pltpu.CompilerParams(vmem_limit_bytes=30 << 20),
-        cost_estimate=pl.CostEstimate(
-            flops=4 * 256 * WIDTH * HIDDEN, bytes_accessed=12 << 20, transcendentals=256 * HIDDEN
-        ),
-    )(*blocks, pre, up, down)
+        [shape(128, WIDTH, f32), shape(128, WIDTH, bf16)],
+        [*blocks, pre, up, down],
+        after=after,
+        scratch_shapes=[pltpu.VMEM((256, WIDTH), bf16)],
+    )
 
 
 def halve_body(keep_ref, got_ref, own_ref, send_ref):
@@ -230,37 +241,50 @@
     start = pl.multiple_of(mine[0] * BLOCK, BLOCK)
     resid = own_ref[...] + got_ref[...].astype(f32) + x_ref[pl.ds(start, BLOCK), :].astype(f32)
     resid_ref[...] = resid
-    normed = centred(resid)[0] * gain_ref[...]
+    normed = centred(resid)[0] * gain_ref[...].reshape(1, WIDTH)
     scale = lax.rsqrt(jnp.sum(normed * normed, axis=-1, keepdims=True) + epsilon)
     z_ref[...] = (normed * scale).astype(bf16)
 
 
-def scattered_embed(mine, keep, sent, tokens, final_gain):
+def rounded_body(rest_ref, send_ref):
+    send_ref[...] = rest_ref[...].astype(bf16)
+
+
+def rounded(rest, after):
+    return call(rounded_body, [shape(128, WIDTH, bf16)], [rest], after=after)[0]
+
+
+def scatter_half(keep, sent):
     got = send(sent, SIBLING)
-    own, sent = call(halve_body, [shape(BLOCK, WIDTH, f32), shape(BLOCK, WIDTH, bf16)], [keep, got])
+    return call(halve_body, [shape(BLOCK, WIDTH, f32), shape(BLOCK, WIDTH, bf16)], [keep, got])
+
+
+def scattered_embed(mine, own, sent, tokens, final_gain, after=()):
     got = send(sent, Z_PAIR)
     return call(
         embed_body,
         [shape(BLOCK, WIDTH, f32), shape(BLOCK, WIDTH, bf16)],
-        [own, got, tokens, final_gain.reshape(1, WIDTH)],
+        [own, got, tokens, final_gain],
         scalar=mine,
-    )
-
-
-def stack_body(first_ref, second_ref, out_ref):
-    out_ref[0:BLOCK, :] = first_ref[...]
-    out_ref[BLOCK:128, :] = second_ref[...]
-
-
-def stacked(first, second):
-    return call(stack_body, [shape(128, WIDTH, bf16)], [first, second])[0]
-
-
-def gather_plane(own):
+        after=after,
+    )
+
+
+def stack_body(*refs):
+    for place, ref in enumerate(refs[:-1]):
+        refs[-1][place * BLOCK : (place + 1) * BLOCK, :] = ref[...]
+
+
+def stacked(*blocks, after=()):
+    rows, columns = len(blocks) * BLOCK, blocks[0].shape[1]
+    return call(stack_body, [shape(rows, columns, bf16)], list(blocks), after=after)[0]
+
+
+def gather_plane(own, waited):
     before = send(own, first_ring(1))
     across = send(own, first_ring(2))
     after = send(own, first_ring(-1))
-    near = (stacked(own, before), stacked(after, across))
+    near = (stacked(own, before, after=waited), stacked(after, across))
     left = [send(near[0], second_ring(1)), None]
     right = [None, send(near[1], second_ring(-1))]
     left[1] = send(near[1], second_ring(1))
@@ -273,8 +297,8 @@
     ahead = send(own, Z_OUT)
     behind = send(own, Z_BACK)
     across = send(ahead, Z_OUT)
-    blocks = [own, ahead, behind, across]
-    return blocks + [send(block, SIBLING) for block in blocks]
+    blocks = stacked(own, ahead, behind, across)
+    return blocks, send(blocks, SIBLING)
 
 
 def pair_chunk(images, texts, has_own):
@@ -296,12 +320,12 @@
 
 
 def early_body(*refs):
-    image_refs, refs = refs[:8], refs[8:]
+    image_refs, refs = refs[:2], refs[2:]
     near0, near1, left0, left1, right0, right1 = refs[:6]
     image_ref, total_ref, loss_ref, near_ref, left_keep, left_send, right_send, right_keep = refs[6:14]
     texts = refs[14]
     for place, ref in enumerate(image_refs):
-        image_ref[place * BLOCK : (place + 1) * BLOCK, :] = ref[...]
+        image_ref[place * 256 : (place + 1) * 256, :] = ref[...]
     losses = 0.0
     for chunk, parts in enumerate(((near0, near1), (left0, left1), (right0, right1))):
         texts[0:128, :] = parts[0][...]
@@ -338,14 +362,12 @@
         [shape(512, WIDTH, bf16), shape(512, WIDTH, f32), shape(512, 128, f32)]
         + [shape(256, WIDTH, f32), half32, half16, half16, half32],
         [*images, *near, *left, *right],
-        flops=6 * 512 * 768 * WIDTH,
         scratch_shapes=[pltpu.VMEM((256, WIDTH), bf16)],
     )
     far0, far1, image_keep, image_send = call(
         late_body,
         [half16, half16, shape(256, PACKED, f32), shape(256, PACKED, bf16)],
         [image, total, loss, *far],
-        flops=6 * 512 * 256 * WIDTH,
         scratch_shapes=[pltpu.VMEM((256, WIDTH), bf16)],
     )
     return near_grad, left_keep, left_send, right_send, right_keep, far0, far1, image_keep, image_send
@@ -376,25 +398,7 @@
 def text_head_body(own_ref, before_ref, after_ref, across_ref, resid_ref, gain_ref, out_ref):
     d_embed = own_ref[...] + before_ref[...].astype(f32)
     d_embed = d_embed + after_ref[...].astype(f32) + across_ref[...].astype(f32)
-    out_ref[...] = head_back(resid_ref[...], gain_ref[...], d_embed).astype(bf16)
-
-
-def scatter_plane(grads, resid, gain):
-    near, left_keep, left_send, right_send, right_keep, far0, far1 = grads
-    half16, block16 = shape(128, WIDTH, bf16), shape(BLOCK, WIDTH, bf16)
-    l1 = send(left_send, second_ring(-1))
-    r0 = send(right_send, second_ring(1))
-    got0 = send(far0, second_ring(-1))
-    got1 = send(far1, second_ring(1))
-    l0 = send(call(joined_body, [half16], [left_keep, got0])[0], second_ring(-1))
-    r1 = send(call(joined_body, [half16], [right_keep, got1])[0], second_ring(1))
-    own, before, after, across = call(
-        near_body, [shape(BLOCK, WIDTH, f32), block16, block16, block16], [near, l0, l1, r0, r1]
-    )
-    across = send(across, first_ring(2))
-    before = send(before, first_ring(-1))
-    after = send(after, first_ring(1))
-    return call(text_head_body, [block16], [own, before, after, across, resid, gain.reshape(1, WIDTH)])[0]
+    out_ref[...] = head_back(resid_ref[...], gain_ref[...].reshape(1, WIDTH), d_embed).astype(bf16)
 
 
 def add_packed(values, loss, ref, start):
@@ -427,18 +431,42 @@
     values, loss = packed_rows(near_ref, 0, BLOCK)
     values, loss = add_packed(values, loss, ahead_ref, 0)
     values, loss = add_packed(values, loss, behind_ref, 0)
-    pack(out_ref, 0, head_back(resid_ref[...], gain_ref[...], values), loss)
-
-
-def scatter_column(keep, sent, resid, gain):
-    block16 = shape(BLOCK, PACKED, bf16)
+    pack(out_ref, 0, head_back(resid_ref[...], gain_ref[...].reshape(1, WIDTH), values), loss)
+
+
+def scatter_both(grads, keep, sent, text_head, image_head):
+    near, left_keep, left_send, right_send, right_keep, far0, far1 = grads
+    half16, block16 = shape(128, WIDTH, bf16), shape(BLOCK, WIDTH, bf16)
+    packed16 = shape(BLOCK, PACKED, bf16)
     got = send(sent, SIBLING)
-    near, across = call(column_first_body, [shape(3 * BLOCK, PACKED, f32), block16], [keep, got])
-    got = send(across, Z_BACK)
-    ahead, behind = call(column_second_body, [block16, block16], [near, got])
-    ahead = send(ahead, Z_BACK)
-    behind = send(behind, Z_OUT)
-    return call(image_head_body, [block16], [near, ahead, behind, resid, gain.reshape(1, WIDTH)])[0]
+    got0 = send(far0, second_ring(-1))
+    got1 = send(far1, second_ring(1))
+    l1 = send(left_send, second_ring(-1))
+    r0 = send(right_send, second_ring(1))
+    column, across = call(column_first_body, [shape(3 * BLOCK, PACKED, f32), packed16], [keep, got])
+    back = send(across, Z_BACK)
+
+    l0 = call(joined_body, [half16], [left_keep, got0], after=[across])[0]
+    r1 = call(joined_body, [half16], [right_keep, got1], after=[across])[0]
+    l0 = send(l0, second_ring(-1))
+    r1 = send(r1, second_ring(1))
+    ahead, behind = call(column_second_body, [packed16, packed16], [column, back])
+    got_ahead = send(ahead, Z_BACK)
+    got_behind = send(behind, Z_OUT)
+
+    own, before, after, across = call(
+        near_body,
+        [shape(BLOCK, WIDTH, f32), block16, block16, block16],
+        [near, l0, l1, r0, r1],
+        after=[ahead],
+        flops=2 << 30,
+    )
+    across = send(across, first_ring(2))
+    before = send(before, first_ring(-1))
+    after = send(after, first_ring(1))
+    image = call(image_head_body, [packed16], [column, got_ahead, got_behind, *image_head])[0]
+    text = call(text_head_body, [block16], [own, before, after, across, *text_head], after=[image], flops=2 << 30)[0]
+    return image, text
 
 
 def gather_rows(own):
@@ -454,19 +482,20 @@
 
 def grad_body(has_loss, mine, x_ref, gain_ref, r0, r1, r2, r3, own_ref, got_ref, out_ref, *loss_ref):
     losses = jnp.zeros((1, 256), f32)
-    for place, ref in enumerate((r0, r1, r2, r3)):
+    for place in range(4):
         target = place ^ mine[0]
         start = pl.multiple_of(target * BLOCK, BLOCK)
         unit, inverse = centred(x_ref[pl.ds(start, BLOCK), :].astype(f32))
-        half = own_ref if place < 2 else got_ref
-        first = (place % 2) * BLOCK
-        d_norm = half[first : first + BLOCK, :].astype(f32)
-        back = centred_back(unit, inverse, d_norm * gain_ref[...])
-        out_ref[pl.ds(start, BLOCK), :] = ref[:, 0:WIDTH].astype(f32) + back
+        given, norms = (r0, r1, r2, r3)[place], own_ref if place < 2 else got_ref
+        rows = slice((place % 2) * BLOCK, (place % 2 + 1) * BLOCK)
+        d_norm = norms[rows, :].astype(f32)
+        back = centred_back(unit, inverse, d_norm * gain_ref[...].reshape(1, WIDTH))
+        out_ref[pl.ds(start, BLOCK), :] = given[:, 0:WIDTH].astype(f32) + back
         if has_loss:
             row = lax.broadcasted_iota(jnp.int32, (BLOCK, 256), 0)
             column = lax.broadcasted_iota(jnp.int32, (BLOCK, 256), 1)
-            spread = jnp.where(column == target * BLOCK + row, loss_of(ref[:, WIDTH:PACKED]), 0.0)
+            loss = loss_of(given[:, WIDTH:PACKED])
+            spread = jnp.where(column == target * BLOCK + row, loss, 0.0)
             losses = losses + jnp.sum(spread, axis=0, keepdims=True)
     if has_loss:
         loss_ref[0][...] = losses
@@ -483,7 +512,7 @@
     return call(
         functools.partial(grad_body, has_loss),
         outs,
-        [tokens, gain.reshape(1, WIDTH), *blocks, own, got],
+        [tokens, gain, *blocks, own, got],
         scalar=mine,
     )
 
@@ -503,21 +532,27 @@
     mp = lax.axis_index("mp")
     mine = (2 * (mp % 2) + mp // 2).astype(jnp.int32).reshape(1)
 
-    text_pre, keep, sent = tower_forward(mine, text_in, text_gain, text_up, text_down)
-    text_resid, z_text = scattered_embed(mine, keep, sent, text_in, text_final)
-    near, left, right, far = gather_plane(z_text)
-    image_pre, keep, sent = tower_forward(mine, image_in, image_gain, image_up, image_down)
-    image_resid, z_image = scattered_embed(mine, keep, sent, image_in, image_final)
+    text_pre, keep, sent = tower_streamed(mine, text_in, text_gain, text_up, text_down)
+    own, sent = scatter_half(keep, sent)
+    image_pre, image_keep, image_rest = tower_forward(
+        mine, image_in, image_gain, image_up, image_down, [sent]
+    )
+    text_resid, z_text = scattered_embed(mine, own, sent, text_in, text_final, [image_rest])
+    own, sent = scatter_half(image_keep, rounded(image_rest, [z_text]))
+    near, left, right, far = gather_plane(z_text, [sent])
+    image_resid, z_image = scattered_embed(mine, own, sent, image_in, image_final)
     images = gather_column(z_image)
 
     *text_grads, keep, sent = pair_tile(images, near, left, right, far)
-    image_dres = gather_rows(scatter_column(keep, sent, image_resid, image_final))
+    image_own, text_own = scatter_both(
+        text_grads, keep, sent, (text_resid, text_final), (image_resid, image_final)
+    )
+    image_dres = gather_rows(image_own)
+    text_dres = gather_rows(text_own)
     keep, sent = tower_backward(image_dres, image_pre, image_up, image_down)
+    text_keep, text_sent = tower_backward(text_dres, text_pre, text_up, text_down, [sent])
     image_grad, losses = input_grad(mine, image_in, image_gain, image_dres, keep, sent, True)
-
-    text_dres = gather_rows(scatter_plane(text_grads, text_resid, text_final))
-    keep, sent = tower_backward(text_dres, text_pre, text_up, text_down)
-    text_grad = input_grad(mine, text_in, text_gain, text_dres, keep, sent, False)[0]
+    text_grad = input_grad(mine, text_in, text_gain, text_dres, text_keep, text_sent, False)[0]
     return (image_grad, text_grad, losses.reshape(256))
 
 

time: 149 us -> 134 us (0.90)
  Pallas kernels: 47.1 us -> 31.3 us
  waiting for transfers between devices: 35.7 us -> 42.8 us
  local copies, waits for them, and re-layouts: 7.02 us -> 3.4 us
  starting transfers between devices: 58 us -> 55 us
    pallas_call x4 -> x1, Pallas kernels: 31.8 us -> 7.35 us  [tower_streamed(): pl.pallas_call(streamed_body, in_specs=[pl.BlockSpec(memory_space=pltpu.S...]
    pallas_call x21 -> x26, Pallas kernels: 15.2 us -> 24 us  [call(): pl.pallas_call(body, out_shape=outs, in_specs=specs, out_specs=[pl.BlockS...]
    ppermute x45 -> x42, waiting for transfers between devices: 35.7 us -> 42.8 us  [send(): return lax.ppermute(value, AXES, pairs)]
    ppermute x45 -> x42, starting transfers between devices: 58 us -> 55 us  [send(): return lax.ppermute(value, AXES, pairs)]
    unnamed x26 -> x34, local copies, waits for them, and re-layouts: 5.61 us -> 3.4 us
  transfers between devices with their start and end apart: 45 -> 42, of which waited for: 11 -> 12; matrix products, arithmetic and copies ran while one was open for 0% -> 0% of each run, Pallas kernels for 23% -> 14%
where the time goes in v1:
time: 134 us
  starting transfers between devices  55 us (41%)
  waiting for transfers between devices  42.8 us (32%)
  Pallas kernels  31.3 us (23%)
  local copies, waits for them, and re-layouts  3.4 us (3%)
    ppermute x42, starting transfers between devices, send(): return lax.ppermute(value, AXES, pairs)  55 us
    ppermute x42, waiting for transfers between devices, send(): return lax.ppermute(value, AXES, pairs)  42.8 us
    pallas_call x26, Pallas kernels, call(): pl.pallas_call(body, out_shape=outs, in_specs=specs, out_specs=[pl.BlockS...  24 us
    pallas_call x1, Pallas kernels, tower_streamed(): pl.pallas_call(streamed_body, in_specs=[pl.BlockSpec(memory_space=pltpu.S...  7.35 us
    unnamed x34, local copies, waits for them, and re-layouts  3.4 us
  transfers between devices with their start and end apart: 42, of which 12 were waited for; matrix products, arithmetic and copies ran while one was open for 0% of the time, Pallas kernels for 14%

profile of v1, /device:TPU:1, one launch (start us, length us, event | category | flops | bytes accessed | tf_op | source)
XLA Modules:
  0.0 133.7 jit_solution(8073753030010848237)
XLA Ops:
  0.7 7.3 %shard_map.121 = (f32[256,1536]{1,0:T(8,128)}, f32[128,1408]{1,0:T(8,128)}, bf16[128,1408]{1,0:T(8,128)(2,1)}) custom-call(s32[1]{0:T(128)} %bitcast.mine.refs_0_, bf16[256,1408]{1,0:T(8,128)(2,1)} %x_ref.7, f32[1408]{0:T(1024)} %gain_ref.9, bf16[1408,1536]{1,0:T(8,128)(2,1)} %refs_5_.3, bf16[1536,1408]{1,0:T(8,128)(2,1)} %refs_6_.1), custom_call_target="tpu_custom_call" | custom-call | flops 1 | bytes 1 | tf_op jit(solution)/shard_map/pallas_call | solution.py:192
  8.0 1.5 %collective-permute-start = (bf16[128,1408]{1,0:T(8,128)(2,1)}, bf16[128,1408]{1,0:T(8,128)(2,1)S(1)}, u32[]{:S(2)}, u32[]{:S(2)}) collective-permute-start(bf16[128,1408]{1,0:T(8,128)(2,1)} %get-tuple-element.44), channel_id=1, source_target_pairs={{0,1},{1,0},{2,3},{3,2},{4,5},{5,4},{6,7},{7,6},{8,9},{9,8},{10,11... | collective-permute-start | bytes 1081352 | tf_op jit(solution)/shard_map/ppermute | solution.py:54
  9.5 1.5 %collective-permute-done.got_ref = bf16[128,1408]{1,0:T(8,128)(2,1)S(1)} collective-permute-done((bf16[128,1408]{1,0:T(8,128)(2,1)}, bf16[128,1408]{1,0:T(8,128)(2,1)S(1)}, u32[]{:S(2)}, u32[]{:S(2)}) %collective-permute-start) | collective-permute-done | bytes 360480 | tf_op jit(solution)/shard_map/ppermute | solution.py:54
  11.1 1.1 copy-done.4
  12.2 1.8 %collective-permute-start.1 = (bf16[64,1408]{1,0:T(8,128)(2,1)S(1)}, bf16[64,1408]{1,0:T(8,128)(2,1)S(1)}, u32[]{:S(2)}, u32[]{:S(2)}) collective-permute-start(bf16[64,1408]{1,0:T(8,128)(2,1)S(1)} %get-tuple-element.45.refs_5_), channel_id=1, source_target_pairs={{0,2},{1,3},{2,0},{3,1},{4,6},{5,7},{6,4},{7,5},{8,10},{9,11},{10,... | collective-permute-start | bytes 540680 | tf_op jit(solution)/shard_map/ppermute | solution.py:54
  14.1 2.2 %copy-done = bf16[1536,1408]{1,0:T(8,128)(2,1)S(1)} copy-done((bf16[1536,1408]{1,0:T(8,128)(2,1)S(1)}, bf16[1536,1408]{1,0:T(8,128)(2,1)}, u32[]{:S(2)}) %copy-start) | copy-done | bytes 4325400
  16.3 3.0 %shard_map.123 = (f32[256,1536]{1,0:T(8,128)S(1)}, f32[128,1408]{1,0:T(8,128)S(1)}, f32[128,1408]{1,0:T(8,128)S(1)}) custom-call(s32[1]{0:T(128)} %bitcast.mine.refs_0_, bf16[256,1408]{1,0:T(8,128)(2,1)S(1)} %copy-done.1, f32[1408]{0:T(1024)S(1)} %copy-done.6, bf16[1408,1536]{1,0:T(8,128)(2,1)S(1)} %bitcast.3, bf16[1536,1408]{1,0:T(8,128)(2,1)S(1)} %copy-done, ...), custom_call_target="tpu_custom_call" | custom-call | flops 2214592512 | bytes 1 | tf_op jit(solution)/shard_map/pallas_call | solution.py:75
  20.5 1.3 collective-permute-done.2.got_ref
  21.8 1.1 collective-permute-start.3
  22.9 4.7 %collective-permute-done.3.got_ref = bf16[64,1408]{1,0:T(8,128)(2,1)S(1)} collective-permute-done((bf16[64,1408]{1,0:T(8,128)(2,1)S(1)}, bf16[64,1408]{1,0:T(8,128)(2,1)S(1)}, u32[]{:S(2)}, u32[]{:S(2)}) %collective-permute-start.3) | collective-permute-done | bytes 180256 | tf_op jit(solution)/shard_map/ppermute | solution.py:54
  28.0 3.2 %collective-permute-start.4 = (bf16[64,1408]{1,0:T(8,128)(2,1)S(1)}, bf16[64,1408]{1,0:T(8,128)(2,1)S(1)}, u32[]{:S(2)}, u32[]{:S(2)}) collective-permute-start(bf16[64,1408]{1,0:T(8,128)(2,1)S(1)} %get-tuple-element.52.refs_0_), channel_id=1, source_target_pairs={{0,2},{1,7},{2,4},{3,1},{4,6},{5,3},{6,0},{7,5},{8,10},{9,15},{10,... | collective-permute-start | bytes 540680 | tf_op jit(solution)/shard_map/ppermute | solution.py:54
  31.2 2.9 %collective-permute-start.10 = (bf16[64,1408]{1,0:T(8,128)(2,1)S(1)}, bf16[64,1408]{1,0:T(8,128)(2,1)S(1)}, u32[]{:S(2)}, u32[]{:S(2)}) collective-permute-start(bf16[64,1408]{1,0:T(8,128)(2,1)S(1)} %get-tuple-element.49.refs_1_.refs_0_), channel_id=1, source_target_pairs={{0,16},{1,65},{2,18},{3,67},{4,20},{5,69},{6,22},{7,71},{8,24},{9,... | collective-permute-start | bytes 540680 | tf_op jit(solution)/shard_map/ppermute | solution.py:54
  34.2 0.8 collective-permute-start.9
  34.9 2.7 %collective-permute-start.6 = (bf16[64,1408]{1,0:T(8,128)(2,1)S(1)}, bf16[64,1408]{1,0:T(8,128)(2,1)S(1)}, u32[]{:S(2)}, u32[]{:S(2)}) collective-permute-start(bf16[64,1408]{1,0:T(8,128)(2,1)S(1)} %collective-permute-done.4.refs_1_), channel_id=1, source_target_pairs={{0,2},{1,7},{2,4},{3,1},{4,6},{5,3},{6,0},{7,5},{8,10},{9,15},{10,... | collective-permute-start | bytes 540680 | tf_op jit(solution)/shard_map/ppermute | solution.py:54
  38.3 1.4 %collective-permute-done.9.refs_0_ = bf16[64,1408]{1,0:T(8,128)(2,1)S(1)} collective-permute-done((bf16[64,1408]{1,0:T(8,128)(2,1)S(1)}, bf16[64,1408]{1,0:T(8,128)(2,1)S(1)}, u32[]{:S(2)}, u32[]{:S(2)}) %collective-permute-start.9) | collective-permute-done | bytes 180256 | tf_op jit(solution)/shard_map/ppermute | solution.py:54
  39.7 2.5 %collective-permute-start.14 = (bf16[128,1408]{1,0:T(8,128)(2,1)S(1)}, bf16[128,1408]{1,0:T(8,128)(2,1)S(1)}, u32[]{:S(2)}, u32[]{:S(2)}) collective-permute-start(bf16[128,1408]{1,0:T(8,128)(2,1)S(1)} %shard_map.130.refs_3_), channel_id=1, source_target_pairs={{0,96},{1,25},{2,98},{3,27},{4,100},{5,29},{6,102},{7,31},{8,104},... | collective-permute-start | bytes 1081352 | tf_op jit(solution)/shard_map/ppermute | solution.py:54
  42.3 1.5 %collective-permute-start.7 = (bf16[256,1408]{1,0:T(8,128)(2,1)S(1)}, bf16[256,1408]{1,0:T(8,128)(2,1)S(1)}, u32[]{:S(2)}, u32[]{:S(2)}) collective-permute-start(bf16[256,1408]{1,0:T(8,128)(2,1)S(1)} %shard_map.128.refs_0_), channel_id=1, source_target_pairs={{0,1},{1,0},{2,3},{3,2},{4,5},{5,4},{6,7},{7,6},{8,9},{9,8},{10,11... | collective-permute-start | bytes 2162696 | tf_op jit(solution)/shard_map/ppermute | solution.py:54
  44.6 1.2 collective-permute-start.12
  45.8 1.5 %collective-permute-start.13 = (bf16[128,1408]{1,0:T(8,128)(2,1)S(1)}, bf16[128,1408]{1,0:T(8,128)(2,1)S(1)}, u32[]{:S(2)}, u32[]{:S(2)}) collective-permute-start(bf16[128,1408]{1,0:T(8,128)(2,1)S(1)} %shard_map.129.refs_2_), channel_id=1, source_target_pairs={{0,96},{1,25},{2,98},{3,27},{4,100},{5,29},{6,102},{7,31},{8,104},... | collective-permute-start | bytes 1081352 | tf_op jit(solution)/shard_map/ppermute | solution.py:54
  47.2 2.5 %collective-permute-start.16 = (bf16[128,1408]{1,0:T(8,128)(2,1)S(1)}, bf16[128,1408]{1,0:T(8,128)(2,1)S(1)}, u32[]{:S(2)}, u32[]{:S(2)}) collective-permute-start(bf16[128,1408]{1,0:T(8,128)(2,1)S(1)} %collective-permute-done.14.refs_7_), channel_id=1, source_target_pairs={{0,96},{1,25},{2,98},{3,27},{4,100},{5,29},{6,102},{7,31},{8,104},... | collective-permute-start | bytes 1081352 | tf_op jit(solution)/shard_map/ppermute | solution.py:54
  49.7 2.0 %collective-permute-done.11.refs_4_ = bf16[128,1408]{1,0:T(8,128)(2,1)S(1)} collective-permute-done((bf16[128,1408]{1,0:T(8,128)(2,1)S(1)}, bf16[128,1408]{1,0:T(8,128)(2,1)S(1)}, u32[]{:S(2)}, u32[]{:S(2)}) %collective-permute-start.11) | collective-permute-done | bytes 360480 | tf_op jit(solution)/shard_map/ppermute | solution.py:54
  51.7 3.9 %collective-permute-done.12.refs_5_ = bf16[128,1408]{1,0:T(8,128)(2,1)S(1)} collective-permute-done((bf16[128,1408]{1,0:T(8,128)(2,1)S(1)}, bf16[128,1408]{1,0:T(8,128)(2,1)S(1)}, u32[]{:S(2)}, u32[]{:S(2)}) %collective-permute-start.12) | collective-permute-done | bytes 360480 | tf_op jit(solution)/shard_map/ppermute | solution.py:54
  55.6 5.8 %shard_map.131 = (bf16[512,1408]{1,0:T(8,128)(2,1)S(1)}, f32[512,1408]{1,0:T(8,128)S(1)}, f32[512,128]{1,0:T(8,128)S(1)}, f32[256,1408]{1,0:T(8,128)S(1)}, f32[1...) custom-call(bf16[256,1408]{1,0:T(8,128)(2,1)S(1)} %shard_map.128.ref, ...), custom_call_target="tpu_custom_call" | custom-call | flops 1 | bytes 1 | tf_op jit(solution)/shard_map/pallas_call | solution.py:75
  61.4 2.3 %shard_map.132 = (bf16[128,1408]{1,0:T(8,128)(2,1)S(1)}, bf16[128,1408]{1,0:T(8,128)(2,1)S(1)}, f32[256,1536]{1,0:T(8,128)S(1)}, bf16[256,1536]{1,0:T(8,128)(2,1)S(1)}) custom-call(bf16[512,1408]{1,0:T(8,128)(2,1)S(1)} %get-tuple-element.53.image_ref, f32[512,1408]{1,0:T(8,128)S(1)} %get-tuple-element.54.total_ref, ...), custom_call_target="tpu_custom_call" | custom-call | flops 1 | bytes 1 | tf_op jit(solution)/shard_map/pallas_call | solution.py:75
  63.7 1.0 collective-permute-start.17
  65.3 2.0 %collective-permute-start.27 = (bf16[128,1408]{1,0:T(8,128)(2,1)S(1)}, bf16[128,1408]{1,0:T(8,128)(2,1)S(1)}, u32[]{:S(2)}, u32[]{:S(2)}) collective-permute-start(bf16[128,1408]{1,0:T(8,128)(2,1)S(1)} %get-tuple-element.69), channel_id=1, source_target_pairs={{0,96},{1,25},{2,98},{3,27},{4,100},{5,29},{6,102},{7,31},{8,104},... | collective-permute-start | bytes 1081352 | tf_op jit(solution)/shard_map/ppermute | solution.py:54
  68.1 0.8 collective-permute-start.30
  69.0 3.4 %collective-permute-done.31.refs_1_ = bf16[128,1408]{1,0:T(8,128)(2,1)S(1)} collective-permute-done((bf16[128,1408]{1,0:T(8,128)(2,1)S(1)}, bf16[128,1408]{1,0:T(8,128)(2,1)S(1)}, u32[]{:S(2)}, u32[]{:S(2)}) %collective-permute-start.31) | collective-permute-done | bytes 360480 | tf_op jit(solution)/shard_map/ppermute | solution.py:54
  72.7 2.7 %collective-permute-start.28 = (bf16[128,1408]{1,0:T(8,128)(2,1)S(1)}, bf16[128,1408]{1,0:T(8,128)(2,1)S(1)}, u32[]{:S(2)}, u32[]{:S(2)}) collective-permute-start(bf16[128,1408]{1,0:T(8,128)(2,1)S(1)} %shard_map.140), channel_id=1, source_target_pairs={{0,96},{1,25},{2,98},{3,27},{4,100},{5,29},{6,102},{7,31},{8,104},... | collective-permute-start | bytes 1081352 | tf_op jit(solution)/shard_map/ppermute | solution.py:54
  75.4 2.0 %collective-permute-start.18 = (bf16[64,1536]{1,0:T(8,128)(2,1)S(1)}, bf16[64,1536]{1,0:T(8,128)(2,1)S(1)}, u32[]{:S(2)}, u32[]{:S(2)}) collective-permute-start(bf16[64,1536]{1,0:T(8,128)(2,1)S(1)} %get-tuple-element.59.refs_2_), channel_id=1, source_target_pairs={{0,6},{1,3},{2,0},{3,5},{4,2},{5,7},{6,4},{7,1},{8,14},{9,11},{10,... | collective-permute-start | bytes 589832 | tf_op jit(solution)/shard_map/ppermute | solution.py:54
  77.4 4.1 %collective-permute-done.18.got_ref = bf16[64,1536]{1,0:T(8,128)(2,1)S(1)} collective-permute-done((bf16[64,1536]{1,0:T(8,128)(2,1)S(1)}, bf16[64,1536]{1,0:T(8,128)(2,1)S(1)}, u32[]{:S(2)}, u32[]{:S(2)}) %collective-permute-start.18) | collective-permute-done | bytes 196640 | tf_op jit(solution)/shard_map/ppermute | solution.py:54
  82.4 2.0 %collective-permute-start.20 = (bf16[64,1536]{1,0:T(8,128)(2,1)S(1)}, bf16[64,1536]{1,0:T(8,128)(2,1)S(1)}, u32[]{:S(2)}, u32[]{:S(2)}) collective-permute-start(bf16[64,1536]{1,0:T(8,128)(2,1)S(1)} %get-tuple-element.61), channel_id=1, source_target_pairs={{0,2},{1,7},{2,4},{3,1},{4,6},{5,3},{6,0},{7,5},{8,10},{9,15},{10,... | collective-permute-start | bytes 589832 | tf_op jit(solution)/shard_map/ppermute | solution.py:54
  84.7 1.9 %collective-permute-start.33 = (bf16[64,1408]{1,0:T(8,128)(2,1)S(1)}, bf16[64,1408]{1,0:T(8,128)(2,1)S(1)}, u32[]{:S(2)}, u32[]{:S(2)}) collective-permute-start(bf16[64,1408]{1,0:T(8,128)(2,1)S(1)} %get-tuple-element.75), channel_id=1, source_target_pairs={{0,24},{1,97},{2,26},{3,99},{4,28},{5,101},{6,30},{7,103},{8,0},{9... | collective-permute-start | bytes 540680 | tf_op jit(solution)/shard_map/ppermute | solution.py:54
  86.6 1.3 collective-permute-start.35
  88.4 1.4 %collective-permute-start.21 = (bf16[64,1536]{1,0:T(8,128)(2,1)S(1)}, bf16[64,1536]{1,0:T(8,128)(2,1)S(1)}, u32[]{:S(2)}, u32[]{:S(2)}) collective-permute-start(bf16[64,1536]{1,0:T(8,128)(2,1)S(1)} %shard_map.135.r0.refs_6_), channel_id=1, source_target_pairs={{0,2},{1,3},{2,0},{3,1},{4,6},{5,7},{6,4},{7,5},{8,10},{9,11},{10,... | collective-permute-start | bytes 589832 | tf_op jit(solution)/shard_map/ppermute | solution.py:54
  89.8 4.6 %collective-permute-done.34.refs_2_ = bf16[64,1408]{1,0:T(8,128)(2,1)S(1)} collective-permute-done((bf16[64,1408]{1,0:T(8,128)(2,1)S(1)}, bf16[64,1408]{1,0:T(8,128)(2,1)S(1)}, u32[]{:S(2)}, u32[]{:S(2)}) %collective-permute-start.34) | collective-permute-done | bytes 180256 | tf_op jit(solution)/shard_map/ppermute | solution.py:54
  95.0 3.4 %collective-permute-start.22 = (bf16[64,1536]{1,0:T(8,128)(2,1)S(1)}, bf16[64,1536]{1,0:T(8,128)(2,1)S(1)}, u32[]{:S(2)}, u32[]{:S(2)}) collective-permute-start(bf16[64,1536]{1,0:T(8,128)(2,1)S(1)} %shard_map.135.r0.refs_6_), channel_id=1, source_target_pairs={{0,1},{1,0},{2,3},{3,2},{4,5},{5,4},{6,7},{7,6},{8,9},{9,8},{10,11... | collective-permute-start | bytes 589832 | tf_op jit(solution)/shard_map/ppermute | solution.py:54
  98.4 3.7 %collective-permute-start.23 = (bf16[64,1536]{1,0:T(8,128)(2,1)S(1)}, bf16[64,1536]{1,0:T(8,128)(2,1)S(1)}, u32[]{:S(2)}, u32[]{:S(2)}) collective-permute-start(bf16[64,1536]{1,0:T(8,128)(2,1)S(1)} %collective-permute-done.21.r1), channel_id=1, source_target_pairs={{0,1},{1,0},{2,3},{3,2},{4,5},{5,4},{6,7},{7,6},{8,9},{9,8},{10,11... | collective-permute-start | bytes 589832 | tf_op jit(solution)/shard_map/ppermute | solution.py:54
  102.1 1.9 %collective-permute-start.38 = (bf16[64,1408]{1,0:T(8,128)(2,1)S(1)}, bf16[64,1408]{1,0:T(8,128)(2,1)S(1)}, u32[]{:S(2)}, u32[]{:S(2)}) collective-permute-start(bf16[64,1408]{1,0:T(8,128)(2,1)S(1)} %collective-permute-done.36.refs_1_.r1), channel_id=1, source_target_pairs={{0,1},{1,0},{2,3},{3,2},{4,5},{5,4},{6,7},{7,6},{8,9},{9,8},{10,11... | collective-permute-start | bytes 540680 | tf_op jit(solution)/shard_map/ppermute | solution.py:54
  104.1 2.9 %shard_map.136 = (f32[128,1408]{1,0:T(8,128)S(1)}, bf16[128,1408]{1,0:T(8,128)(2,1)S(1)}) custom-call(bf16[64,1536]{1,0:T(8,128)(2,1)S(1)} %shard_map.135.r0.refs_6_, bf16[64,1536]{1,0:T(8,128)(2,1)S(1)} %collective-permute-done.21.r1, bf16[64,1536]{1,0:T(8,128)(2,1)S(1)} %collective-permute-done.22.r2, bf16[64,1536]{1,0:T(8,128)(2,1)S(1)} %collective-permute-done.23.r3, ...), custom_call_target="tpu_custom_call" | custom-call | flops 1 | bytes 1 | tf_op jit(solution)/shard_map/pallas_call | solution.py:75
  107.2 2.8 %shard_map.144 = (f32[128,1408]{1,0:T(8,128)S(1)}, bf16[128,1408]{1,0:T(8,128)(2,1)S(1)}) custom-call(bf16[64,1408]{1,0:T(8,128)(2,1)S(1)} %shard_map.143.refs_0_.r0, bf16[64,1408]{1,0:T(8,128)(2,1)S(1)} %collective-permute-done.36.refs_1_.r1, bf16[64,1408]{1,0:T(8,128)(2,1)S(1)} %collective-permute-done.37.refs_2_.r2, ...), custom_call_target="tpu_custom_call" | custom-call | flops 1 | bytes 1 | tf_op jit(solution)/shard_map/pallas_call | solution.py:75
  110.7 1.1 collective-permute-done.39.got_ref
  112.3 8.4 %collective-permute-done.25.got_ref = bf16[128,1408]{1,0:T(8,128)(2,1)S(1)} collective-permute-done((bf16[128,1408]{1,0:T(8,128)(2,1)S(1)}, bf16[128,1408]{1,0:T(8,128)(2,1)S(1)}, u32[]{:S(2)}, u32[]{:S(2)}) %collective-permute-start.25) | collective-permute-done | bytes 360480 | tf_op jit(solution)/shard_map/ppermute | solution.py:54
  120.8 1.3 collective-permute-start.26
  122.1 6.3 %collective-permute-done.40.got_ref = bf16[128,1408]{1,0:T(8,128)(2,1)S(1)} collective-permute-done((bf16[128,1408]{1,0:T(8,128)(2,1)S(1)}, bf16[128,1408]{1,0:T(8,128)(2,1)S(1)}, u32[]{:S(2)}, u32[]{:S(2)}) %collective-permute-start.40) | collective-permute-done | bytes 360480 | tf_op jit(solution)/shard_map/ppermute | solution.py:54
  128.5 0.9 collective-permute-start.41
  129.4 2.1 %shard_map.139 = (f32[256,1408]{1,0:T(8,128)}, f32[1,256]{1,0:T(1,128)}) custom-call(s32[1]{0:T(128)} %bitcast.mine.refs_0_, bf16[256,1408]{1,0:T(8,128)(2,1)S(1)} %copy-done.1, f32[1408]{0:T(1024)S(1)} %copy-done.6, bf16[64,1536]{1,0:T(8,128)(2,1)S(1)} %shard_map.135.r0.refs_6_, bf16[64,1536]{1,0:T(8,128)(2,1)S(1)} %collective-permute-done.21.r1, ...), custom_call_target="tpu_custom_call" | custom-call | flops 1 | bytes 1 | tf_op jit(solution)/shard_map/pallas_call | solution.py:75
  131.6 2.1 %shard_map.147 = f32[256,1408]{1,0:T(8,128)} custom-call(s32[1]{0:T(128)} %bitcast.mine.refs_0_, bf16[256,1408]{1,0:T(8,128)(2,1)S(1)} %copy-done.2, f32[1408]{0:T(1024)S(1)} %copy-done.7, bf16[64,1408]{1,0:T(8,128)(2,1)S(1)} %shard_map.143.refs_0_.r0, bf16[64,1408]{1,0:T(8,128)(2,1)S(1)} %collective-permute-done.36.refs_1_.r1, ...), custom_call_target="tpu_custom_call" | custom-call | flops 1 | bytes 1 | tf_op jit(solution)/shard_map/pallas_call | solution.py:75
  (101 shorter events, 8.7 us)
Async XLA Ops:
  0.7 13.4 %slice-start = ((s8[4325376]{0:T(1024)(128)(4,1)}), s8[4194304]{0:T(1024)(128)(4,1)S(1)}, s32[]{:S(2)}) async-start(s8[4325376]{0:T(1024)(128)(4,1)} %bitcast.2), calls=%async_computation | async-start | bytes 8388608
  0.7 13.4 %slice-start.1 = ((s8[4325376]{0:T(1024)(128)(4,1)}), s8[131072]{0:T(1024)(128)(4,1)S(1)}, s32[]{:S(2)}) async-start(s8[4325376]{0:T(1024)(128)(4,1)} %bitcast.2), calls=%async_computation.1 | async-start | bytes 262144
  0.7 13.4 %copy-start.6 = (f32[1408]{0:T(1024)S(1)}, f32[1408]{0:T(1024)}, u32[]{:S(2)}) copy-start(f32[1408]{0:T(1024)} %gain_ref.8) | copy-start | bytes 16900
  8.0 3.0 %collective-permute-start = (bf16[128,1408]{1,0:T(8,128)(2,1)}, bf16[128,1408]{1,0:T(8,128)(2,1)S(1)}, u32[]{:S(2)}, u32[]{:S(2)}) collective-permute-start(bf16[128,1408]{1,0:T(8,128)(2,1)} %get-tuple-element.44), channel_id=1, source_target_pairs={{0,1},{1,0},{2,3},{3,2},{4,5},{5,4},{6,7},{7,6},{8,9},{9,8},{10,11... | collective-permute-start | bytes 1081352 | tf_op jit(solution)/shard_map/ppermute | solution.py:54
  12.2 7.1 %collective-permute-start.1 = (bf16[64,1408]{1,0:T(8,128)(2,1)S(1)}, bf16[64,1408]{1,0:T(8,128)(2,1)S(1)}, u32[]{:S(2)}, u32[]{:S(2)}) collective-permute-start(bf16[64,1408]{1,0:T(8,128)(2,1)S(1)} %get-tuple-element.45.refs_5_), channel_id=1, source_target_pairs={{0,2},{1,3},{2,0},{3,1},{4,6},{5,7},{6,4},{7,5},{8,10},{9,11},{10,... | collective-permute-start | bytes 540680 | tf_op jit(solution)/shard_map/ppermute | solution.py:54
  19.7 2.0 %collective-permute-start.2 = (bf16[128,1408]{1,0:T(8,128)(2,1)S(1)}, bf16[128,1408]{1,0:T(8,128)(2,1)S(1)}, u32[]{:S(2)}, u32[]{:S(2)}) collective-permute-start(bf16[128,1408]{1,0:T(8,128)(2,1)S(1)} %shard_map.125), channel_id=1, source_target_pairs={{0,1},{1,0},{2,3},{3,2},{4,5},{5,4},{6,7},{7,6},{8,9},{9,8},{10,11... | collective-permute-start | bytes 1081352 | tf_op jit(solution)/shard_map/ppermute | solution.py:54
  21.8 5.8 %collective-permute-start.3 = (bf16[64,1408]{1,0:T(8,128)(2,1)S(1)}, bf16[64,1408]{1,0:T(8,128)(2,1)S(1)}, u32[]{:S(2)}, u32[]{:S(2)}) collective-permute-start(bf16[64,1408]{1,0:T(8,128)(2,1)S(1)} %get-tuple-element.51.refs_2_), channel_id=1, source_target_pairs={{0,2},{1,3},{2,0},{3,1},{4,6},{5,7},{6,4},{7,5},{8,10},{9,11},{10,... | collective-permute-start | bytes 540680 | tf_op jit(solution)/shard_map/ppermute | solution.py:54
  28.0 6.9 %collective-permute-start.4 = (bf16[64,1408]{1,0:T(8,128)(2,1)S(1)}, bf16[64,1408]{1,0:T(8,128)(2,1)S(1)}, u32[]{:S(2)}, u32[]{:S(2)}) collective-permute-start(bf16[64,1408]{1,0:T(8,128)(2,1)S(1)} %get-tuple-element.52.refs_0_), channel_id=1, source_target_pairs={{0,2},{1,7},{2,4},{3,1},{4,6},{5,3},{6,0},{7,5},{8,10},{9,15},{10,... | collective-permute-start | bytes 540680 | tf_op jit(solution)/shard_map/ppermute | solution.py:54
  31.2 7.1 %collective-permute-start.10 = (bf16[64,1408]{1,0:T(8,128)(2,1)S(1)}, bf16[64,1408]{1,0:T(8,128)(2,1)S(1)}, u32[]{:S(2)}, u32[]{:S(2)}) collective-permute-start(bf16[64,1408]{1,0:T(8,128)(2,1)S(1)} %get-tuple-element.49.refs_1_.refs_0_), channel_id=1, source_target_pairs={{0,16},{1,65},{2,18},{3,67},{4,20},{5,69},{6,22},{7,71},{8,24},{9,... | collective-permute-start | bytes 540680 | tf_op jit(solution)/shard_map/ppermute | solution.py:54
  34.2 5.5 %collective-permute-start.9 = (bf16[64,1408]{1,0:T(8,128)(2,1)S(1)}, bf16[64,1408]{1,0:T(8,128)(2,1)S(1)}, u32[]{:S(2)}, u32[]{:S(2)}) collective-permute-start(bf16[64,1408]{1,0:T(8,128)(2,1)S(1)} %get-tuple-element.49.refs_1_.refs_0_), channel_id=1, source_target_pairs={{0,24},{1,97},{2,26},{3,99},{4,28},{5,101},{6,30},{7,103},{8,0},{9... | collective-permute-start | bytes 540680 | tf_op jit(solution)/shard_map/ppermute | solution.py:54
  34.9 7.3 %collective-permute-start.5 = (bf16[64,1408]{1,0:T(8,128)(2,1)S(1)}, bf16[64,1408]{1,0:T(8,128)(2,1)S(1)}, u32[]{:S(2)}, u32[]{:S(2)}) collective-permute-start(bf16[64,1408]{1,0:T(8,128)(2,1)S(1)} %get-tuple-element.52.refs_0_), channel_id=1, source_target_pairs={{0,6},{1,3},{2,0},{3,5},{4,2},{5,7},{6,4},{7,1},{8,14},{9,11},{10,... | collective-permute-start | bytes 540680 | tf_op jit(solution)/shard_map/ppermute | solution.py:54
  34.9 7.3 %collective-permute-start.6 = (bf16[64,1408]{1,0:T(8,128)(2,1)S(1)}, bf16[64,1408]{1,0:T(8,128)(2,1)S(1)}, u32[]{:S(2)}, u32[]{:S(2)}) collective-permute-start(bf16[64,1408]{1,0:T(8,128)(2,1)S(1)} %collective-permute-done.4.refs_1_), channel_id=1, source_target_pairs={{0,2},{1,7},{2,4},{3,1},{4,6},{5,3},{6,0},{7,5},{8,10},{9,15},{10,... | collective-permute-start | bytes 540680 | tf_op jit(solution)/shard_map/ppermute | solution.py:54
  37.6 6.2 %collective-permute-start.8 = (bf16[64,1408]{1,0:T(8,128)(2,1)S(1)}, bf16[64,1408]{1,0:T(8,128)(2,1)S(1)}, u32[]{:S(2)}, u32[]{:S(2)}) collective-permute-start(bf16[64,1408]{1,0:T(8,128)(2,1)S(1)} %get-tuple-element.49.refs_1_.refs_0_), channel_id=1, source_target_pairs={{0,8},{1,33},{2,10},{3,35},{4,12},{5,37},{6,14},{7,39},{8,16},{9,4... | collective-permute-start | bytes 540680 | tf_op jit(solution)/shard_map/ppermute | solution.py:54
  39.7 7.6 %collective-permute-start.14 = (bf16[128,1408]{1,0:T(8,128)(2,1)S(1)}, bf16[128,1408]{1,0:T(8,128)(2,1)S(1)}, u32[]{:S(2)}, u32[]{:S(2)}) collective-permute-start(bf16[128,1408]{1,0:T(8,128)(2,1)S(1)} %shard_map.130.refs_3_), channel_id=1, source_target_pairs={{0,96},{1,25},{2,98},{3,27},{4,100},{5,29},{6,102},{7,31},{8,104},... | collective-permute-start | bytes 1081352 | tf_op jit(solution)/shard_map/ppermute | solution.py:54
  42.3 13.3 %collective-permute-start.7 = (bf16[256,1408]{1,0:T(8,128)(2,1)S(1)}, bf16[256,1408]{1,0:T(8,128)(2,1)S(1)}, u32[]{:S(2)}, u32[]{:S(2)}) collective-permute-start(bf16[256,1408]{1,0:T(8,128)(2,1)S(1)} %shard_map.128.refs_0_), channel_id=1, source_target_pairs={{0,1},{1,0},{2,3},{3,2},{4,5},{5,4},{6,7},{7,6},{8,9},{9,8},{10,11... | collective-permute-start | bytes 2162696 | tf_op jit(solution)/shard_map/ppermute | solution.py:54
  43.9 7.9 %collective-permute-start.11 = (bf16[128,1408]{1,0:T(8,128)(2,1)S(1)}, bf16[128,1408]{1,0:T(8,128)(2,1)S(1)}, u32[]{:S(2)}, u32[]{:S(2)}) collective-permute-start(bf16[128,1408]{1,0:T(8,128)(2,1)S(1)} %shard_map.129.refs_2_), channel_id=1, source_target_pairs={{0,32},{1,9},{2,34},{3,11},{4,36},{5,13},{6,38},{7,15},{8,40},{9,1... | collective-permute-start | bytes 1081352 | tf_op jit(solution)/shard_map/ppermute | solution.py:54
  44.6 11.0 %collective-permute-start.12 = (bf16[128,1408]{1,0:T(8,128)(2,1)S(1)}, bf16[128,1408]{1,0:T(8,128)(2,1)S(1)}, u32[]{:S(2)}, u32[]{:S(2)}) collective-permute-start(bf16[128,1408]{1,0:T(8,128)(2,1)S(1)} %shard_map.130.refs_3_), channel_id=1, source_target_pairs={{0,32},{1,9},{2,34},{3,11},{4,36},{5,13},{6,38},{7,15},{8,40},{9,1... | collective-permute-start | bytes 1081352 | tf_op jit(solution)/shard_map/ppermute | solution.py:54
  45.8 9.8 %collective-permute-start.13 = (bf16[128,1408]{1,0:T(8,128)(2,1)S(1)}, bf16[128,1408]{1,0:T(8,128)(2,1)S(1)}, u32[]{:S(2)}, u32[]{:S(2)}) collective-permute-start(bf16[128,1408]{1,0:T(8,128)(2,1)S(1)} %shard_map.129.refs_2_), channel_id=1, source_target_pairs={{0,96},{1,25},{2,98},{3,27},{4,100},{5,29},{6,102},{7,31},{8,104},... | collective-permute-start | bytes 1081352 | tf_op jit(solution)/shard_map/ppermute | solution.py:54
  47.2 14.1 %collective-permute-start.16 = (bf16[128,1408]{1,0:T(8,128)(2,1)S(1)}, bf16[128,1408]{1,0:T(8,128)(2,1)S(1)}, u32[]{:S(2)}, u32[]{:S(2)}) collective-permute-start(bf16[128,1408]{1,0:T(8,128)(2,1)S(1)} %collective-permute-done.14.refs_7_), channel_id=1, source_target_pairs={{0,96},{1,25},{2,98},{3,27},{4,100},{5,29},{6,102},{7,31},{8,104},... | collective-permute-start | bytes 1081352 | tf_op jit(solution)/shard_map/ppermute | solution.py:54
  51.7 9.6 %collective-permute-start.15 = (bf16[128,1408]{1,0:T(8,128)(2,1)S(1)}, bf16[128,1408]{1,0:T(8,128)(2,1)S(1)}, u32[]{:S(2)}, u32[]{:S(2)}) collective-permute-start(bf16[128,1408]{1,0:T(8,128)(2,1)S(1)} %collective-permute-done.11.refs_4_), channel_id=1, source_target_pairs={{0,32},{1,9},{2,34},{3,11},{4,36},{5,13},{6,38},{7,15},{8,40},{9,1... | collective-permute-start | bytes 1081352 | tf_op jit(solution)/shard_map/ppermute | solution.py:54
  63.7 5.1 %collective-permute-start.17 = (bf16[256,1536]{1,0:T(8,128)(2,1)S(1)}, bf16[256,1536]{1,0:T(8,128)(2,1)S(1)}, u32[]{:S(2)}, u32[]{:S(2)}) collective-permute-start(bf16[256,1536]{1,0:T(8,128)(2,1)S(1)} %get-tuple-element.57), channel_id=1, source_target_pairs={{0,1},{1,0},{2,3},{3,2},{4,5},{5,4},{6,7},{7,6},{8,9},{9,8},{10,11... | collective-permute-start | bytes 2359304 | tf_op jit(solution)/shard_map/ppermute | solution.py:54
  64.7 7.8 %collective-permute-start.31 = (bf16[128,1408]{1,0:T(8,128)(2,1)S(1)}, bf16[128,1408]{1,0:T(8,128)(2,1)S(1)}, u32[]{:S(2)}, u32[]{:S(2)}) collective-permute-start(bf16[128,1408]{1,0:T(8,128)(2,1)S(1)} %get-tuple-element.73), channel_id=1, source_target_pairs={{0,32},{1,9},{2,34},{3,11},{4,36},{5,13},{6,38},{7,15},{8,40},{9,1... | collective-permute-start | bytes 1081352 | tf_op jit(solution)/shard_map/ppermute | solution.py:54
  65.3 7.3 %collective-permute-start.27 = (bf16[128,1408]{1,0:T(8,128)(2,1)S(1)}, bf16[128,1408]{1,0:T(8,128)(2,1)S(1)}, u32[]{:S(2)}, u32[]{:S(2)}) collective-permute-start(bf16[128,1408]{1,0:T(8,128)(2,1)S(1)} %get-tuple-element.69), channel_id=1, source_target_pairs={{0,96},{1,25},{2,98},{3,27},{4,100},{5,29},{6,102},{7,31},{8,104},... | collective-permute-start | bytes 1081352 | tf_op jit(solution)/shard_map/ppermute | solution.py:54
  67.3 15.1 %collective-permute-start.29 = (bf16[128,1408]{1,0:T(8,128)(2,1)S(1)}, bf16[128,1408]{1,0:T(8,128)(2,1)S(1)}, u32[]{:S(2)}, u32[]{:S(2)}) collective-permute-start(bf16[128,1408]{1,0:T(8,128)(2,1)S(1)} %get-tuple-element.70), channel_id=1, source_target_pairs={{0,96},{1,25},{2,98},{3,27},{4,100},{5,29},{6,102},{7,31},{8,104},... | collective-permute-start | bytes 1081352 | tf_op jit(solution)/shard_map/ppermute | solution.py:54
  68.1 16.4 %collective-permute-start.30 = (bf16[128,1408]{1,0:T(8,128)(2,1)S(1)}, bf16[128,1408]{1,0:T(8,128)(2,1)S(1)}, u32[]{:S(2)}, u32[]{:S(2)}) collective-permute-start(bf16[128,1408]{1,0:T(8,128)(2,1)S(1)} %get-tuple-element.71), channel_id=1, source_target_pairs={{0,32},{1,9},{2,34},{3,11},{4,36},{5,13},{6,38},{7,15},{8,40},{9,1... | collective-permute-start | bytes 1081352 | tf_op jit(solution)/shard_map/ppermute | solution.py:54
  72.5 11.9 %collective-permute-start.32 = (bf16[128,1408]{1,0:T(8,128)(2,1)S(1)}, bf16[128,1408]{1,0:T(8,128)(2,1)S(1)}, u32[]{:S(2)}, u32[]{:S(2)}) collective-permute-start(bf16[128,1408]{1,0:T(8,128)(2,1)S(1)} %shard_map.141), channel_id=1, source_target_pairs={{0,32},{1,9},{2,34},{3,11},{4,36},{5,13},{6,38},{7,15},{8,40},{9,1... | collective-permute-start | bytes 1081352 | tf_op jit(solution)/shard_map/ppermute | solution.py:54
  72.7 11.8 %collective-permute-start.28 = (bf16[128,1408]{1,0:T(8,128)(2,1)S(1)}, bf16[128,1408]{1,0:T(8,128)(2,1)S(1)}, u32[]{:S(2)}, u32[]{:S(2)}) collective-permute-start(bf16[128,1408]{1,0:T(8,128)(2,1)S(1)} %shard_map.140), channel_id=1, source_target_pairs={{0,96},{1,25},{2,98},{3,27},{4,100},{5,29},{6,102},{7,31},{8,104},... | collective-permute-start | bytes 1081352 | tf_op jit(solution)/shard_map/ppermute | solution.py:54
  75.4 6.2 %collective-permute-start.18 = (bf16[64,1536]{1,0:T(8,128)(2,1)S(1)}, bf16[64,1536]{1,0:T(8,128)(2,1)S(1)}, u32[]{:S(2)}, u32[]{:S(2)}) collective-permute-start(bf16[64,1536]{1,0:T(8,128)(2,1)S(1)} %get-tuple-element.59.refs_2_), channel_id=1, source_target_pairs={{0,6},{1,3},{2,0},{3,5},{4,2},{5,7},{6,4},{7,1},{8,14},{9,11},{10,... | collective-permute-start | bytes 589832 | tf_op jit(solution)/shard_map/ppermute | solution.py:54
  81.7 6.2 %collective-permute-start.19 = (bf16[64,1536]{1,0:T(8,128)(2,1)S(1)}, bf16[64,1536]{1,0:T(8,128)(2,1)S(1)}, u32[]{:S(2)}, u32[]{:S(2)}) collective-permute-start(bf16[64,1536]{1,0:T(8,128)(2,1)S(1)} %get-tuple-element.60.refs_5_), channel_id=1, source_target_pairs={{0,6},{1,3},{2,0},{3,5},{4,2},{5,7},{6,4},{7,1},{8,14},{9,11},{10,... | collective-permute-start | bytes 589832 | tf_op jit(solution)/shard_map/ppermute | solution.py:54
  82.4 5.5 %collective-permute-start.20 = (bf16[64,1536]{1,0:T(8,128)(2,1)S(1)}, bf16[64,1536]{1,0:T(8,128)(2,1)S(1)}, u32[]{:S(2)}, u32[]{:S(2)}) collective-permute-start(bf16[64,1536]{1,0:T(8,128)(2,1)S(1)} %get-tuple-element.61), channel_id=1, source_target_pairs={{0,2},{1,7},{2,4},{3,1},{4,6},{5,3},{6,0},{7,5},{8,10},{9,15},{10,... | collective-permute-start | bytes 589832 | tf_op jit(solution)/shard_map/ppermute | solution.py:54
  84.5 22.7 %slice-start.6 = ((s8[4325376]{0:T(1024)(128)(4,1)}), s8[4194304]{0:T(1024)(128)(4,1)S(1)}, s32[]{:S(2)}) async-start(s8[4325376]{0:T(1024)(128)(4,1)} %bitcast.8), calls=%async_computation.6 | async-start | bytes 8388608
  84.7 5.1 %collective-permute-start.33 = (bf16[64,1408]{1,0:T(8,128)(2,1)S(1)}, bf16[64,1408]{1,0:T(8,128)(2,1)S(1)}, u32[]{:S(2)}, u32[]{:S(2)}) collective-permute-start(bf16[64,1408]{1,0:T(8,128)(2,1)S(1)} %get-tuple-element.75), channel_id=1, source_target_pairs={{0,24},{1,97},{2,26},{3,99},{4,28},{5,101},{6,30},{7,103},{8,0},{9... | collective-permute-start | bytes 540680 | tf_op jit(solution)/shard_map/ppermute | solution.py:54
  86.6 7.8 %collective-permute-start.34 = (bf16[64,1408]{1,0:T(8,128)(2,1)S(1)}, bf16[64,1408]{1,0:T(8,128)(2,1)S(1)}, u32[]{:S(2)}, u32[]{:S(2)}) collective-permute-start(bf16[64,1408]{1,0:T(8,128)(2,1)S(1)} %get-tuple-element.76), channel_id=1, source_target_pairs={{0,8},{1,33},{2,10},{3,35},{4,12},{5,37},{6,14},{7,39},{8,16},{9,4... | collective-permute-start | bytes 540680 | tf_op jit(solution)/shard_map/ppermute | solution.py:54
  86.6 7.8 %collective-permute-start.35 = (bf16[64,1408]{1,0:T(8,128)(2,1)S(1)}, bf16[64,1408]{1,0:T(8,128)(2,1)S(1)}, u32[]{:S(2)}, u32[]{:S(2)}) collective-permute-start(bf16[64,1408]{1,0:T(8,128)(2,1)S(1)} %get-tuple-element.77), channel_id=1, source_target_pairs={{0,16},{1,65},{2,18},{3,67},{4,20},{5,69},{6,22},{7,71},{8,24},{9,... | collective-permute-start | bytes 540680 | tf_op jit(solution)/shard_map/ppermute | solution.py:54
  88.4 10.0 %collective-permute-start.21 = (bf16[64,1536]{1,0:T(8,128)(2,1)S(1)}, bf16[64,1536]{1,0:T(8,128)(2,1)S(1)}, u32[]{:S(2)}, u32[]{:S(2)}) collective-permute-start(bf16[64,1536]{1,0:T(8,128)(2,1)S(1)} %shard_map.135.r0.refs_6_), channel_id=1, source_target_pairs={{0,2},{1,3},{2,0},{3,1},{4,6},{5,7},{6,4},{7,5},{8,10},{9,11},{10,... | collective-permute-start | bytes 589832 | tf_op jit(solution)/shard_map/ppermute | solution.py:54
  94.4 12.7 %slice-start.7 = ((s8[4325376]{0:T(1024)(128)(4,1)}), s8[131072]{0:T(1024)(128)(4,1)S(1)}, s32[]{:S(2)}) async-start(s8[4325376]{0:T(1024)(128)(4,1)} %bitcast.8), calls=%async_computation.7 | async-start | bytes 262144
  94.9 7.2 %collective-permute-start.36 = (bf16[64,1408]{1,0:T(8,128)(2,1)S(1)}, bf16[64,1408]{1,0:T(8,128)(2,1)S(1)}, u32[]{:S(2)}, u32[]{:S(2)}) collective-permute-start(bf16[64,1408]{1,0:T(8,128)(2,1)S(1)} %shard_map.143.refs_0_.r0), channel_id=1, source_target_pairs={{0,2},{1,3},{2,0},{3,1},{4,6},{5,7},{6,4},{7,5},{8,10},{9,11},{10,... | collective-permute-start | bytes 540680 | tf_op jit(solution)/shard_map/ppermute | solution.py:54
  95.0 9.0 %collective-permute-start.22 = (bf16[64,1536]{1,0:T(8,128)(2,1)S(1)}, bf16[64,1536]{1,0:T(8,128)(2,1)S(1)}, u32[]{:S(2)}, u32[]{:S(2)}) collective-permute-start(bf16[64,1536]{1,0:T(8,128)(2,1)S(1)} %shard_map.135.r0.refs_6_), channel_id=1, source_target_pairs={{0,1},{1,0},{2,3},{3,2},{4,5},{5,4},{6,7},{7,6},{8,9},{9,8},{10,11... | collective-permute-start | bytes 589832 | tf_op jit(solution)/shard_map/ppermute | solution.py:54
  98.4 5.7 %collective-permute-start.23 = (bf16[64,1536]{1,0:T(8,128)(2,1)S(1)}, bf16[64,1536]{1,0:T(8,128)(2,1)S(1)}, u32[]{:S(2)}, u32[]{:S(2)}) collective-permute-start(bf16[64,1536]{1,0:T(8,128)(2,1)S(1)} %collective-permute-done.21.r1), channel_id=1, source_target_pairs={{0,1},{1,0},{2,3},{3,2},{4,5},{5,4},{6,7},{7,6},{8,9},{9,8},{10,11... | collective-permute-start | bytes 589832 | tf_op jit(solution)/shard_map/ppermute | solution.py:54
  102.1 5.0 %collective-permute-start.37 = (bf16[64,1408]{1,0:T(8,128)(2,1)S(1)}, bf16[64,1408]{1,0:T(8,128)(2,1)S(1)}, u32[]{:S(2)}, u32[]{:S(2)}) collective-permute-start(bf16[64,1408]{1,0:T(8,128)(2,1)S(1)} %shard_map.143.refs_0_.r0), channel_id=1, source_target_pairs={{0,1},{1,0},{2,3},{3,2},{4,5},{5,4},{6,7},{7,6},{8,9},{9,8},{10,11... | collective-permute-start | bytes 540680 | tf_op jit(solution)/shard_map/ppermute | solution.py:54
  102.1 5.0 %collective-permute-start.38 = (bf16[64,1408]{1,0:T(8,128)(2,1)S(1)}, bf16[64,1408]{1,0:T(8,128)(2,1)S(1)}, u32[]{:S(2)}, u32[]{:S(2)}) collective-permute-start(bf16[64,1408]{1,0:T(8,128)(2,1)S(1)} %collective-permute-done.36.refs_1_.r1), channel_id=1, source_target_pairs={{0,1},{1,0},{2,3},{3,2},{4,5},{5,4},{6,7},{7,6},{8,9},{9,8},{10,11... | collective-permute-start | bytes 540680 | tf_op jit(solution)/shard_map/ppermute | solution.py:54
  107.0 3.6 %collective-permute-start.24 = (bf16[128,1408]{1,0:T(8,128)(2,1)S(1)}, bf16[128,1408]{1,0:T(8,128)(2,1)S(1)}, u32[]{:S(2)}, u32[]{:S(2)}) collective-permute-start(bf16[128,1408]{1,0:T(8,128)(2,1)S(1)} %get-tuple-element.65.refs_7_), channel_id=1, source_target_pairs={{0,1},{1,0},{2,3},{3,2},{4,5},{5,4},{6,7},{7,6},{8,9},{9,8},{10,11... | collective-permute-start | bytes 1081352 | tf_op jit(solution)/shard_map/ppermute | solution.py:54
  110.0 1.9 %collective-permute-start.39 = (bf16[128,1408]{1,0:T(8,128)(2,1)S(1)}, bf16[128,1408]{1,0:T(8,128)(2,1)S(1)}, u32[]{:S(2)}, u32[]{:S(2)}) collective-permute-start(bf16[128,1408]{1,0:T(8,128)(2,1)S(1)} %get-tuple-element.81), channel_id=1, source_target_pairs={{0,1},{1,0},{2,3},{3,2},{4,5},{5,4},{6,7},{7,6},{8,9},{9,8},{10,11... | collective-permute-start | bytes 1081352 | tf_op jit(solution)/shard_map/ppermute | solution.py:54
  110.6 10.1 %collective-permute-start.25 = (bf16[128,1408]{1,0:T(8,128)(2,1)S(1)}, bf16[128,1408]{1,0:T(8,128)(2,1)S(1)}, u32[]{:S(2)}, u32[]{:S(2)}) collective-permute-start(bf16[128,1408]{1,0:T(8,128)(2,1)S(1)} %shard_map.137.own_ref), channel_id=1, source_target_pairs={{0,2},{1,3},{2,0},{3,1},{4,6},{5,7},{6,4},{7,5},{8,10},{9,11},{10,... | collective-permute-start | bytes 1081352 | tf_op jit(solution)/shard_map/ppermute | solution.py:54
  111.9 16.5 %collective-permute-start.40 = (bf16[128,1408]{1,0:T(8,128)(2,1)S(1)}, bf16[128,1408]{1,0:T(8,128)(2,1)S(1)}, u32[]{:S(2)}, u32[]{:S(2)}) collective-permute-start(bf16[128,1408]{1,0:T(8,128)(2,1)S(1)} %shard_map.145.own_ref), channel_id=1, source_target_pairs={{0,2},{1,3},{2,0},{3,1},{4,6},{5,7},{6,4},{7,5},{8,10},{9,11},{10,... | collective-permute-start | bytes 1081352 | tf_op jit(solution)/shard_map/ppermute | solution.py:54
  120.8 10.8 %copy-start.7 = (f32[1408]{0:T(1024)S(1)}, f32[1408]{0:T(1024)}, u32[]{:S(2)}) copy-start(f32[1408]{0:T(1024)} %gain_ref.9) | copy-start | bytes 16900
  120.8 8.6 %collective-permute-start.26 = (bf16[128,1408]{1,0:T(8,128)(2,1)S(1)}, bf16[128,1408]{1,0:T(8,128)(2,1)S(1)}, u32[]{:S(2)}, u32[]{:S(2)}) collective-permute-start(bf16[128,1408]{1,0:T(8,128)(2,1)S(1)} %shard_map.138.own_ref), channel_id=1, source_target_pairs={{0,1},{1,0},{2,3},{3,2},{4,5},{5,4},{6,7},{7,6},{8,9},{9,8},{10,11... | collective-permute-start | bytes 1081352 | tf_op jit(solution)/shard_map/ppermute | solution.py:54
  128.5 3.0 %collective-permute-start.41 = (bf16[128,1408]{1,0:T(8,128)(2,1)S(1)}, bf16[128,1408]{1,0:T(8,128)(2,1)S(1)}, u32[]{:S(2)}, u32[]{:S(2)}) collective-permute-start(bf16[128,1408]{1,0:T(8,128)(2,1)S(1)} %shard_map.146.own_ref), channel_id=1, source_target_pairs={{0,1},{1,0},{2,3},{3,2},{4,5},{5,4},{6,7},{7,6},{8,9},{9,8},{10,11... | collective-permute-start | bytes 1081352 | tf_op jit(solution)/shard_map/ppermute | solution.py:54
  (11 other events, 51.9 us)

commit v2 on v1

--- a/solution.py
+++ b/solution.py
@@ -200,7 +200,7 @@
             pltpu.VMEM((HIDDEN, WIDTH), bf16),
             pltpu.SemaphoreType.DMA((len(UP_CUTS) + len(DOWN_CUTS),)),
         ],
-        compiler_params=pltpu.CompilerParams(vmem_limit_bytes=58 << 20),
+        compiler_params=pltpu.CompilerParams(vmem_limit_bytes=46 << 20),
         cost_estimate=pl.CostEstimate(
             flops=1, bytes_accessed=1, transcendentals=0
         ),
@@ -320,27 +320,19 @@
 
 
 def early_body(*refs):
-    image_refs, refs = refs[:2], refs[2:]
-    near0, near1, left0, left1, right0, right1 = refs[:6]
-    image_ref, total_ref, loss_ref, near_ref, left_keep, left_send, right_send, right_keep = refs[6:14]
-    texts = refs[14]
+    image_refs, text_refs = refs[:2], refs[2:8]
+    image_ref, total_ref, loss_ref, near_ref, left_keep, left_send, right_send, right_keep = refs[8:16]
+    texts = refs[16]
     for place, ref in enumerate(image_refs):
         image_ref[place * 256 : (place + 1) * 256, :] = ref[...]
-    losses = 0.0
-    for chunk, parts in enumerate(((near0, near1), (left0, left1), (right0, right1))):
-        texts[0:128, :] = parts[0][...]
-        texts[128:256, :] = parts[1][...]
-        loss, to_image, to_text = pair_chunk(image_ref[...], texts[...], chunk == 0)
-        losses = losses + loss
-        if chunk == 0:
-            total_ref[...] = to_image
-            near_ref[...] = to_text
-        else:
-            total_ref[...] += to_image
-            halves = (left_keep, left_send) if chunk == 1 else (right_send, right_keep)
-            halves[0][...] = to_text[0:128, :].astype(halves[0].dtype)
-            halves[1][...] = to_text[128:256, :].astype(halves[1].dtype)
-    loss_ref[...] = jnp.broadcast_to(losses, (512, 128))
+    for place, ref in enumerate(text_refs):
+        texts[place * 128 : (place + 1) * 128, :] = ref[...]
+    loss, to_image, to_text = pair_chunk(image_ref[...], texts[...], True)
+    total_ref[...] = to_image
+    near_ref[...] = to_text[0:256, :]
+    for place, ref in enumerate((left_keep, left_send, right_send, right_keep)):
+        ref[...] = to_text[256 + place * 128 : 384 + place * 128, :].astype(ref.dtype)
+    loss_ref[...] = jnp.broadcast_to(loss, (512, 128))
 
 
 def late_body(image_ref, total_ref, loss_ref, far0, far1, far0_ref, far1_ref, keep_ref, send_ref, texts):
@@ -362,7 +354,7 @@
         [shape(512, WIDTH, bf16), shape(512, WIDTH, f32), shape(512, 128, f32)]
         + [shape(256, WIDTH, f32), half32, half16, half16, half32],
         [*images, *near, *left, *right],
-        scratch_shapes=[pltpu.VMEM((256, WIDTH), bf16)],
+        scratch_shapes=[pltpu.VMEM((768, WIDTH), bf16)],
     )
     far0, far1, image_keep, image_send = call(
         late_body,

time: 134 us -> 133 us (level)
  Pallas kernels: 31.3 us -> 27.6 us
    pallas_call x1, Pallas kernels: 7.35 us -> 4.44 us  [tower_streamed(): pl.pallas_call(streamed_body, in_specs=[pl.BlockSpec(memory_space=pltpu.S...]
    unnamed x34 -> x36, local copies, waits for them, and re-layouts: 3.4 us -> 4.43 us
  transfers between devices with their start and end apart: 42 -> 42, of which waited for: 12 -> 13; matrix products, arithmetic and copies ran while one was open for 0% -> 0% of each run, Pallas kernels for 14% -> 13%
where the time goes in v2:
time: 133 us
  starting transfers between devices  55.9 us (42%)
  waiting for transfers between devices  43.8 us (33%)
  Pallas kernels  27.6 us (21%)
  local copies, waits for them, and re-layouts  4.43 us (3%)
    ppermute x42, starting transfers between devices, send(): return lax.ppermute(value, AXES, pairs)  55.9 us
    ppermute x42, waiting for transfers between devices, send(): return lax.ppermute(value, AXES, pairs)  43.8 us
    pallas_call x26, Pallas kernels, call(): pl.pallas_call(body, out_shape=outs, in_specs=specs, out_specs=[pl.BlockS...  23.1 us
    pallas_call x1, Pallas kernels, tower_streamed(): pl.pallas_call(streamed_body, in_specs=[pl.BlockSpec(memory_space=pltpu.S...  4.44 us
    unnamed x36, local copies, waits for them, and re-layouts  4.43 us
  transfers between devices with their start and end apart: 42, of which 13 were waited for; matrix products, arithmetic and copies ran while one was open for 0% of the time, Pallas kernels for 13%

profile of v2, /device:TPU:1, one launch (start us, length us, event | category | flops | bytes accessed | tf_op | source)
XLA Modules:
  0.0 132.8 jit_solution(9166399491506981787)
XLA Ops:
  0.7 2.4 %copy-done.1 = bf16[1408,1536]{1,0:T(8,128)(2,1)S(1)} copy-done((bf16[1408,1536]{1,0:T(8,128)(2,1)S(1)}, bf16[1408,1536]{1,0:T(8,128)(2,1)}, u32[]{:S(2)}) %copy-start.1) | copy-done | bytes 4325400
  3.0 1.3 copy-done.3
  5.0 4.4 %shard_map.121 = (f32[256,1536]{1,0:T(8,128)S(1)}, f32[128,1408]{1,0:T(8,128)S(1)}, bf16[128,1408]{1,0:T(8,128)(2,1)S(1)}) custom-call(s32[1]{0:T(128)} %bitcast.mine.refs_0_, bf16[256,1408]{1,0:T(8,128)(2,1)S(1)} %copy-done.3, f32[1408]{0:T(1024)S(1)} %copy-done.9, bf16[1408,1536]{1,0:T(8,128)(2,1)S(1)} %copy-done.1, bf16[1536,1408]{1,0:T(8,128)(2,1)} %refs_6_.1), custom_call_target="tpu_custom_call" | custom-call | flops 1 | bytes 1 | tf_op jit(solution)/shard_map/pallas_call | solution.py:192
  9.5 1.5 %collective-permute-start = (bf16[128,1408]{1,0:T(8,128)(2,1)S(1)}, bf16[128,1408]{1,0:T(8,128)(2,1)S(1)}, u32[]{:S(2)}, u32[]{:S(2)}) collective-permute-start(bf16[128,1408]{1,0:T(8,128)(2,1)S(1)} %get-tuple-element.44), channel_id=1, source_target_pairs={{0,1},{1,0},{2,3},{3,2},{4,5},{5,4},{6,7},{7,6},{8,9},{9,8},{10,11... | collective-permute-start | bytes 1081352 | tf_op jit(solution)/shard_map/ppermute | solution.py:54
  11.0 1.3 collective-permute-done.got_ref
  12.4 1.8 %collective-permute-start.1 = (bf16[64,1408]{1,0:T(8,128)(2,1)S(1)}, bf16[64,1408]{1,0:T(8,128)(2,1)S(1)}, u32[]{:S(2)}, u32[]{:S(2)}) collective-permute-start(bf16[64,1408]{1,0:T(8,128)(2,1)S(1)} %get-tuple-element.45.refs_5_), channel_id=1, source_target_pairs={{0,2},{1,3},{2,0},{3,1},{4,6},{5,7},{6,4},{7,5},{8,10},{9,11},{10,... | collective-permute-start | bytes 540680 | tf_op jit(solution)/shard_map/ppermute | solution.py:54
  14.2 3.1 %shard_map.123 = (f32[256,1536]{1,0:T(8,128)S(1)}, f32[128,1408]{1,0:T(8,128)S(1)}, f32[128,1408]{1,0:T(8,128)S(1)}) custom-call(s32[1]{0:T(128)} %bitcast.mine.refs_0_, bf16[256,1408]{1,0:T(8,128)(2,1)S(1)} %copy-done.2, f32[1408]{0:T(1024)S(1)} %copy-done.8, bf16[1408,1536]{1,0:T(8,128)(2,1)S(1)} %bitcast.3, bf16[1536,1408]{1,0:T(8,128)(2,1)S(1)} %copy-done, ...), custom_call_target="tpu_custom_call" | custom-call | flops 2214592512 | bytes 1 | tf_op jit(solution)/shard_map/pallas_call | solution.py:75
  17.3 1.5 %collective-permute-done.1.refs_2_ = bf16[64,1408]{1,0:T(8,128)(2,1)S(1)} collective-permute-done((bf16[64,1408]{1,0:T(8,128)(2,1)S(1)}, bf16[64,1408]{1,0:T(8,128)(2,1)S(1)}, u32[]{:S(2)}, u32[]{:S(2)}) %collective-permute-start.1) | collective-permute-done | bytes 180256 | tf_op jit(solution)/shard_map/ppermute | solution.py:54
  19.2 1.0 collective-permute-start.2
  20.2 1.3 collective-permute-done.2.got_ref
  21.6 1.5 %collective-permute-start.3 = (bf16[64,1408]{1,0:T(8,128)(2,1)S(1)}, bf16[64,1408]{1,0:T(8,128)(2,1)S(1)}, u32[]{:S(2)}, u32[]{:S(2)}) collective-permute-start(bf16[64,1408]{1,0:T(8,128)(2,1)S(1)} %get-tuple-element.51.refs_2_), channel_id=1, source_target_pairs={{0,2},{1,3},{2,0},{3,1},{4,6},{5,7},{6,4},{7,5},{8,10},{9,11},{10,... | collective-permute-start | bytes 540680 | tf_op jit(solution)/shard_map/ppermute | solution.py:54
  23.1 4.3 %collective-permute-done.3.got_ref = bf16[64,1408]{1,0:T(8,128)(2,1)S(1)} collective-permute-done((bf16[64,1408]{1,0:T(8,128)(2,1)S(1)}, bf16[64,1408]{1,0:T(8,128)(2,1)S(1)}, u32[]{:S(2)}, u32[]{:S(2)}) %collective-permute-start.3) | collective-permute-done | bytes 180256 | tf_op jit(solution)/shard_map/ppermute | solution.py:54
  27.8 3.6 %collective-permute-start.4 = (bf16[64,1408]{1,0:T(8,128)(2,1)S(1)}, bf16[64,1408]{1,0:T(8,128)(2,1)S(1)}, u32[]{:S(2)}, u32[]{:S(2)}) collective-permute-start(bf16[64,1408]{1,0:T(8,128)(2,1)S(1)} %get-tuple-element.52.refs_0_), channel_id=1, source_target_pairs={{0,2},{1,7},{2,4},{3,1},{4,6},{5,3},{6,0},{7,5},{8,10},{9,15},{10,... | collective-permute-start | bytes 540680 | tf_op jit(solution)/shard_map/ppermute | solution.py:54
  31.4 2.9 %collective-permute-start.10 = (bf16[64,1408]{1,0:T(8,128)(2,1)S(1)}, bf16[64,1408]{1,0:T(8,128)(2,1)S(1)}, u32[]{:S(2)}, u32[]{:S(2)}) collective-permute-start(bf16[64,1408]{1,0:T(8,128)(2,1)S(1)} %get-tuple-element.49.refs_1_.refs_0_), channel_id=1, source_target_pairs={{0,16},{1,65},{2,18},{3,67},{4,20},{5,69},{6,22},{7,71},{8,24},{9,... | collective-permute-start | bytes 540680 | tf_op jit(solution)/shard_map/ppermute | solution.py:54
  35.1 2.7 %collective-permute-start.6 = (bf16[64,1408]{1,0:T(8,128)(2,1)S(1)}, bf16[64,1408]{1,0:T(8,128)(2,1)S(1)}, u32[]{:S(2)}, u32[]{:S(2)}) collective-permute-start(bf16[64,1408]{1,0:T(8,128)(2,1)S(1)} %collective-permute-done.4.refs_1_), channel_id=1, source_target_pairs={{0,2},{1,7},{2,4},{3,1},{4,6},{5,3},{6,0},{7,5},{8,10},{9,15},{10,... | collective-permute-start | bytes 540680 | tf_op jit(solution)/shard_map/ppermute | solution.py:54
  38.5 1.4 %collective-permute-done.9.refs_0_ = bf16[64,1408]{1,0:T(8,128)(2,1)S(1)} collective-permute-done((bf16[64,1408]{1,0:T(8,128)(2,1)S(1)}, bf16[64,1408]{1,0:T(8,128)(2,1)S(1)}, u32[]{:S(2)}, u32[]{:S(2)}) %collective-permute-start.9) | collective-permute-done | bytes 180256 | tf_op jit(solution)/shard_map/ppermute | solution.py:54
  39.9 2.6 %collective-permute-start.14 = (bf16[128,1408]{1,0:T(8,128)(2,1)S(1)}, bf16[128,1408]{1,0:T(8,128)(2,1)S(1)}, u32[]{:S(2)}, u32[]{:S(2)}) collective-permute-start(bf16[128,1408]{1,0:T(8,128)(2,1)S(1)} %shard_map.130.refs_3_), channel_id=1, source_target_pairs={{0,96},{1,25},{2,98},{3,27},{4,100},{5,29},{6,102},{7,31},{8,104},... | collective-permute-start | bytes 1081352 | tf_op jit(solution)/shard_map/ppermute | solution.py:54
  42.5 1.5 %collective-permute-start.7 = (bf16[256,1408]{1,0:T(8,128)(2,1)S(1)}, bf16[256,1408]{1,0:T(8,128)(2,1)S(1)}, u32[]{:S(2)}, u32[]{:S(2)}) collective-permute-start(bf16[256,1408]{1,0:T(8,128)(2,1)S(1)} %shard_map.128.refs_0_), channel_id=1, source_target_pairs={{0,1},{1,0},{2,3},{3,2},{4,5},{5,4},{6,7},{7,6},{8,9},{9,8},{10,11... | collective-permute-start | bytes 2162696 | tf_op jit(solution)/shard_map/ppermute | solution.py:54
  44.7 1.2 collective-permute-start.12
  45.9 1.5 %collective-permute-start.13 = (bf16[128,1408]{1,0:T(8,128)(2,1)S(1)}, bf16[128,1408]{1,0:T(8,128)(2,1)S(1)}, u32[]{:S(2)}, u32[]{:S(2)}) collective-permute-start(bf16[128,1408]{1,0:T(8,128)(2,1)S(1)} %shard_map.129.refs_2_), channel_id=1, source_target_pairs={{0,96},{1,25},{2,98},{3,27},{4,100},{5,29},{6,102},{7,31},{8,104},... | collective-permute-start | bytes 1081352 | tf_op jit(solution)/shard_map/ppermute | solution.py:54
  47.4 2.5 %collective-permute-start.16 = (bf16[128,1408]{1,0:T(8,128)(2,1)S(1)}, bf16[128,1408]{1,0:T(8,128)(2,1)S(1)}, u32[]{:S(2)}, u32[]{:S(2)}) collective-permute-start(bf16[128,1408]{1,0:T(8,128)(2,1)S(1)} %collective-permute-done.14.refs_7_), channel_id=1, source_target_pairs={{0,96},{1,25},{2,98},{3,27},{4,100},{5,29},{6,102},{7,31},{8,104},... | collective-permute-start | bytes 1081352 | tf_op jit(solution)/shard_map/ppermute | solution.py:54
  49.9 2.0 %collective-permute-done.11.refs_4_ = bf16[128,1408]{1,0:T(8,128)(2,1)S(1)} collective-permute-done((bf16[128,1408]{1,0:T(8,128)(2,1)S(1)}, bf16[128,1408]{1,0:T(8,128)(2,1)S(1)}, u32[]{:S(2)}, u32[]{:S(2)}) %collective-permute-start.11) | collective-permute-done | bytes 360480 | tf_op jit(solution)/shard_map/ppermute | solution.py:54
  51.9 3.9 %collective-permute-done.12.refs_5_ = bf16[128,1408]{1,0:T(8,128)(2,1)S(1)} collective-permute-done((bf16[128,1408]{1,0:T(8,128)(2,1)S(1)}, bf16[128,1408]{1,0:T(8,128)(2,1)S(1)}, u32[]{:S(2)}, u32[]{:S(2)}) %collective-permute-start.12) | collective-permute-done | bytes 360480 | tf_op jit(solution)/shard_map/ppermute | solution.py:54
  55.7 4.7 %shard_map.131 = (bf16[512,1408]{1,0:T(8,128)(2,1)S(1)}, f32[512,1408]{1,0:T(8,128)S(1)}, f32[512,128]{1,0:T(8,128)S(1)}, f32[256,1408]{1,0:T(8,128)S(1)}, f32[1...) custom-call(bf16[256,1408]{1,0:T(8,128)(2,1)S(1)} %shard_map.128.ref, ...), custom_call_target="tpu_custom_call" | custom-call | flops 1 | bytes 1 | tf_op jit(solution)/shard_map/pallas_call | solution.py:75
  60.4 2.3 %shard_map.132 = (bf16[128,1408]{1,0:T(8,128)(2,1)S(1)}, bf16[128,1408]{1,0:T(8,128)(2,1)S(1)}, f32[256,1536]{1,0:T(8,128)S(1)}, bf16[256,1536]{1,0:T(8,128)(2,1)S(1)}) custom-call(bf16[512,1408]{1,0:T(8,128)(2,1)S(1)} %get-tuple-element.53.image_ref, f32[512,1408]{1,0:T(8,128)S(1)} %get-tuple-element.54.total_ref, ...), custom_call_target="tpu_custom_call" | custom-call | flops 1 | bytes 1 | tf_op jit(solution)/shard_map/pallas_call | solution.py:75
  62.8 1.0 collective-permute-start.17
  64.5 2.0 %collective-permute-start.27 = (bf16[128,1408]{1,0:T(8,128)(2,1)S(1)}, bf16[128,1408]{1,0:T(8,128)(2,1)S(1)}, u32[]{:S(2)}, u32[]{:S(2)}) collective-permute-start(bf16[128,1408]{1,0:T(8,128)(2,1)S(1)} %get-tuple-element.69), channel_id=1, source_target_pairs={{0,96},{1,25},{2,98},{3,27},{4,100},{5,29},{6,102},{7,31},{8,104},... | collective-permute-start | bytes 1081352 | tf_op jit(solution)/shard_map/ppermute | solution.py:54
  68.2 3.4 %collective-permute-done.31.refs_1_ = bf16[128,1408]{1,0:T(8,128)(2,1)S(1)} collective-permute-done((bf16[128,1408]{1,0:T(8,128)(2,1)S(1)}, bf16[128,1408]{1,0:T(8,128)(2,1)S(1)}, u32[]{:S(2)}, u32[]{:S(2)}) %collective-permute-start.31) | collective-permute-done | bytes 360480 | tf_op jit(solution)/shard_map/ppermute | solution.py:54
  71.9 2.7 %collective-permute-start.28 = (bf16[128,1408]{1,0:T(8,128)(2,1)S(1)}, bf16[128,1408]{1,0:T(8,128)(2,1)S(1)}, u32[]{:S(2)}, u32[]{:S(2)}) collective-permute-start(bf16[128,1408]{1,0:T(8,128)(2,1)S(1)} %shard_map.140), channel_id=1, source_target_pairs={{0,96},{1,25},{2,98},{3,27},{4,100},{5,29},{6,102},{7,31},{8,104},... | collective-permute-start | bytes 1081352 | tf_op jit(solution)/shard_map/ppermute | solution.py:54
  74.6 1.7 %collective-permute-start.18 = (bf16[64,1536]{1,0:T(8,128)(2,1)S(1)}, bf16[64,1536]{1,0:T(8,128)(2,1)S(1)}, u32[]{:S(2)}, u32[]{:S(2)}) collective-permute-start(bf16[64,1536]{1,0:T(8,128)(2,1)S(1)} %get-tuple-element.59.refs_2_), channel_id=1, source_target_pairs={{0,6},{1,3},{2,0},{3,5},{4,2},{5,7},{6,4},{7,1},{8,14},{9,11},{10,... | collective-permute-start | bytes 589832 | tf_op jit(solution)/shard_map/ppermute | solution.py:54
  76.3 4.4 %collective-permute-done.18.got_ref = bf16[64,1536]{1,0:T(8,128)(2,1)S(1)} collective-permute-done((bf16[64,1536]{1,0:T(8,128)(2,1)S(1)}, bf16[64,1536]{1,0:T(8,128)(2,1)S(1)}, u32[]{:S(2)}, u32[]{:S(2)}) %collective-permute-start.18) | collective-permute-done | bytes 196640 | tf_op jit(solution)/shard_map/ppermute | solution.py:54
  81.3 2.3 %collective-permute-start.20 = (bf16[64,1536]{1,0:T(8,128)(2,1)S(1)}, bf16[64,1536]{1,0:T(8,128)(2,1)S(1)}, u32[]{:S(2)}, u32[]{:S(2)}) collective-permute-start(bf16[64,1536]{1,0:T(8,128)(2,1)S(1)} %get-tuple-element.61), channel_id=1, source_target_pairs={{0,2},{1,7},{2,4},{3,1},{4,6},{5,3},{6,0},{7,5},{8,10},{9,15},{10,... | collective-permute-start | bytes 589832 | tf_op jit(solution)/shard_map/ppermute | solution.py:54
  83.9 1.8 %collective-permute-start.33 = (bf16[64,1408]{1,0:T(8,128)(2,1)S(1)}, bf16[64,1408]{1,0:T(8,128)(2,1)S(1)}, u32[]{:S(2)}, u32[]{:S(2)}) collective-permute-start(bf16[64,1408]{1,0:T(8,128)(2,1)S(1)} %get-tuple-element.75), channel_id=1, source_target_pairs={{0,24},{1,97},{2,26},{3,99},{4,28},{5,101},{6,30},{7,103},{8,0},{9... | collective-permute-start | bytes 540680 | tf_op jit(solution)/shard_map/ppermute | solution.py:54
  85.7 1.3 collective-permute-start.35
  87.5 1.5 %collective-permute-start.21 = (bf16[64,1536]{1,0:T(8,128)(2,1)S(1)}, bf16[64,1536]{1,0:T(8,128)(2,1)S(1)}, u32[]{:S(2)}, u32[]{:S(2)}) collective-permute-start(bf16[64,1536]{1,0:T(8,128)(2,1)S(1)} %shard_map.135.r0.refs_6_), channel_id=1, source_target_pairs={{0,2},{1,3},{2,0},{3,1},{4,6},{5,7},{6,4},{7,5},{8,10},{9,11},{10,... | collective-permute-start | bytes 589832 | tf_op jit(solution)/shard_map/ppermute | solution.py:54
  88.9 4.5 %collective-permute-done.34.refs_2_ = bf16[64,1408]{1,0:T(8,128)(2,1)S(1)} collective-permute-done((bf16[64,1408]{1,0:T(8,128)(2,1)S(1)}, bf16[64,1408]{1,0:T(8,128)(2,1)S(1)}, u32[]{:S(2)}, u32[]{:S(2)}) %collective-permute-start.34) | collective-permute-done | bytes 180256 | tf_op jit(solution)/shard_map/ppermute | solution.py:54
  94.1 3.1 %collective-permute-start.22 = (bf16[64,1536]{1,0:T(8,128)(2,1)S(1)}, bf16[64,1536]{1,0:T(8,128)(2,1)S(1)}, u32[]{:S(2)}, u32[]{:S(2)}) collective-permute-start(bf16[64,1536]{1,0:T(8,128)(2,1)S(1)} %shard_map.135.r0.refs_6_), channel_id=1, source_target_pairs={{0,1},{1,0},{2,3},{3,2},{4,5},{5,4},{6,7},{7,6},{8,9},{9,8},{10,11... | collective-permute-start | bytes 589832 | tf_op jit(solution)/shard_map/ppermute | solution.py:54
  97.2 4.0 %collective-permute-start.23 = (bf16[64,1536]{1,0:T(8,128)(2,1)S(1)}, bf16[64,1536]{1,0:T(8,128)(2,1)S(1)}, u32[]{:S(2)}, u32[]{:S(2)}) collective-permute-start(bf16[64,1536]{1,0:T(8,128)(2,1)S(1)} %collective-permute-done.21.r1), channel_id=1, source_target_pairs={{0,1},{1,0},{2,3},{3,2},{4,5},{5,4},{6,7},{7,6},{8,9},{9,8},{10,11... | collective-permute-start | bytes 589832 | tf_op jit(solution)/shard_map/ppermute | solution.py:54
  101.2 1.9 %collective-permute-start.38 = (bf16[64,1408]{1,0:T(8,128)(2,1)S(1)}, bf16[64,1408]{1,0:T(8,128)(2,1)S(1)}, u32[]{:S(2)}, u32[]{:S(2)}) collective-permute-start(bf16[64,1408]{1,0:T(8,128)(2,1)S(1)} %collective-permute-done.36.refs_1_.r1), channel_id=1, source_target_pairs={{0,1},{1,0},{2,3},{3,2},{4,5},{5,4},{6,7},{7,6},{8,9},{9,8},{10,11... | collective-permute-start | bytes 540680 | tf_op jit(solution)/shard_map/ppermute | solution.py:54
  103.2 2.9 %shard_map.136 = (f32[128,1408]{1,0:T(8,128)S(1)}, bf16[128,1408]{1,0:T(8,128)(2,1)S(1)}) custom-call(bf16[64,1536]{1,0:T(8,128)(2,1)S(1)} %shard_map.135.r0.refs_6_, bf16[64,1536]{1,0:T(8,128)(2,1)S(1)} %collective-permute-done.21.r1, bf16[64,1536]{1,0:T(8,128)(2,1)S(1)} %collective-permute-done.22.r2, bf16[64,1536]{1,0:T(8,128)(2,1)S(1)} %collective-permute-done.23.r3, ...), custom_call_target="tpu_custom_call" | custom-call | flops 1 | bytes 1 | tf_op jit(solution)/shard_map/pallas_call | solution.py:75
  106.2 2.9 %shard_map.144 = (f32[128,1408]{1,0:T(8,128)S(1)}, bf16[128,1408]{1,0:T(8,128)(2,1)S(1)}) custom-call(bf16[64,1408]{1,0:T(8,128)(2,1)S(1)} %shard_map.143.refs_0_.r0, bf16[64,1408]{1,0:T(8,128)(2,1)S(1)} %collective-permute-done.36.refs_1_.r1, bf16[64,1408]{1,0:T(8,128)(2,1)S(1)} %collective-permute-done.37.refs_2_.r2, ...), custom_call_target="tpu_custom_call" | custom-call | flops 1 | bytes 1 | tf_op jit(solution)/shard_map/pallas_call | solution.py:75
  109.9 1.1 collective-permute-done.39.got_ref
  111.5 8.4 %collective-permute-done.25.got_ref = bf16[128,1408]{1,0:T(8,128)(2,1)S(1)} collective-permute-done((bf16[128,1408]{1,0:T(8,128)(2,1)S(1)}, bf16[128,1408]{1,0:T(8,128)(2,1)S(1)}, u32[]{:S(2)}, u32[]{:S(2)}) %collective-permute-start.25) | collective-permute-done | bytes 360480 | tf_op jit(solution)/shard_map/ppermute | solution.py:54
  120.0 1.3 collective-permute-start.26
  121.3 6.3 %collective-permute-done.40.got_ref = bf16[128,1408]{1,0:T(8,128)(2,1)S(1)} collective-permute-done((bf16[128,1408]{1,0:T(8,128)(2,1)S(1)}, bf16[128,1408]{1,0:T(8,128)(2,1)S(1)}, u32[]{:S(2)}, u32[]{:S(2)}) %collective-permute-start.40) | collective-permute-done | bytes 360480 | tf_op jit(solution)/shard_map/ppermute | solution.py:54
  127.7 0.9 collective-permute-start.41
  128.6 2.1 %shard_map.139 = (f32[256,1408]{1,0:T(8,128)}, f32[1,256]{1,0:T(1,128)}) custom-call(s32[1]{0:T(128)} %bitcast.mine.refs_0_, bf16[256,1408]{1,0:T(8,128)(2,1)S(1)} %copy-done.2, f32[1408]{0:T(1024)S(1)} %copy-done.8, bf16[64,1536]{1,0:T(8,128)(2,1)S(1)} %shard_map.135.r0.refs_6_, bf16[64,1536]{1,0:T(8,128)(2,1)S(1)} %collective-permute-done.21.r1, ...), custom_call_target="tpu_custom_call" | custom-call | flops 1 | bytes 1 | tf_op jit(solution)/shard_map/pallas_call | solution.py:75
  130.7 2.1 %shard_map.147 = f32[256,1408]{1,0:T(8,128)} custom-call(s32[1]{0:T(128)} %bitcast.mine.refs_0_, bf16[256,1408]{1,0:T(8,128)(2,1)S(1)} %copy-done.4, f32[1408]{0:T(1024)S(1)} %copy-done.10, bf16[64,1408]{1,0:T(8,128)(2,1)S(1)} %shard_map.143.refs_0_.r0, bf16[64,1408]{1,0:T(8,128)(2,1)S(1)} %collective-permute-done.36.refs_1_.r1, ...), custom_call_target="tpu_custom_call" | custom-call | flops 1 | bytes 1 | tf_op jit(solution)/shard_map/pallas_call | solution.py:75
  (101 shorter events, 9.9 us)
Async XLA Ops:
  0.7 13.5 %slice-start = ((s8[4325376]{0:T(1024)(128)(4,1)}), s8[4194304]{0:T(1024)(128)(4,1)S(1)}, s32[]{:S(2)}) async-start(s8[4325376]{0:T(1024)(128)(4,1)} %bitcast.2), calls=%async_computation | async-start | bytes 8388608
  5.0 9.2 %copy-start = (bf16[1536,1408]{1,0:T(8,128)(2,1)S(1)}, bf16[1536,1408]{1,0:T(8,128)(2,1)}, u32[]{:S(2)}) copy-start(bf16[1536,1408]{1,0:T(8,128)(2,1)} %down_ref.1) | copy-start | bytes 12976132
  5.0 9.2 %copy-start.8 = (f32[1408]{0:T(1024)S(1)}, f32[1408]{0:T(1024)}, u32[]{:S(2)}) copy-start(f32[1408]{0:T(1024)} %gain_ref.8) | copy-start | bytes 16900
  9.5 2.8 %collective-permute-start = (bf16[128,1408]{1,0:T(8,128)(2,1)S(1)}, bf16[128,1408]{1,0:T(8,128)(2,1)S(1)}, u32[]{:S(2)}, u32[]{:S(2)}) collective-permute-start(bf16[128,1408]{1,0:T(8,128)(2,1)S(1)} %get-tuple-element.44), channel_id=1, source_target_pairs={{0,1},{1,0},{2,3},{3,2},{4,5},{5,4},{6,7},{7,6},{8,9},{9,8},{10,11... | collective-permute-start | bytes 1081352 | tf_op jit(solution)/shard_map/ppermute | solution.py:54
  12.4 6.4 %collective-permute-start.1 = (bf16[64,1408]{1,0:T(8,128)(2,1)S(1)}, bf16[64,1408]{1,0:T(8,128)(2,1)S(1)}, u32[]{:S(2)}, u32[]{:S(2)}) collective-permute-start(bf16[64,1408]{1,0:T(8,128)(2,1)S(1)} %get-tuple-element.45.refs_5_), channel_id=1, source_target_pairs={{0,2},{1,3},{2,0},{3,1},{4,6},{5,7},{6,4},{7,5},{8,10},{9,11},{10,... | collective-permute-start | bytes 540680 | tf_op jit(solution)/shard_map/ppermute | solution.py:54
  19.2 2.3 %collective-permute-start.2 = (bf16[128,1408]{1,0:T(8,128)(2,1)S(1)}, bf16[128,1408]{1,0:T(8,128)(2,1)S(1)}, u32[]{:S(2)}, u32[]{:S(2)}) collective-permute-start(bf16[128,1408]{1,0:T(8,128)(2,1)S(1)} %shard_map.125), channel_id=1, source_target_pairs={{0,1},{1,0},{2,3},{3,2},{4,5},{5,4},{6,7},{7,6},{8,9},{9,8},{10,11... | collective-permute-start | bytes 1081352 | tf_op jit(solution)/shard_map/ppermute | solution.py:54
  21.6 5.8 %collective-permute-start.3 = (bf16[64,1408]{1,0:T(8,128)(2,1)S(1)}, bf16[64,1408]{1,0:T(8,128)(2,1)S(1)}, u32[]{:S(2)}, u32[]{:S(2)}) collective-permute-start(bf16[64,1408]{1,0:T(8,128)(2,1)S(1)} %get-tuple-element.51.refs_2_), channel_id=1, source_target_pairs={{0,2},{1,3},{2,0},{3,1},{4,6},{5,7},{6,4},{7,5},{8,10},{9,11},{10,... | collective-permute-start | bytes 540680 | tf_op jit(solution)/shard_map/ppermute | solution.py:54
  27.8 7.3 %collective-permute-start.4 = (bf16[64,1408]{1,0:T(8,128)(2,1)S(1)}, bf16[64,1408]{1,0:T(8,128)(2,1)S(1)}, u32[]{:S(2)}, u32[]{:S(2)}) collective-permute-start(bf16[64,1408]{1,0:T(8,128)(2,1)S(1)} %get-tuple-element.52.refs_0_), channel_id=1, source_target_pairs={{0,2},{1,7},{2,4},{3,1},{4,6},{5,3},{6,0},{7,5},{8,10},{9,15},{10,... | collective-permute-start | bytes 540680 | tf_op jit(solution)/shard_map/ppermute | solution.py:54
  31.4 7.1 %collective-permute-start.10 = (bf16[64,1408]{1,0:T(8,128)(2,1)S(1)}, bf16[64,1408]{1,0:T(8,128)(2,1)S(1)}, u32[]{:S(2)}, u32[]{:S(2)}) collective-permute-start(bf16[64,1408]{1,0:T(8,128)(2,1)S(1)} %get-tuple-element.49.refs_1_.refs_0_), channel_id=1, source_target_pairs={{0,16},{1,65},{2,18},{3,67},{4,20},{5,69},{6,22},{7,71},{8,24},{9,... | collective-permute-start | bytes 540680 | tf_op jit(solution)/shard_map/ppermute | solution.py:54
  34.3 5.5 %collective-permute-start.9 = (bf16[64,1408]{1,0:T(8,128)(2,1)S(1)}, bf16[64,1408]{1,0:T(8,128)(2,1)S(1)}, u32[]{:S(2)}, u32[]{:S(2)}) collective-permute-start(bf16[64,1408]{1,0:T(8,128)(2,1)S(1)} %get-tuple-element.49.refs_1_.refs_0_), channel_id=1, source_target_pairs={{0,24},{1,97},{2,26},{3,99},{4,28},{5,101},{6,30},{7,103},{8,0},{9... | collective-permute-start | bytes 540680 | tf_op jit(solution)/shard_map/ppermute | solution.py:54
  35.1 7.3 %collective-permute-start.5 = (bf16[64,1408]{1,0:T(8,128)(2,1)S(1)}, bf16[64,1408]{1,0:T(8,128)(2,1)S(1)}, u32[]{:S(2)}, u32[]{:S(2)}) collective-permute-start(bf16[64,1408]{1,0:T(8,128)(2,1)S(1)} %get-tuple-element.52.refs_0_), channel_id=1, source_target_pairs={{0,6},{1,3},{2,0},{3,5},{4,2},{5,7},{6,4},{7,1},{8,14},{9,11},{10,... | collective-permute-start | bytes 540680 | tf_op jit(solution)/shard_map/ppermute | solution.py:54
  35.1 7.3 %collective-permute-start.6 = (bf16[64,1408]{1,0:T(8,128)(2,1)S(1)}, bf16[64,1408]{1,0:T(8,128)(2,1)S(1)}, u32[]{:S(2)}, u32[]{:S(2)}) collective-permute-start(bf16[64,1408]{1,0:T(8,128)(2,1)S(1)} %collective-permute-done.4.refs_1_), channel_id=1, source_target_pairs={{0,2},{1,7},{2,4},{3,1},{4,6},{5,3},{6,0},{7,5},{8,10},{9,15},{10,... | collective-permute-start | bytes 540680 | tf_op jit(solution)/shard_map/ppermute | solution.py:54
  37.8 6.2 %collective-permute-start.8 = (bf16[64,1408]{1,0:T(8,128)(2,1)S(1)}, bf16[64,1408]{1,0:T(8,128)(2,1)S(1)}, u32[]{:S(2)}, u32[]{:S(2)}) collective-permute-start(bf16[64,1408]{1,0:T(8,128)(2,1)S(1)} %get-tuple-element.49.refs_1_.refs_0_), channel_id=1, source_target_pairs={{0,8},{1,33},{2,10},{3,35},{4,12},{5,37},{6,14},{7,39},{8,16},{9,4... | collective-permute-start | bytes 540680 | tf_op jit(solution)/shard_map/ppermute | solution.py:54
  39.9 7.5 %collective-permute-start.14 = (bf16[128,1408]{1,0:T(8,128)(2,1)S(1)}, bf16[128,1408]{1,0:T(8,128)(2,1)S(1)}, u32[]{:S(2)}, u32[]{:S(2)}) collective-permute-start(bf16[128,1408]{1,0:T(8,128)(2,1)S(1)} %shard_map.130.refs_3_), channel_id=1, source_target_pairs={{0,96},{1,25},{2,98},{3,27},{4,100},{5,29},{6,102},{7,31},{8,104},... | collective-permute-start | bytes 1081352 | tf_op jit(solution)/shard_map/ppermute | solution.py:54
  42.5 13.3 %collective-permute-start.7 = (bf16[256,1408]{1,0:T(8,128)(2,1)S(1)}, bf16[256,1408]{1,0:T(8,128)(2,1)S(1)}, u32[]{:S(2)}, u32[]{:S(2)}) collective-permute-start(bf16[256,1408]{1,0:T(8,128)(2,1)S(1)} %shard_map.128.refs_0_), channel_id=1, source_target_pairs={{0,1},{1,0},{2,3},{3,2},{4,5},{5,4},{6,7},{7,6},{8,9},{9,8},{10,11... | collective-permute-start | bytes 2162696 | tf_op jit(solution)/shard_map/ppermute | solution.py:54
  44.0 7.9 %collective-permute-start.11 = (bf16[128,1408]{1,0:T(8,128)(2,1)S(1)}, bf16[128,1408]{1,0:T(8,128)(2,1)S(1)}, u32[]{:S(2)}, u32[]{:S(2)}) collective-permute-start(bf16[128,1408]{1,0:T(8,128)(2,1)S(1)} %shard_map.129.refs_2_), channel_id=1, source_target_pairs={{0,32},{1,9},{2,34},{3,11},{4,36},{5,13},{6,38},{7,15},{8,40},{9,1... | collective-permute-start | bytes 1081352 | tf_op jit(solution)/shard_map/ppermute | solution.py:54
  44.7 11.0 %collective-permute-start.12 = (bf16[128,1408]{1,0:T(8,128)(2,1)S(1)}, bf16[128,1408]{1,0:T(8,128)(2,1)S(1)}, u32[]{:S(2)}, u32[]{:S(2)}) collective-permute-start(bf16[128,1408]{1,0:T(8,128)(2,1)S(1)} %shard_map.130.refs_3_), channel_id=1, source_target_pairs={{0,32},{1,9},{2,34},{3,11},{4,36},{5,13},{6,38},{7,15},{8,40},{9,1... | collective-permute-start | bytes 1081352 | tf_op jit(solution)/shard_map/ppermute | solution.py:54
  45.9 9.8 %collective-permute-start.13 = (bf16[128,1408]{1,0:T(8,128)(2,1)S(1)}, bf16[128,1408]{1,0:T(8,128)(2,1)S(1)}, u32[]{:S(2)}, u32[]{:S(2)}) collective-permute-start(bf16[128,1408]{1,0:T(8,128)(2,1)S(1)} %shard_map.129.refs_2_), channel_id=1, source_target_pairs={{0,96},{1,25},{2,98},{3,27},{4,100},{5,29},{6,102},{7,31},{8,104},... | collective-permute-start | bytes 1081352 | tf_op jit(solution)/shard_map/ppermute | solution.py:54
  47.4 13.0 %collective-permute-start.16 = (bf16[128,1408]{1,0:T(8,128)(2,1)S(1)}, bf16[128,1408]{1,0:T(8,128)(2,1)S(1)}, u32[]{:S(2)}, u32[]{:S(2)}) collective-permute-start(bf16[128,1408]{1,0:T(8,128)(2,1)S(1)} %collective-permute-done.14.refs_7_), channel_id=1, source_target_pairs={{0,96},{1,25},{2,98},{3,27},{4,100},{5,29},{6,102},{7,31},{8,104},... | collective-permute-start | bytes 1081352 | tf_op jit(solution)/shard_map/ppermute | solution.py:54
  51.9 8.6 %collective-permute-start.15 = (bf16[128,1408]{1,0:T(8,128)(2,1)S(1)}, bf16[128,1408]{1,0:T(8,128)(2,1)S(1)}, u32[]{:S(2)}, u32[]{:S(2)}) collective-permute-start(bf16[128,1408]{1,0:T(8,128)(2,1)S(1)} %collective-permute-done.11.refs_4_), channel_id=1, source_target_pairs={{0,32},{1,9},{2,34},{3,11},{4,36},{5,13},{6,38},{7,15},{8,40},{9,1... | collective-permute-start | bytes 1081352 | tf_op jit(solution)/shard_map/ppermute | solution.py:54
  62.8 5.2 %collective-permute-start.17 = (bf16[256,1536]{1,0:T(8,128)(2,1)S(1)}, bf16[256,1536]{1,0:T(8,128)(2,1)S(1)}, u32[]{:S(2)}, u32[]{:S(2)}) collective-permute-start(bf16[256,1536]{1,0:T(8,128)(2,1)S(1)} %get-tuple-element.57), channel_id=1, source_target_pairs={{0,1},{1,0},{2,3},{3,2},{4,5},{5,4},{6,7},{7,6},{8,9},{9,8},{10,11... | collective-permute-start | bytes 2359304 | tf_op jit(solution)/shard_map/ppermute | solution.py:54
  63.8 7.8 %collective-permute-start.31 = (bf16[128,1408]{1,0:T(8,128)(2,1)S(1)}, bf16[128,1408]{1,0:T(8,128)(2,1)S(1)}, u32[]{:S(2)}, u32[]{:S(2)}) collective-permute-start(bf16[128,1408]{1,0:T(8,128)(2,1)S(1)} %get-tuple-element.73), channel_id=1, source_target_pairs={{0,32},{1,9},{2,34},{3,11},{4,36},{5,13},{6,38},{7,15},{8,40},{9,1... | collective-permute-start | bytes 1081352 | tf_op jit(solution)/shard_map/ppermute | solution.py:54
  64.5 7.3 %collective-permute-start.27 = (bf16[128,1408]{1,0:T(8,128)(2,1)S(1)}, bf16[128,1408]{1,0:T(8,128)(2,1)S(1)}, u32[]{:S(2)}, u32[]{:S(2)}) collective-permute-start(bf16[128,1408]{1,0:T(8,128)(2,1)S(1)} %get-tuple-element.69), channel_id=1, source_target_pairs={{0,96},{1,25},{2,98},{3,27},{4,100},{5,29},{6,102},{7,31},{8,104},... | collective-permute-start | bytes 1081352 | tf_op jit(solution)/shard_map/ppermute | solution.py:54
  66.5 14.8 %collective-permute-start.29 = (bf16[128,1408]{1,0:T(8,128)(2,1)S(1)}, bf16[128,1408]{1,0:T(8,128)(2,1)S(1)}, u32[]{:S(2)}, u32[]{:S(2)}) collective-permute-start(bf16[128,1408]{1,0:T(8,128)(2,1)S(1)} %get-tuple-element.70), channel_id=1, source_target_pairs={{0,96},{1,25},{2,98},{3,27},{4,100},{5,29},{6,102},{7,31},{8,104},... | collective-permute-start | bytes 1081352 | tf_op jit(solution)/shard_map/ppermute | solution.py:54
  67.2 16.4 %collective-permute-start.30 = (bf16[128,1408]{1,0:T(8,128)(2,1)S(1)}, bf16[128,1408]{1,0:T(8,128)(2,1)S(1)}, u32[]{:S(2)}, u32[]{:S(2)}) collective-permute-start(bf16[128,1408]{1,0:T(8,128)(2,1)S(1)} %get-tuple-element.71), channel_id=1, source_target_pairs={{0,32},{1,9},{2,34},{3,11},{4,36},{5,13},{6,38},{7,15},{8,40},{9,1... | collective-permute-start | bytes 1081352 | tf_op jit(solution)/shard_map/ppermute | solution.py:54
  71.7 12.0 %copy-start.13 = (f32[256,1408]{1,0:T(8,128)S(1)}, f32[256,1408]{1,0:T(8,128)}, u32[]{:S(2)}) copy-start(f32[256,1408]{1,0:T(8,128)} %copy-done.12) | copy-start | bytes 4325380
  71.7 11.9 %collective-permute-start.32 = (bf16[128,1408]{1,0:T(8,128)(2,1)S(1)}, bf16[128,1408]{1,0:T(8,128)(2,1)S(1)}, u32[]{:S(2)}, u32[]{:S(2)}) collective-permute-start(bf16[128,1408]{1,0:T(8,128)(2,1)S(1)} %shard_map.141), channel_id=1, source_target_pairs={{0,32},{1,9},{2,34},{3,11},{4,36},{5,13},{6,38},{7,15},{8,40},{9,1... | collective-permute-start | bytes 1081352 | tf_op jit(solution)/shard_map/ppermute | solution.py:54
  71.9 11.8 %collective-permute-start.28 = (bf16[128,1408]{1,0:T(8,128)(2,1)S(1)}, bf16[128,1408]{1,0:T(8,128)(2,1)S(1)}, u32[]{:S(2)}, u32[]{:S(2)}) collective-permute-start(bf16[128,1408]{1,0:T(8,128)(2,1)S(1)} %shard_map.140), channel_id=1, source_target_pairs={{0,96},{1,25},{2,98},{3,27},{4,100},{5,29},{6,102},{7,31},{8,104},... | collective-permute-start | bytes 1081352 | tf_op jit(solution)/shard_map/ppermute | solution.py:54
  74.6 6.1 %collective-permute-start.18 = (bf16[64,1536]{1,0:T(8,128)(2,1)S(1)}, bf16[64,1536]{1,0:T(8,128)(2,1)S(1)}, u32[]{:S(2)}, u32[]{:S(2)}) collective-permute-start(bf16[64,1536]{1,0:T(8,128)(2,1)S(1)} %get-tuple-element.59.refs_2_), channel_id=1, source_target_pairs={{0,6},{1,3},{2,0},{3,5},{4,2},{5,7},{6,4},{7,1},{8,14},{9,11},{10,... | collective-permute-start | bytes 589832 | tf_op jit(solution)/shard_map/ppermute | solution.py:54
  80.9 6.1 %collective-permute-start.19 = (bf16[64,1536]{1,0:T(8,128)(2,1)S(1)}, bf16[64,1536]{1,0:T(8,128)(2,1)S(1)}, u32[]{:S(2)}, u32[]{:S(2)}) collective-permute-start(bf16[64,1536]{1,0:T(8,128)(2,1)S(1)} %get-tuple-element.60.refs_5_), channel_id=1, source_target_pairs={{0,6},{1,3},{2,0},{3,5},{4,2},{5,7},{6,4},{7,1},{8,14},{9,11},{10,... | collective-permute-start | bytes 589832 | tf_op jit(solution)/shard_map/ppermute | solution.py:54
  81.3 5.6 %collective-permute-start.20 = (bf16[64,1536]{1,0:T(8,128)(2,1)S(1)}, bf16[64,1536]{1,0:T(8,128)(2,1)S(1)}, u32[]{:S(2)}, u32[]{:S(2)}) collective-permute-start(bf16[64,1536]{1,0:T(8,128)(2,1)S(1)} %get-tuple-element.61), channel_id=1, source_target_pairs={{0,2},{1,7},{2,4},{3,1},{4,6},{5,3},{6,0},{7,5},{8,10},{9,15},{10,... | collective-permute-start | bytes 589832 | tf_op jit(solution)/shard_map/ppermute | solution.py:54
  83.9 5.1 %collective-permute-start.33 = (bf16[64,1408]{1,0:T(8,128)(2,1)S(1)}, bf16[64,1408]{1,0:T(8,128)(2,1)S(1)}, u32[]{:S(2)}, u32[]{:S(2)}) collective-permute-start(bf16[64,1408]{1,0:T(8,128)(2,1)S(1)} %get-tuple-element.75), channel_id=1, source_target_pairs={{0,24},{1,97},{2,26},{3,99},{4,28},{5,101},{6,30},{7,103},{8,0},{9... | collective-permute-start | bytes 540680 | tf_op jit(solution)/shard_map/ppermute | solution.py:54
  85.7 7.8 %collective-permute-start.34 = (bf16[64,1408]{1,0:T(8,128)(2,1)S(1)}, bf16[64,1408]{1,0:T(8,128)(2,1)S(1)}, u32[]{:S(2)}, u32[]{:S(2)}) collective-permute-start(bf16[64,1408]{1,0:T(8,128)(2,1)S(1)} %get-tuple-element.76), channel_id=1, source_target_pairs={{0,8},{1,33},{2,10},{3,35},{4,12},{5,37},{6,14},{7,39},{8,16},{9,4... | collective-permute-start | bytes 540680 | tf_op jit(solution)/shard_map/ppermute | solution.py:54
  85.7 7.8 %collective-permute-start.35 = (bf16[64,1408]{1,0:T(8,128)(2,1)S(1)}, bf16[64,1408]{1,0:T(8,128)(2,1)S(1)}, u32[]{:S(2)}, u32[]{:S(2)}) collective-permute-start(bf16[64,1408]{1,0:T(8,128)(2,1)S(1)} %get-tuple-element.77), channel_id=1, source_target_pairs={{0,16},{1,65},{2,18},{3,67},{4,20},{5,69},{6,22},{7,71},{8,24},{9,... | collective-permute-start | bytes 540680 | tf_op jit(solution)/shard_map/ppermute | solution.py:54
  87.5 9.7 %collective-permute-start.21 = (bf16[64,1536]{1,0:T(8,128)(2,1)S(1)}, bf16[64,1536]{1,0:T(8,128)(2,1)S(1)}, u32[]{:S(2)}, u32[]{:S(2)}) collective-permute-start(bf16[64,1536]{1,0:T(8,128)(2,1)S(1)} %shard_map.135.r0.refs_6_), channel_id=1, source_target_pairs={{0,2},{1,3},{2,0},{3,1},{4,6},{5,7},{6,4},{7,5},{8,10},{9,11},{10,... | collective-permute-start | bytes 589832 | tf_op jit(solution)/shard_map/ppermute | solution.py:54
  93.4 9.7 %copy-start.6 = (f32[256,1536]{1,0:T(8,128)S(1)}, f32[256,1536]{1,0:T(8,128)}, u32[]{:S(2)}) copy-start(f32[256,1536]{1,0:T(8,128)} %copy-done.5) | copy-start | bytes 4718596
  94.0 7.2 %collective-permute-start.36 = (bf16[64,1408]{1,0:T(8,128)(2,1)S(1)}, bf16[64,1408]{1,0:T(8,128)(2,1)S(1)}, u32[]{:S(2)}, u32[]{:S(2)}) collective-permute-start(bf16[64,1408]{1,0:T(8,128)(2,1)S(1)} %shard_map.143.refs_0_.r0), channel_id=1, source_target_pairs={{0,2},{1,3},{2,0},{3,1},{4,6},{5,7},{6,4},{7,5},{8,10},{9,11},{10,... | collective-permute-start | bytes 540680 | tf_op jit(solution)/shard_map/ppermute | solution.py:54
  94.1 9.1 %collective-permute-start.22 = (bf16[64,1536]{1,0:T(8,128)(2,1)S(1)}, bf16[64,1536]{1,0:T(8,128)(2,1)S(1)}, u32[]{:S(2)}, u32[]{:S(2)}) collective-permute-start(bf16[64,1536]{1,0:T(8,128)(2,1)S(1)} %shard_map.135.r0.refs_6_), channel_id=1, source_target_pairs={{0,1},{1,0},{2,3},{3,2},{4,5},{5,4},{6,7},{7,6},{8,9},{9,8},{10,11... | collective-permute-start | bytes 589832 | tf_op jit(solution)/shard_map/ppermute | solution.py:54
  97.2 5.9 %collective-permute-start.23 = (bf16[64,1536]{1,0:T(8,128)(2,1)S(1)}, bf16[64,1536]{1,0:T(8,128)(2,1)S(1)}, u32[]{:S(2)}, u32[]{:S(2)}) collective-permute-start(bf16[64,1536]{1,0:T(8,128)(2,1)S(1)} %collective-permute-done.21.r1), channel_id=1, source_target_pairs={{0,1},{1,0},{2,3},{3,2},{4,5},{5,4},{6,7},{7,6},{8,9},{9,8},{10,11... | collective-permute-start | bytes 589832 | tf_op jit(solution)/shard_map/ppermute | solution.py:54
  101.2 5.0 %collective-permute-start.37 = (bf16[64,1408]{1,0:T(8,128)(2,1)S(1)}, bf16[64,1408]{1,0:T(8,128)(2,1)S(1)}, u32[]{:S(2)}, u32[]{:S(2)}) collective-permute-start(bf16[64,1408]{1,0:T(8,128)(2,1)S(1)} %shard_map.143.refs_0_.r0), channel_id=1, source_target_pairs={{0,1},{1,0},{2,3},{3,2},{4,5},{5,4},{6,7},{7,6},{8,9},{9,8},{10,11... | collective-permute-start | bytes 540680 | tf_op jit(solution)/shard_map/ppermute | solution.py:54
  101.2 5.0 %collective-permute-start.38 = (bf16[64,1408]{1,0:T(8,128)(2,1)S(1)}, bf16[64,1408]{1,0:T(8,128)(2,1)S(1)}, u32[]{:S(2)}, u32[]{:S(2)}) collective-permute-start(bf16[64,1408]{1,0:T(8,128)(2,1)S(1)} %collective-permute-done.36.refs_1_.r1), channel_id=1, source_target_pairs={{0,1},{1,0},{2,3},{3,2},{4,5},{5,4},{6,7},{7,6},{8,9},{9,8},{10,11... | collective-permute-start | bytes 540680 | tf_op jit(solution)/shard_map/ppermute | solution.py:54
  106.1 3.6 %collective-permute-start.24 = (bf16[128,1408]{1,0:T(8,128)(2,1)S(1)}, bf16[128,1408]{1,0:T(8,128)(2,1)S(1)}, u32[]{:S(2)}, u32[]{:S(2)}) collective-permute-start(bf16[128,1408]{1,0:T(8,128)(2,1)S(1)} %get-tuple-element.65.refs_7_), channel_id=1, source_target_pairs={{0,1},{1,0},{2,3},{3,2},{4,5},{5,4},{6,7},{7,6},{8,9},{9,8},{10,11... | collective-permute-start | bytes 1081352 | tf_op jit(solution)/shard_map/ppermute | solution.py:54
  109.1 1.9 %collective-permute-start.39 = (bf16[128,1408]{1,0:T(8,128)(2,1)S(1)}, bf16[128,1408]{1,0:T(8,128)(2,1)S(1)}, u32[]{:S(2)}, u32[]{:S(2)}) collective-permute-start(bf16[128,1408]{1,0:T(8,128)(2,1)S(1)} %get-tuple-element.81), channel_id=1, source_target_pairs={{0,1},{1,0},{2,3},{3,2},{4,5},{5,4},{6,7},{7,6},{8,9},{9,8},{10,11... | collective-permute-start | bytes 1081352 | tf_op jit(solution)/shard_map/ppermute | solution.py:54
  109.8 10.1 %collective-permute-start.25 = (bf16[128,1408]{1,0:T(8,128)(2,1)S(1)}, bf16[128,1408]{1,0:T(8,128)(2,1)S(1)}, u32[]{:S(2)}, u32[]{:S(2)}) collective-permute-start(bf16[128,1408]{1,0:T(8,128)(2,1)S(1)} %shard_map.137.own_ref), channel_id=1, source_target_pairs={{0,2},{1,3},{2,0},{3,1},{4,6},{5,7},{6,4},{7,5},{8,10},{9,11},{10,... | collective-permute-start | bytes 1081352 | tf_op jit(solution)/shard_map/ppermute | solution.py:54
  111.0 16.5 %collective-permute-start.40 = (bf16[128,1408]{1,0:T(8,128)(2,1)S(1)}, bf16[128,1408]{1,0:T(8,128)(2,1)S(1)}, u32[]{:S(2)}, u32[]{:S(2)}) collective-permute-start(bf16[128,1408]{1,0:T(8,128)(2,1)S(1)} %shard_map.145.own_ref), channel_id=1, source_target_pairs={{0,2},{1,3},{2,0},{3,1},{4,6},{5,7},{6,4},{7,5},{8,10},{9,11},{10,... | collective-permute-start | bytes 1081352 | tf_op jit(solution)/shard_map/ppermute | solution.py:54
  120.0 10.8 %copy-start.10 = (f32[1408]{0:T(1024)S(1)}, f32[1408]{0:T(1024)}, u32[]{:S(2)}) copy-start(f32[1408]{0:T(1024)} %gain_ref.9) | copy-start | bytes 16900
  120.0 8.6 %collective-permute-start.26 = (bf16[128,1408]{1,0:T(8,128)(2,1)S(1)}, bf16[128,1408]{1,0:T(8,128)(2,1)S(1)}, u32[]{:S(2)}, u32[]{:S(2)}) collective-permute-start(bf16[128,1408]{1,0:T(8,128)(2,1)S(1)} %shard_map.138.own_ref), channel_id=1, source_target_pairs={{0,1},{1,0},{2,3},{3,2},{4,5},{5,4},{6,7},{7,6},{8,9},{9,8},{10,11... | collective-permute-start | bytes 1081352 | tf_op jit(solution)/shard_map/ppermute | solution.py:54
  127.7 3.0 %collective-permute-start.41 = (bf16[128,1408]{1,0:T(8,128)(2,1)S(1)}, bf16[128,1408]{1,0:T(8,128)(2,1)S(1)}, u32[]{:S(2)}, u32[]{:S(2)}) collective-permute-start(bf16[128,1408]{1,0:T(8,128)(2,1)S(1)} %shard_map.146.own_ref), channel_id=1, source_target_pairs={{0,1},{1,0},{2,3},{3,2},{4,5},{5,4},{6,7},{7,6},{8,9},{9,8},{10,11... | collective-permute-start | bytes 1081352 | tf_op jit(solution)/shard_map/ppermute | solution.py:54
  (12 other events, 49.8 us)

commit v3 on v2

--- a/solution.py
+++ b/solution.py
@@ -293,11 +293,16 @@
     return near, left, right, far
 
 
-def gather_column(own):
+def passed_body(block_ref, out_ref):
+    out_ref[...] = block_ref[...]
+
+
+def gather_column(own, left, right, far):
     ahead = send(own, Z_OUT)
     behind = send(own, Z_BACK)
-    across = send(ahead, Z_OUT)
-    blocks = stacked(own, ahead, behind, across)
+    passed = call(passed_body, [shape(BLOCK, WIDTH, bf16)], [ahead], after=[left[0], right[1]])[0]
+    across = send(passed, Z_OUT)
+    blocks = stacked(own, ahead, behind, across, after=[left[1], right[0], *far])
     return blocks, send(blocks, SIBLING)
 
 
@@ -456,7 +461,7 @@
     across = send(across, first_ring(2))
     before = send(before, first_ring(-1))
     after = send(after, first_ring(1))
-    image = call(image_head_body, [packed16], [column, got_ahead, got_behind, *image_head])[0]
+    image = call(image_head_body, [packed16], [column, got_ahead, got_behind, *image_head], after=[own])[0]
     text = call(text_head_body, [block16], [own, before, after, across, *text_head], after=[image], flops=2 << 30)[0]
     return image, text
 
@@ -532,8 +537,8 @@
     text_resid, z_text = scattered_embed(mine, own, sent, text_in, text_final, [image_rest])
     own, sent = scatter_half(image_keep, rounded(image_rest, [z_text]))
     near, left, right, far = gather_plane(z_text, [sent])
-    image_resid, z_image = scattered_embed(mine, own, sent, image_in, image_final)
-    images = gather_column(z_image)
+    image_resid, z_image = scattered_embed(mine, own, sent, image_in, image_final, list(near))
+    images = gather_column(z_image, left, right, far)
 
     *text_grads, keep, sent = pair_tile(images, near, left, right, far)
     image_own, text_own = scatter_both(

time: 133 us -> 133 us (level)
    pallas_call x26 -> x27, Pallas kernels: 23.1 us -> 23.1 us  [call(): pl.pallas_call(body, out_shape=outs, in_specs=specs, out_specs=[pl.BlockS...]
  transfers between devices with their start and end apart: 42 -> 42, of which waited for: 13 -> 16; matrix products, arithmetic and copies ran while one was open for 0% -> 0% of each run, Pallas kernels for 13% -> 10%
where the time goes in v3:
time: 133 us
  starting transfers between devices  57 us (43%)
  waiting for transfers between devices  43.1 us (32%)
  Pallas kernels  27.6 us (21%)
  local copies, waits for them, and re-layouts  4.43 us (3%)
    ppermute x42, starting transfers between devices, send(): return lax.ppermute(value, AXES, pairs)  57 us
    ppermute x42, waiting for transfers between devices, send(): return lax.ppermute(value, AXES, pairs)  43.1 us
    pallas_call x27, Pallas kernels, call(): pl.pallas_call(body, out_shape=outs, in_specs=specs, out_specs=[pl.BlockS...  23.1 us
    pallas_call x1, Pallas kernels, tower_streamed(): pl.pallas_call(streamed_body, in_specs=[pl.BlockSpec(memory_space=pltpu.S...  4.44 us
    unnamed x36, local copies, waits for them, and re-layouts  4.43 us
  transfers between devices with their start and end apart: 42, of which 16 were waited for; matrix products, arithmetic and copies ran while one was open for 0% of the time, Pallas kernels for 10%

profile of v3, /device:TPU:1, one launch (start us, length us, event | category | flops | bytes accessed | tf_op | source)
XLA Modules:
  0.0 133.2 jit_solution(6739225711923511991)
XLA Ops:
  0.7 2.4 %copy-done.1 = bf16[1408,1536]{1,0:T(8,128)(2,1)S(1)} copy-done((bf16[1408,1536]{1,0:T(8,128)(2,1)S(1)}, bf16[1408,1536]{1,0:T(8,128)(2,1)}, u32[]{:S(2)}) %copy-start.1) | copy-done | bytes 4325400
  3.0 1.3 copy-done.3
  5.0 4.4 %shard_map.121 = (f32[256,1536]{1,0:T(8,128)S(1)}, f32[128,1408]{1,0:T(8,128)S(1)}, bf16[128,1408]{1,0:T(8,128)(2,1)S(1)}) custom-call(s32[1]{0:T(128)} %bitcast.mine.refs_0_, bf16[256,1408]{1,0:T(8,128)(2,1)S(1)} %copy-done.3, f32[1408]{0:T(1024)S(1)} %copy-done.9, bf16[1408,1536]{1,0:T(8,128)(2,1)S(1)} %copy-done.1, bf16[1536,1408]{1,0:T(8,128)(2,1)} %refs_6_.1), custom_call_target="tpu_custom_call" | custom-call | flops 1 | bytes 1 | tf_op jit(solution)/shard_map/pallas_call | solution.py:192
  9.5 1.5 %collective-permute-start = (bf16[128,1408]{1,0:T(8,128)(2,1)S(1)}, bf16[128,1408]{1,0:T(8,128)(2,1)S(1)}, u32[]{:S(2)}, u32[]{:S(2)}) collective-permute-start(bf16[128,1408]{1,0:T(8,128)(2,1)S(1)} %get-tuple-element.44), channel_id=1, source_target_pairs={{0,1},{1,0},{2,3},{3,2},{4,5},{5,4},{6,7},{7,6},{8,9},{9,8},{10,11... | collective-permute-start | bytes 1081352 | tf_op jit(solution)/shard_map/ppermute | solution.py:54
  11.0 1.3 collective-permute-done.got_ref
  12.4 1.8 %collective-permute-start.1 = (bf16[64,1408]{1,0:T(8,128)(2,1)S(1)}, bf16[64,1408]{1,0:T(8,128)(2,1)S(1)}, u32[]{:S(2)}, u32[]{:S(2)}) collective-permute-start(bf16[64,1408]{1,0:T(8,128)(2,1)S(1)} %get-tuple-element.45.refs_5_), channel_id=1, source_target_pairs={{0,2},{1,3},{2,0},{3,1},{4,6},{5,7},{6,4},{7,5},{8,10},{9,11},{10,... | collective-permute-start | bytes 540680 | tf_op jit(solution)/shard_map/ppermute | solution.py:54
  14.2 3.1 %shard_map.123 = (f32[256,1536]{1,0:T(8,128)S(1)}, f32[128,1408]{1,0:T(8,128)S(1)}, f32[128,1408]{1,0:T(8,128)S(1)}) custom-call(s32[1]{0:T(128)} %bitcast.mine.refs_0_, bf16[256,1408]{1,0:T(8,128)(2,1)S(1)} %copy-done.2, f32[1408]{0:T(1024)S(1)} %copy-done.8, bf16[1408,1536]{1,0:T(8,128)(2,1)S(1)} %bitcast.3, bf16[1536,1408]{1,0:T(8,128)(2,1)S(1)} %copy-done, ...), custom_call_target="tpu_custom_call" | custom-call | flops 2214592512 | bytes 1 | tf_op jit(solution)/shard_map/pallas_call | solution.py:75
  17.3 1.5 %collective-permute-done.1.refs_2_ = bf16[64,1408]{1,0:T(8,128)(2,1)S(1)} collective-permute-done((bf16[64,1408]{1,0:T(8,128)(2,1)S(1)}, bf16[64,1408]{1,0:T(8,128)(2,1)S(1)}, u32[]{:S(2)}, u32[]{:S(2)}) %collective-permute-start.1) | collective-permute-done | bytes 180256 | tf_op jit(solution)/shard_map/ppermute | solution.py:54
  19.2 1.0 collective-permute-start.2
  20.2 2.9 %collective-permute-start.6 = (bf16[64,1408]{1,0:T(8,128)(2,1)S(1)}, bf16[64,1408]{1,0:T(8,128)(2,1)S(1)}, u32[]{:S(2)}, u32[]{:S(2)}) collective-permute-start(bf16[64,1408]{1,0:T(8,128)(2,1)S(1)} %get-tuple-element.49.refs_1_.refs_0_), channel_id=1, source_target_pairs={{0,16},{1,65},{2,18},{3,67},{4,20},{5,69},{6,22},{7,71},{8,24},{9,... | collective-permute-start | bytes 540680 | tf_op jit(solution)/shard_map/ppermute | solution.py:54
  23.1 0.8 collective-permute-start.5
  24.6 1.8 %collective-permute-done.6.refs_1_ = bf16[64,1408]{1,0:T(8,128)(2,1)S(1)} collective-permute-done((bf16[64,1408]{1,0:T(8,128)(2,1)S(1)}, bf16[64,1408]{1,0:T(8,128)(2,1)S(1)}, u32[]{:S(2)}, u32[]{:S(2)}) %collective-permute-start.6) | collective-permute-done | bytes 180256 | tf_op jit(solution)/shard_map/ppermute | solution.py:54
  26.3 2.3 %collective-permute-done.5.refs_0_ = bf16[64,1408]{1,0:T(8,128)(2,1)S(1)} collective-permute-done((bf16[64,1408]{1,0:T(8,128)(2,1)S(1)}, bf16[64,1408]{1,0:T(8,128)(2,1)S(1)}, u32[]{:S(2)}, u32[]{:S(2)}) %collective-permute-start.5) | collective-permute-done | bytes 180256 | tf_op jit(solution)/shard_map/ppermute | solution.py:54
  28.6 2.5 %collective-permute-start.10 = (bf16[128,1408]{1,0:T(8,128)(2,1)S(1)}, bf16[128,1408]{1,0:T(8,128)(2,1)S(1)}, u32[]{:S(2)}, u32[]{:S(2)}) collective-permute-start(bf16[128,1408]{1,0:T(8,128)(2,1)S(1)} %shard_map.128.refs_6_.refs_3_), channel_id=1, source_target_pairs={{0,96},{1,25},{2,98},{3,27},{4,100},{5,29},{6,102},{7,31},{8,104},... | collective-permute-start | bytes 1081352 | tf_op jit(solution)/shard_map/ppermute | solution.py:54
  31.4 1.5 %collective-permute-start.3 = (bf16[64,1408]{1,0:T(8,128)(2,1)S(1)}, bf16[64,1408]{1,0:T(8,128)(2,1)S(1)}, u32[]{:S(2)}, u32[]{:S(2)}) collective-permute-start(bf16[64,1408]{1,0:T(8,128)(2,1)S(1)} %get-tuple-element.51.refs_2_), channel_id=1, source_target_pairs={{0,2},{1,3},{2,0},{3,1},{4,6},{5,7},{6,4},{7,5},{8,10},{9,11},{10,... | collective-permute-start | bytes 540680 | tf_op jit(solution)/shard_map/ppermute | solution.py:54
  33.4 2.8 %collective-permute-done.3.refs_2_ = bf16[64,1408]{1,0:T(8,128)(2,1)S(1)} collective-permute-done((bf16[64,1408]{1,0:T(8,128)(2,1)S(1)}, bf16[64,1408]{1,0:T(8,128)(2,1)S(1)}, u32[]{:S(2)}, u32[]{:S(2)}) %collective-permute-start.3) | collective-permute-done | bytes 180256 | tf_op jit(solution)/shard_map/ppermute | solution.py:54
  36.5 3.7 %collective-permute-start.7 = (bf16[64,1408]{1,0:T(8,128)(2,1)S(1)}, bf16[64,1408]{1,0:T(8,128)(2,1)S(1)}, u32[]{:S(2)}, u32[]{:S(2)}) collective-permute-start(bf16[64,1408]{1,0:T(8,128)(2,1)S(1)} %get-tuple-element.52.refs_0_), channel_id=1, source_target_pairs={{0,2},{1,7},{2,4},{3,1},{4,6},{5,3},{6,0},{7,5},{8,10},{9,15},{10,... | collective-permute-start | bytes 540680 | tf_op jit(solution)/shard_map/ppermute | solution.py:54
  40.2 2.9 %collective-permute-start.13 = (bf16[128,1408]{1,0:T(8,128)(2,1)S(1)}, bf16[128,1408]{1,0:T(8,128)(2,1)S(1)}, u32[]{:S(2)}, u32[]{:S(2)}) collective-permute-start(bf16[128,1408]{1,0:T(8,128)(2,1)S(1)} %shard_map.127.refs_5_.refs_2_), channel_id=1, source_target_pairs={{0,96},{1,25},{2,98},{3,27},{4,100},{5,29},{6,102},{7,31},{8,104},... | collective-permute-start | bytes 1081352 | tf_op jit(solution)/shard_map/ppermute | solution.py:54
  43.1 1.4 %collective-permute-start.14 = (bf16[128,1408]{1,0:T(8,128)(2,1)S(1)}, bf16[128,1408]{1,0:T(8,128)(2,1)S(1)}, u32[]{:S(2)}, u32[]{:S(2)}) collective-permute-start(bf16[128,1408]{1,0:T(8,128)(2,1)S(1)} %collective-permute-done.9.refs_1_.refs_4_), channel_id=1, source_target_pairs={{0,32},{1,9},{2,34},{3,11},{4,36},{5,13},{6,38},{7,15},{8,40},{9,1... | collective-permute-start | bytes 1081352 | tf_op jit(solution)/shard_map/ppermute | solution.py:54
  44.6 2.9 %collective-permute-start.11 = (bf16[64,1408]{1,0:T(8,128)(2,1)S(1)}, bf16[64,1408]{1,0:T(8,128)(2,1)S(1)}, u32[]{:S(2)}, u32[]{:S(2)}) collective-permute-start(bf16[64,1408]{1,0:T(8,128)(2,1)S(1)} %shard_map.130), channel_id=1, source_target_pairs={{0,2},{1,7},{2,4},{3,1},{4,6},{5,3},{6,0},{7,5},{8,10},{9,15},{10,... | collective-permute-start | bytes 540680 | tf_op jit(solution)/shard_map/ppermute | solution.py:54
  47.5 2.9 %collective-permute-done.8.refs_2_ = bf16[64,1408]{1,0:T(8,128)(2,1)S(1)} collective-permute-done((bf16[64,1408]{1,0:T(8,128)(2,1)S(1)}, bf16[64,1408]{1,0:T(8,128)(2,1)S(1)}, u32[]{:S(2)}, u32[]{:S(2)}) %collective-permute-start.8) | collective-permute-done | bytes 180256 | tf_op jit(solution)/shard_map/ppermute | solution.py:54
  50.4 0.9 collective-permute-done.15.refs_7_.far1
  51.4 4.0 %collective-permute-start.16 = (bf16[256,1408]{1,0:T(8,128)(2,1)S(1)}, bf16[256,1408]{1,0:T(8,128)(2,1)S(1)}, u32[]{:S(2)}, u32[]{:S(2)}) collective-permute-start(bf16[256,1408]{1,0:T(8,128)(2,1)S(1)} %shard_map.131.refs_0_), channel_id=1, source_target_pairs={{0,1},{1,0},{2,3},{3,2},{4,5},{5,4},{6,7},{7,6},{8,9},{9,8},{10,11... | collective-permute-start | bytes 2162696 | tf_op jit(solution)/shard_map/ppermute | solution.py:54
  55.4 1.8 %collective-permute-done.16.refs_1_ = bf16[256,1408]{1,0:T(8,128)(2,1)S(1)} collective-permute-done((bf16[256,1408]{1,0:T(8,128)(2,1)S(1)}, bf16[256,1408]{1,0:T(8,128)(2,1)S(1)}, u32[]{:S(2)}, u32[]{:S(2)}) %collective-permute-start.16) | collective-permute-done | bytes 720928 | tf_op jit(solution)/shard_map/ppermute | solution.py:54
  57.2 4.7 %shard_map.132 = (bf16[512,1408]{1,0:T(8,128)(2,1)S(1)}, f32[512,1408]{1,0:T(8,128)S(1)}, f32[512,128]{1,0:T(8,128)S(1)}, f32[256,1408]{1,0:T(8,128)S(1)}, f32[1...) custom-call(bf16[256,1408]{1,0:T(8,128)(2,1)S(1)} %shard_map.131.ref, ...), custom_call_target="tpu_custom_call" | custom-call | flops 1 | bytes 1 | tf_op jit(solution)/shard_map/pallas_call | solution.py:75
  61.8 2.3 %shard_map.133 = (bf16[128,1408]{1,0:T(8,128)(2,1)S(1)}, bf16[128,1408]{1,0:T(8,128)(2,1)S(1)}, f32[256,1536]{1,0:T(8,128)S(1)}, bf16[256,1536]{1,0:T(8,128)(2,1)S(1)}) custom-call(bf16[512,1408]{1,0:T(8,128)(2,1)S(1)} %get-tuple-element.53.image_ref, f32[512,1408]{1,0:T(8,128)S(1)} %get-tuple-element.54.total_ref, ...), custom_call_target="tpu_custom_call" | custom-call | flops 1 | bytes 1 | tf_op jit(solution)/shard_map/pallas_call | solution.py:75
  64.6 2.6 %collective-permute-start.21 = (bf16[128,1408]{1,0:T(8,128)(2,1)S(1)}, bf16[128,1408]{1,0:T(8,128)(2,1)S(1)}, u32[]{:S(2)}, u32[]{:S(2)}) collective-permute-start(bf16[128,1408]{1,0:T(8,128)(2,1)S(1)} %get-tuple-element.65), channel_id=1, source_target_pairs={{0,96},{1,25},{2,98},{3,27},{4,100},{5,29},{6,102},{7,31},{8,104},... | collective-permute-start | bytes 1081352 | tf_op jit(solution)/shard_map/ppermute | solution.py:54
  67.2 2.7 %collective-permute-start.23 = (bf16[128,1408]{1,0:T(8,128)(2,1)S(1)}, bf16[128,1408]{1,0:T(8,128)(2,1)S(1)}, u32[]{:S(2)}, u32[]{:S(2)}) collective-permute-start(bf16[128,1408]{1,0:T(8,128)(2,1)S(1)} %get-tuple-element.66), channel_id=1, source_target_pairs={{0,96},{1,25},{2,98},{3,27},{4,100},{5,29},{6,102},{7,31},{8,104},... | collective-permute-start | bytes 1081352 | tf_op jit(solution)/shard_map/ppermute | solution.py:54
  70.1 1.5 %collective-permute-done.21.refs_1_ = bf16[128,1408]{1,0:T(8,128)(2,1)S(1)} collective-permute-done((bf16[128,1408]{1,0:T(8,128)(2,1)S(1)}, bf16[128,1408]{1,0:T(8,128)(2,1)S(1)}, u32[]{:S(2)}, u32[]{:S(2)}) %collective-permute-start.21) | collective-permute-done | bytes 360480 | tf_op jit(solution)/shard_map/ppermute | solution.py:54
  71.7 3.5 %collective-permute-start.22 = (bf16[128,1408]{1,0:T(8,128)(2,1)S(1)}, bf16[128,1408]{1,0:T(8,128)(2,1)S(1)}, u32[]{:S(2)}, u32[]{:S(2)}) collective-permute-start(bf16[128,1408]{1,0:T(8,128)(2,1)S(1)} %shard_map.136), channel_id=1, source_target_pairs={{0,96},{1,25},{2,98},{3,27},{4,100},{5,29},{6,102},{7,31},{8,104},... | collective-permute-start | bytes 1081352 | tf_op jit(solution)/shard_map/ppermute | solution.py:54
  75.4 6.0 %collective-permute-done.18.got_ref = bf16[64,1536]{1,0:T(8,128)(2,1)S(1)} collective-permute-done((bf16[64,1536]{1,0:T(8,128)(2,1)S(1)}, bf16[64,1536]{1,0:T(8,128)(2,1)S(1)}, u32[]{:S(2)}, u32[]{:S(2)}) %collective-permute-start.18) | collective-permute-done | bytes 196640 | tf_op jit(solution)/shard_map/ppermute | solution.py:54
  81.6 1.4 %collective-permute-start.19 = (bf16[64,1536]{1,0:T(8,128)(2,1)S(1)}, bf16[64,1536]{1,0:T(8,128)(2,1)S(1)}, u32[]{:S(2)}, u32[]{:S(2)}) collective-permute-start(bf16[64,1536]{1,0:T(8,128)(2,1)S(1)} %get-tuple-element.60.refs_5_), channel_id=1, source_target_pairs={{0,6},{1,3},{2,0},{3,5},{4,2},{5,7},{6,4},{7,1},{8,14},{9,11},{10,... | collective-permute-start | bytes 589832 | tf_op jit(solution)/shard_map/ppermute | solution.py:54
  83.3 2.5 %collective-permute-start.33 = (bf16[64,1408]{1,0:T(8,128)(2,1)S(1)}, bf16[64,1408]{1,0:T(8,128)(2,1)S(1)}, u32[]{:S(2)}, u32[]{:S(2)}) collective-permute-start(bf16[64,1408]{1,0:T(8,128)(2,1)S(1)} %get-tuple-element.75), channel_id=1, source_target_pairs={{0,24},{1,97},{2,26},{3,99},{4,28},{5,101},{6,30},{7,103},{8,0},{9... | collective-permute-start | bytes 540680 | tf_op jit(solution)/shard_map/ppermute | solution.py:54
  85.8 1.3 collective-permute-start.35
  87.1 1.4 %collective-permute-done.19.refs_1_ = bf16[64,1536]{1,0:T(8,128)(2,1)S(1)} collective-permute-done((bf16[64,1536]{1,0:T(8,128)(2,1)S(1)}, bf16[64,1536]{1,0:T(8,128)(2,1)S(1)}, u32[]{:S(2)}, u32[]{:S(2)}) %collective-permute-start.19) | collective-permute-done | bytes 196640 | tf_op jit(solution)/shard_map/ppermute | solution.py:54
  89.0 1.5 %collective-permute-start.27 = (bf16[64,1536]{1,0:T(8,128)(2,1)S(1)}, bf16[64,1536]{1,0:T(8,128)(2,1)S(1)}, u32[]{:S(2)}, u32[]{:S(2)}) collective-permute-start(bf16[64,1536]{1,0:T(8,128)(2,1)S(1)} %shard_map.139.r0.refs_6_), channel_id=1, source_target_pairs={{0,2},{1,3},{2,0},{3,1},{4,6},{5,7},{6,4},{7,5},{8,10},{9,11},{10,... | collective-permute-start | bytes 589832 | tf_op jit(solution)/shard_map/ppermute | solution.py:54
  90.5 3.1 %collective-permute-done.34.refs_2_ = bf16[64,1408]{1,0:T(8,128)(2,1)S(1)} collective-permute-done((bf16[64,1408]{1,0:T(8,128)(2,1)S(1)}, bf16[64,1408]{1,0:T(8,128)(2,1)S(1)}, u32[]{:S(2)}, u32[]{:S(2)}) %collective-permute-start.34) | collective-permute-done | bytes 180256 | tf_op jit(solution)/shard_map/ppermute | solution.py:54
  94.2 3.9 %collective-permute-start.28 = (bf16[64,1536]{1,0:T(8,128)(2,1)S(1)}, bf16[64,1536]{1,0:T(8,128)(2,1)S(1)}, u32[]{:S(2)}, u32[]{:S(2)}) collective-permute-start(bf16[64,1536]{1,0:T(8,128)(2,1)S(1)} %shard_map.139.r0.refs_6_), channel_id=1, source_target_pairs={{0,1},{1,0},{2,3},{3,2},{4,5},{5,4},{6,7},{7,6},{8,9},{9,8},{10,11... | collective-permute-start | bytes 589832 | tf_op jit(solution)/shard_map/ppermute | solution.py:54
  98.7 4.8 %collective-permute-start.38 = (bf16[64,1408]{1,0:T(8,128)(2,1)S(1)}, bf16[64,1408]{1,0:T(8,128)(2,1)S(1)}, u32[]{:S(2)}, u32[]{:S(2)}) collective-permute-start(bf16[64,1408]{1,0:T(8,128)(2,1)S(1)} %collective-permute-done.36.refs_1_.r1), channel_id=1, source_target_pairs={{0,1},{1,0},{2,3},{3,2},{4,5},{5,4},{6,7},{7,6},{8,9},{9,8},{10,11... | collective-permute-start | bytes 540680 | tf_op jit(solution)/shard_map/ppermute | solution.py:54
  103.6 2.9 %shard_map.140 = (f32[128,1408]{1,0:T(8,128)S(1)}, bf16[128,1408]{1,0:T(8,128)(2,1)S(1)}) custom-call(bf16[64,1536]{1,0:T(8,128)(2,1)S(1)} %shard_map.139.r0.refs_6_, bf16[64,1536]{1,0:T(8,128)(2,1)S(1)} %collective-permute-done.27.r1, bf16[64,1536]{1,0:T(8,128)(2,1)S(1)} %collective-permute-done.28.r2, bf16[64,1536]{1,0:T(8,128)(2,1)S(1)} %collective-permute-done.29.r3, ...), custom_call_target="tpu_custom_call" | custom-call | flops 1 | bytes 1 | tf_op jit(solution)/shard_map/pallas_call | solution.py:75
  106.6 2.9 %shard_map.145 = (f32[128,1408]{1,0:T(8,128)S(1)}, bf16[128,1408]{1,0:T(8,128)(2,1)S(1)}) custom-call(bf16[64,1408]{1,0:T(8,128)(2,1)S(1)} %shard_map.144.refs_0_.r0, bf16[64,1408]{1,0:T(8,128)(2,1)S(1)} %collective-permute-done.36.refs_1_.r1, bf16[64,1408]{1,0:T(8,128)(2,1)S(1)} %collective-permute-done.37.refs_2_.r2, ...), custom_call_target="tpu_custom_call" | custom-call | flops 1 | bytes 1 | tf_op jit(solution)/shard_map/pallas_call | solution.py:75
  110.3 1.1 collective-permute-done.39.got_ref
  111.9 8.4 %collective-permute-done.31.got_ref = bf16[128,1408]{1,0:T(8,128)(2,1)S(1)} collective-permute-done((bf16[128,1408]{1,0:T(8,128)(2,1)S(1)}, bf16[128,1408]{1,0:T(8,128)(2,1)S(1)}, u32[]{:S(2)}, u32[]{:S(2)}) %collective-permute-start.31) | collective-permute-done | bytes 360480 | tf_op jit(solution)/shard_map/ppermute | solution.py:54
  120.4 1.3 collective-permute-start.32
  121.7 6.3 %collective-permute-done.40.got_ref = bf16[128,1408]{1,0:T(8,128)(2,1)S(1)} collective-permute-done((bf16[128,1408]{1,0:T(8,128)(2,1)S(1)}, bf16[128,1408]{1,0:T(8,128)(2,1)S(1)}, u32[]{:S(2)}, u32[]{:S(2)}) %collective-permute-start.40) | collective-permute-done | bytes 360480 | tf_op jit(solution)/shard_map/ppermute | solution.py:54
  128.1 0.9 collective-permute-start.41
  129.0 2.1 %shard_map.143 = (f32[256,1408]{1,0:T(8,128)}, f32[1,256]{1,0:T(1,128)}) custom-call(s32[1]{0:T(128)} %bitcast.mine.refs_0_, bf16[256,1408]{1,0:T(8,128)(2,1)S(1)} %copy-done.2, f32[1408]{0:T(1024)S(1)} %copy-done.8, bf16[64,1536]{1,0:T(8,128)(2,1)S(1)} %shard_map.139.r0.refs_6_, bf16[64,1536]{1,0:T(8,128)(2,1)S(1)} %collective-permute-done.27.r1, ...), custom_call_target="tpu_custom_call" | custom-call | flops 1 | bytes 1 | tf_op jit(solution)/shard_map/pallas_call | solution.py:75
  131.1 2.1 %shard_map.148 = f32[256,1408]{1,0:T(8,128)} custom-call(s32[1]{0:T(128)} %bitcast.mine.refs_0_, bf16[256,1408]{1,0:T(8,128)(2,1)S(1)} %copy-done.4, f32[1408]{0:T(1024)S(1)} %copy-done.10, bf16[64,1408]{1,0:T(8,128)(2,1)S(1)} %shard_map.144.refs_0_.r0, bf16[64,1408]{1,0:T(8,128)(2,1)S(1)} %collective-permute-done.36.refs_1_.r1, ...), custom_call_target="tpu_custom_call" | custom-call | flops 1 | bytes 1 | tf_op jit(solution)/shard_map/pallas_call | solution.py:75
  (102 shorter events, 7.7 us)
Async XLA Ops:
  0.7 13.5 %slice-start = ((s8[4325376]{0:T(1024)(128)(4,1)}), s8[4194304]{0:T(1024)(128)(4,1)S(1)}, s32[]{:S(2)}) async-start(s8[4325376]{0:T(1024)(128)(4,1)} %bitcast.2), calls=%async_computation | async-start | bytes 8388608
  5.0 9.2 %copy-start.8 = (f32[1408]{0:T(1024)S(1)}, f32[1408]{0:T(1024)}, u32[]{:S(2)}) copy-start(f32[1408]{0:T(1024)} %gain_ref.4) | copy-start | bytes 16900
  9.5 2.8 %collective-permute-start = (bf16[128,1408]{1,0:T(8,128)(2,1)S(1)}, bf16[128,1408]{1,0:T(8,128)(2,1)S(1)}, u32[]{:S(2)}, u32[]{:S(2)}) collective-permute-start(bf16[128,1408]{1,0:T(8,128)(2,1)S(1)} %get-tuple-element.44), channel_id=1, source_target_pairs={{0,1},{1,0},{2,3},{3,2},{4,5},{5,4},{6,7},{7,6},{8,9},{9,8},{10,11... | collective-permute-start | bytes 1081352 | tf_op jit(solution)/shard_map/ppermute | solution.py:54
  12.4 6.4 %collective-permute-start.1 = (bf16[64,1408]{1,0:T(8,128)(2,1)S(1)}, bf16[64,1408]{1,0:T(8,128)(2,1)S(1)}, u32[]{:S(2)}, u32[]{:S(2)}) collective-permute-start(bf16[64,1408]{1,0:T(8,128)(2,1)S(1)} %get-tuple-element.45.refs_5_), channel_id=1, source_target_pairs={{0,2},{1,3},{2,0},{3,1},{4,6},{5,7},{6,4},{7,5},{8,10},{9,11},{10,... | collective-permute-start | bytes 540680 | tf_op jit(solution)/shard_map/ppermute | solution.py:54
  19.2 17.0 %copy-start.7 = (f32[1408]{0:T(1024)S(1)}, f32[1408]{0:T(1024)}, u32[]{:S(2)}) copy-start(f32[1408]{0:T(1024)} %refs_4_.7) | copy-start | bytes 16900
  19.2 12.0 %collective-permute-start.2 = (bf16[128,1408]{1,0:T(8,128)(2,1)S(1)}, bf16[128,1408]{1,0:T(8,128)(2,1)S(1)}, u32[]{:S(2)}, u32[]{:S(2)}) collective-permute-start(bf16[128,1408]{1,0:T(8,128)(2,1)S(1)} %shard_map.125), channel_id=1, source_target_pairs={{0,1},{1,0},{2,3},{3,2},{4,5},{5,4},{6,7},{7,6},{8,9},{9,8},{10,11... | collective-permute-start | bytes 1081352 | tf_op jit(solution)/shard_map/ppermute | solution.py:54
  20.2 6.1 %collective-permute-start.6 = (bf16[64,1408]{1,0:T(8,128)(2,1)S(1)}, bf16[64,1408]{1,0:T(8,128)(2,1)S(1)}, u32[]{:S(2)}, u32[]{:S(2)}) collective-permute-start(bf16[64,1408]{1,0:T(8,128)(2,1)S(1)} %get-tuple-element.49.refs_1_.refs_0_), channel_id=1, source_target_pairs={{0,16},{1,65},{2,18},{3,67},{4,20},{5,69},{6,22},{7,71},{8,24},{9,... | collective-permute-start | bytes 540680 | tf_op jit(solution)/shard_map/ppermute | solution.py:54
  23.1 5.5 %collective-permute-start.5 = (bf16[64,1408]{1,0:T(8,128)(2,1)S(1)}, bf16[64,1408]{1,0:T(8,128)(2,1)S(1)}, u32[]{:S(2)}, u32[]{:S(2)}) collective-permute-start(bf16[64,1408]{1,0:T(8,128)(2,1)S(1)} %get-tuple-element.49.refs_1_.refs_0_), channel_id=1, source_target_pairs={{0,24},{1,97},{2,26},{3,99},{4,28},{5,101},{6,30},{7,103},{8,0},{9... | collective-permute-start | bytes 540680 | tf_op jit(solution)/shard_map/ppermute | solution.py:54
  23.9 7.4 %collective-permute-start.4 = (bf16[64,1408]{1,0:T(8,128)(2,1)S(1)}, bf16[64,1408]{1,0:T(8,128)(2,1)S(1)}, u32[]{:S(2)}, u32[]{:S(2)}) collective-permute-start(bf16[64,1408]{1,0:T(8,128)(2,1)S(1)} %get-tuple-element.49.refs_1_.refs_0_), channel_id=1, source_target_pairs={{0,8},{1,33},{2,10},{3,35},{4,12},{5,37},{6,14},{7,39},{8,16},{9,4... | collective-permute-start | bytes 540680 | tf_op jit(solution)/shard_map/ppermute | solution.py:54
  28.6 14.4 %collective-permute-start.10 = (bf16[128,1408]{1,0:T(8,128)(2,1)S(1)}, bf16[128,1408]{1,0:T(8,128)(2,1)S(1)}, u32[]{:S(2)}, u32[]{:S(2)}) collective-permute-start(bf16[128,1408]{1,0:T(8,128)(2,1)S(1)} %shard_map.128.refs_6_.refs_3_), channel_id=1, source_target_pairs={{0,96},{1,25},{2,98},{3,27},{4,100},{5,29},{6,102},{7,31},{8,104},... | collective-permute-start | bytes 1081352 | tf_op jit(solution)/shard_map/ppermute | solution.py:54
  31.3 11.8 %collective-permute-start.9 = (bf16[128,1408]{1,0:T(8,128)(2,1)S(1)}, bf16[128,1408]{1,0:T(8,128)(2,1)S(1)}, u32[]{:S(2)}, u32[]{:S(2)}) collective-permute-start(bf16[128,1408]{1,0:T(8,128)(2,1)S(1)} %shard_map.127.refs_5_.refs_2_), channel_id=1, source_target_pairs={{0,32},{1,9},{2,34},{3,11},{4,36},{5,13},{6,38},{7,15},{8,40},{9,1... | collective-permute-start | bytes 1081352 | tf_op jit(solution)/shard_map/ppermute | solution.py:54
  31.4 4.8 %collective-permute-start.3 = (bf16[64,1408]{1,0:T(8,128)(2,1)S(1)}, bf16[64,1408]{1,0:T(8,128)(2,1)S(1)}, u32[]{:S(2)}, u32[]{:S(2)}) collective-permute-start(bf16[64,1408]{1,0:T(8,128)(2,1)S(1)} %get-tuple-element.51.refs_2_), channel_id=1, source_target_pairs={{0,2},{1,3},{2,0},{3,1},{4,6},{5,7},{6,4},{7,5},{8,10},{9,11},{10,... | collective-permute-start | bytes 540680 | tf_op jit(solution)/shard_map/ppermute | solution.py:54
  32.9 11.6 %collective-permute-start.12 = (bf16[128,1408]{1,0:T(8,128)(2,1)S(1)}, bf16[128,1408]{1,0:T(8,128)(2,1)S(1)}, u32[]{:S(2)}, u32[]{:S(2)}) collective-permute-start(bf16[128,1408]{1,0:T(8,128)(2,1)S(1)} %shard_map.128.refs_6_.refs_3_), channel_id=1, source_target_pairs={{0,32},{1,9},{2,34},{3,11},{4,36},{5,13},{6,38},{7,15},{8,40},{9,1... | collective-permute-start | bytes 1081352 | tf_op jit(solution)/shard_map/ppermute | solution.py:54
  36.5 8.0 %collective-permute-start.7 = (bf16[64,1408]{1,0:T(8,128)(2,1)S(1)}, bf16[64,1408]{1,0:T(8,128)(2,1)S(1)}, u32[]{:S(2)}, u32[]{:S(2)}) collective-permute-start(bf16[64,1408]{1,0:T(8,128)(2,1)S(1)} %get-tuple-element.52.refs_0_), channel_id=1, source_target_pairs={{0,2},{1,7},{2,4},{3,1},{4,6},{5,3},{6,0},{7,5},{8,10},{9,15},{10,... | collective-permute-start | bytes 540680 | tf_op jit(solution)/shard_map/ppermute | solution.py:54
  40.2 10.2 %collective-permute-start.13 = (bf16[128,1408]{1,0:T(8,128)(2,1)S(1)}, bf16[128,1408]{1,0:T(8,128)(2,1)S(1)}, u32[]{:S(2)}, u32[]{:S(2)}) collective-permute-start(bf16[128,1408]{1,0:T(8,128)(2,1)S(1)} %shard_map.127.refs_5_.refs_2_), channel_id=1, source_target_pairs={{0,96},{1,25},{2,98},{3,27},{4,100},{5,29},{6,102},{7,31},{8,104},... | collective-permute-start | bytes 1081352 | tf_op jit(solution)/shard_map/ppermute | solution.py:54
  43.1 8.2 %collective-permute-start.15 = (bf16[128,1408]{1,0:T(8,128)(2,1)S(1)}, bf16[128,1408]{1,0:T(8,128)(2,1)S(1)}, u32[]{:S(2)}, u32[]{:S(2)}) collective-permute-start(bf16[128,1408]{1,0:T(8,128)(2,1)S(1)} %collective-permute-done.10.refs_2_.refs_7_), channel_id=1, source_target_pairs={{0,96},{1,25},{2,98},{3,27},{4,100},{5,29},{6,102},{7,31},{8,104},... | collective-permute-start | bytes 1081352 | tf_op jit(solution)/shard_map/ppermute | solution.py:54
  43.1 8.2 %collective-permute-start.14 = (bf16[128,1408]{1,0:T(8,128)(2,1)S(1)}, bf16[128,1408]{1,0:T(8,128)(2,1)S(1)}, u32[]{:S(2)}, u32[]{:S(2)}) collective-permute-start(bf16[128,1408]{1,0:T(8,128)(2,1)S(1)} %collective-permute-done.9.refs_1_.refs_4_), channel_id=1, source_target_pairs={{0,32},{1,9},{2,34},{3,11},{4,36},{5,13},{6,38},{7,15},{8,40},{9,1... | collective-permute-start | bytes 1081352 | tf_op jit(solution)/shard_map/ppermute | solution.py:54
  44.6 5.9 %collective-permute-start.8 = (bf16[64,1408]{1,0:T(8,128)(2,1)S(1)}, bf16[64,1408]{1,0:T(8,128)(2,1)S(1)}, u32[]{:S(2)}, u32[]{:S(2)}) collective-permute-start(bf16[64,1408]{1,0:T(8,128)(2,1)S(1)} %get-tuple-element.52.refs_0_), channel_id=1, source_target_pairs={{0,6},{1,3},{2,0},{3,5},{4,2},{5,7},{6,4},{7,1},{8,14},{9,11},{10,... | collective-permute-start | bytes 540680 | tf_op jit(solution)/shard_map/ppermute | solution.py:54
  44.6 6.7 %collective-permute-start.11 = (bf16[64,1408]{1,0:T(8,128)(2,1)S(1)}, bf16[64,1408]{1,0:T(8,128)(2,1)S(1)}, u32[]{:S(2)}, u32[]{:S(2)}) collective-permute-start(bf16[64,1408]{1,0:T(8,128)(2,1)S(1)} %shard_map.130), channel_id=1, source_target_pairs={{0,2},{1,7},{2,4},{3,1},{4,6},{5,3},{6,0},{7,5},{8,10},{9,15},{10,... | collective-permute-start | bytes 540680 | tf_op jit(solution)/shard_map/ppermute | solution.py:54
  51.4 5.8 %collective-permute-start.16 = (bf16[256,1408]{1,0:T(8,128)(2,1)S(1)}, bf16[256,1408]{1,0:T(8,128)(2,1)S(1)}, u32[]{:S(2)}, u32[]{:S(2)}) collective-permute-start(bf16[256,1408]{1,0:T(8,128)(2,1)S(1)} %shard_map.131.refs_0_), channel_id=1, source_target_pairs={{0,1},{1,0},{2,3},{3,2},{4,5},{5,4},{6,7},{7,6},{8,9},{9,8},{10,11... | collective-permute-start | bytes 2162696 | tf_op jit(solution)/shard_map/ppermute | solution.py:54
  64.2 5.7 %collective-permute-start.17 = (bf16[256,1536]{1,0:T(8,128)(2,1)S(1)}, bf16[256,1536]{1,0:T(8,128)(2,1)S(1)}, u32[]{:S(2)}, u32[]{:S(2)}) collective-permute-start(bf16[256,1536]{1,0:T(8,128)(2,1)S(1)} %get-tuple-element.57), channel_id=1, source_target_pairs={{0,1},{1,0},{2,3},{3,2},{4,5},{5,4},{6,7},{7,6},{8,9},{9,8},{10,11... | collective-permute-start | bytes 2359304 | tf_op jit(solution)/shard_map/ppermute | solution.py:54
  64.6 7.0 %collective-permute-start.21 = (bf16[128,1408]{1,0:T(8,128)(2,1)S(1)}, bf16[128,1408]{1,0:T(8,128)(2,1)S(1)}, u32[]{:S(2)}, u32[]{:S(2)}) collective-permute-start(bf16[128,1408]{1,0:T(8,128)(2,1)S(1)} %get-tuple-element.65), channel_id=1, source_target_pairs={{0,96},{1,25},{2,98},{3,27},{4,100},{5,29},{6,102},{7,31},{8,104},... | collective-permute-start | bytes 1081352 | tf_op jit(solution)/shard_map/ppermute | solution.py:54
  67.2 7.9 %collective-permute-start.25 = (bf16[128,1408]{1,0:T(8,128)(2,1)S(1)}, bf16[128,1408]{1,0:T(8,128)(2,1)S(1)}, u32[]{:S(2)}, u32[]{:S(2)}) collective-permute-start(bf16[128,1408]{1,0:T(8,128)(2,1)S(1)} %get-tuple-element.69), channel_id=1, source_target_pairs={{0,32},{1,9},{2,34},{3,11},{4,36},{5,13},{6,38},{7,15},{8,40},{9,1... | collective-permute-start | bytes 1081352 | tf_op jit(solution)/shard_map/ppermute | solution.py:54
  67.2 14.4 %collective-permute-start.23 = (bf16[128,1408]{1,0:T(8,128)(2,1)S(1)}, bf16[128,1408]{1,0:T(8,128)(2,1)S(1)}, u32[]{:S(2)}, u32[]{:S(2)}) collective-permute-start(bf16[128,1408]{1,0:T(8,128)(2,1)S(1)} %get-tuple-element.66), channel_id=1, source_target_pairs={{0,96},{1,25},{2,98},{3,27},{4,100},{5,29},{6,102},{7,31},{8,104},... | collective-permute-start | bytes 1081352 | tf_op jit(solution)/shard_map/ppermute | solution.py:54
  69.9 13.2 %collective-permute-start.24 = (bf16[128,1408]{1,0:T(8,128)(2,1)S(1)}, bf16[128,1408]{1,0:T(8,128)(2,1)S(1)}, u32[]{:S(2)}, u32[]{:S(2)}) collective-permute-start(bf16[128,1408]{1,0:T(8,128)(2,1)S(1)} %get-tuple-element.67), channel_id=1, source_target_pairs={{0,32},{1,9},{2,34},{3,11},{4,36},{5,13},{6,38},{7,15},{8,40},{9,1... | collective-permute-start | bytes 1081352 | tf_op jit(solution)/shard_map/ppermute | solution.py:54
  71.7 11.4 %copy-start.13 = (f32[256,1408]{1,0:T(8,128)S(1)}, f32[256,1408]{1,0:T(8,128)}, u32[]{:S(2)}) copy-start(f32[256,1408]{1,0:T(8,128)} %copy-done.12) | copy-start | bytes 4325380
  71.7 11.4 %collective-permute-start.22 = (bf16[128,1408]{1,0:T(8,128)(2,1)S(1)}, bf16[128,1408]{1,0:T(8,128)(2,1)S(1)}, u32[]{:S(2)}, u32[]{:S(2)}) collective-permute-start(bf16[128,1408]{1,0:T(8,128)(2,1)S(1)} %shard_map.136), channel_id=1, source_target_pairs={{0,96},{1,25},{2,98},{3,27},{4,100},{5,29},{6,102},{7,31},{8,104},... | collective-permute-start | bytes 1081352 | tf_op jit(solution)/shard_map/ppermute | solution.py:54
  75.2 7.9 %collective-permute-start.26 = (bf16[128,1408]{1,0:T(8,128)(2,1)S(1)}, bf16[128,1408]{1,0:T(8,128)(2,1)S(1)}, u32[]{:S(2)}, u32[]{:S(2)}) collective-permute-start(bf16[128,1408]{1,0:T(8,128)(2,1)S(1)} %shard_map.137), channel_id=1, source_target_pairs={{0,32},{1,9},{2,34},{3,11},{4,36},{5,13},{6,38},{7,15},{8,40},{9,1... | collective-permute-start | bytes 1081352 | tf_op jit(solution)/shard_map/ppermute | solution.py:54
  75.3 6.1 %collective-permute-start.18 = (bf16[64,1536]{1,0:T(8,128)(2,1)S(1)}, bf16[64,1536]{1,0:T(8,128)(2,1)S(1)}, u32[]{:S(2)}, u32[]{:S(2)}) collective-permute-start(bf16[64,1536]{1,0:T(8,128)(2,1)S(1)} %get-tuple-element.59.refs_2_), channel_id=1, source_target_pairs={{0,6},{1,3},{2,0},{3,5},{4,2},{5,7},{6,4},{7,1},{8,14},{9,11},{10,... | collective-permute-start | bytes 589832 | tf_op jit(solution)/shard_map/ppermute | solution.py:54
  81.6 5.5 %collective-permute-start.20 = (bf16[64,1536]{1,0:T(8,128)(2,1)S(1)}, bf16[64,1536]{1,0:T(8,128)(2,1)S(1)}, u32[]{:S(2)}, u32[]{:S(2)}) collective-permute-start(bf16[64,1536]{1,0:T(8,128)(2,1)S(1)} %get-tuple-element.61), channel_id=1, source_target_pairs={{0,2},{1,7},{2,4},{3,1},{4,6},{5,3},{6,0},{7,5},{8,10},{9,15},{10,... | collective-permute-start | bytes 589832 | tf_op jit(solution)/shard_map/ppermute | solution.py:54
  81.6 6.8 %collective-permute-start.19 = (bf16[64,1536]{1,0:T(8,128)(2,1)S(1)}, bf16[64,1536]{1,0:T(8,128)(2,1)S(1)}, u32[]{:S(2)}, u32[]{:S(2)}) collective-permute-start(bf16[64,1536]{1,0:T(8,128)(2,1)S(1)} %get-tuple-element.60.refs_5_), channel_id=1, source_target_pairs={{0,6},{1,3},{2,0},{3,5},{4,2},{5,7},{6,4},{7,1},{8,14},{9,11},{10,... | collective-permute-start | bytes 589832 | tf_op jit(solution)/shard_map/ppermute | solution.py:54
  83.3 7.2 %collective-permute-start.33 = (bf16[64,1408]{1,0:T(8,128)(2,1)S(1)}, bf16[64,1408]{1,0:T(8,128)(2,1)S(1)}, u32[]{:S(2)}, u32[]{:S(2)}) collective-permute-start(bf16[64,1408]{1,0:T(8,128)(2,1)S(1)} %get-tuple-element.75), channel_id=1, source_target_pairs={{0,24},{1,97},{2,26},{3,99},{4,28},{5,101},{6,30},{7,103},{8,0},{9... | collective-permute-start | bytes 540680 | tf_op jit(solution)/shard_map/ppermute | solution.py:54
  85.8 7.8 %collective-permute-start.34 = (bf16[64,1408]{1,0:T(8,128)(2,1)S(1)}, bf16[64,1408]{1,0:T(8,128)(2,1)S(1)}, u32[]{:S(2)}, u32[]{:S(2)}) collective-permute-start(bf16[64,1408]{1,0:T(8,128)(2,1)S(1)} %get-tuple-element.76), channel_id=1, source_target_pairs={{0,8},{1,33},{2,10},{3,35},{4,12},{5,37},{6,14},{7,39},{8,16},{9,4... | collective-permute-start | bytes 540680 | tf_op jit(solution)/shard_map/ppermute | solution.py:54
  85.8 7.8 %collective-permute-start.35 = (bf16[64,1408]{1,0:T(8,128)(2,1)S(1)}, bf16[64,1408]{1,0:T(8,128)(2,1)S(1)}, u32[]{:S(2)}, u32[]{:S(2)}) collective-permute-start(bf16[64,1408]{1,0:T(8,128)(2,1)S(1)} %get-tuple-element.77), channel_id=1, source_target_pairs={{0,16},{1,65},{2,18},{3,67},{4,20},{5,69},{6,22},{7,71},{8,24},{9,... | collective-permute-start | bytes 540680 | tf_op jit(solution)/shard_map/ppermute | solution.py:54
  89.0 9.1 %collective-permute-start.27 = (bf16[64,1536]{1,0:T(8,128)(2,1)S(1)}, bf16[64,1536]{1,0:T(8,128)(2,1)S(1)}, u32[]{:S(2)}, u32[]{:S(2)}) collective-permute-start(bf16[64,1536]{1,0:T(8,128)(2,1)S(1)} %shard_map.139.r0.refs_6_), channel_id=1, source_target_pairs={{0,2},{1,3},{2,0},{3,1},{4,6},{5,7},{6,4},{7,5},{8,10},{9,11},{10,... | collective-permute-start | bytes 589832 | tf_op jit(solution)/shard_map/ppermute | solution.py:54
  93.6 9.9 %copy-start.6 = (f32[256,1536]{1,0:T(8,128)S(1)}, f32[256,1536]{1,0:T(8,128)}, u32[]{:S(2)}) copy-start(f32[256,1536]{1,0:T(8,128)} %copy-done.5) | copy-start | bytes 4718596
  94.1 4.6 %collective-permute-start.36 = (bf16[64,1408]{1,0:T(8,128)(2,1)S(1)}, bf16[64,1408]{1,0:T(8,128)(2,1)S(1)}, u32[]{:S(2)}, u32[]{:S(2)}) collective-permute-start(bf16[64,1408]{1,0:T(8,128)(2,1)S(1)} %shard_map.144.refs_0_.r0), channel_id=1, source_target_pairs={{0,2},{1,3},{2,0},{3,1},{4,6},{5,7},{6,4},{7,5},{8,10},{9,11},{10,... | collective-permute-start | bytes 540680 | tf_op jit(solution)/shard_map/ppermute | solution.py:54
  94.2 9.3 %collective-permute-start.28 = (bf16[64,1536]{1,0:T(8,128)(2,1)S(1)}, bf16[64,1536]{1,0:T(8,128)(2,1)S(1)}, u32[]{:S(2)}, u32[]{:S(2)}) collective-permute-start(bf16[64,1536]{1,0:T(8,128)(2,1)S(1)} %shard_map.139.r0.refs_6_), channel_id=1, source_target_pairs={{0,1},{1,0},{2,3},{3,2},{4,5},{5,4},{6,7},{7,6},{8,9},{9,8},{10,11... | collective-permute-start | bytes 589832 | tf_op jit(solution)/shard_map/ppermute | solution.py:54
  98.1 5.4 %collective-permute-start.29 = (bf16[64,1536]{1,0:T(8,128)(2,1)S(1)}, bf16[64,1536]{1,0:T(8,128)(2,1)S(1)}, u32[]{:S(2)}, u32[]{:S(2)}) collective-permute-start(bf16[64,1536]{1,0:T(8,128)(2,1)S(1)} %collective-permute-done.27.r1), channel_id=1, source_target_pairs={{0,1},{1,0},{2,3},{3,2},{4,5},{5,4},{6,7},{7,6},{8,9},{9,8},{10,11... | collective-permute-start | bytes 589832 | tf_op jit(solution)/shard_map/ppermute | solution.py:54
  98.2 8.4 %collective-permute-start.37 = (bf16[64,1408]{1,0:T(8,128)(2,1)S(1)}, bf16[64,1408]{1,0:T(8,128)(2,1)S(1)}, u32[]{:S(2)}, u32[]{:S(2)}) collective-permute-start(bf16[64,1408]{1,0:T(8,128)(2,1)S(1)} %shard_map.144.refs_0_.r0), channel_id=1, source_target_pairs={{0,1},{1,0},{2,3},{3,2},{4,5},{5,4},{6,7},{7,6},{8,9},{9,8},{10,11... | collective-permute-start | bytes 540680 | tf_op jit(solution)/shard_map/ppermute | solution.py:54
  98.7 7.9 %collective-permute-start.38 = (bf16[64,1408]{1,0:T(8,128)(2,1)S(1)}, bf16[64,1408]{1,0:T(8,128)(2,1)S(1)}, u32[]{:S(2)}, u32[]{:S(2)}) collective-permute-start(bf16[64,1408]{1,0:T(8,128)(2,1)S(1)} %collective-permute-done.36.refs_1_.r1), channel_id=1, source_target_pairs={{0,1},{1,0},{2,3},{3,2},{4,5},{5,4},{6,7},{7,6},{8,9},{9,8},{10,11... | collective-permute-start | bytes 540680 | tf_op jit(solution)/shard_map/ppermute | solution.py:54
  106.5 3.6 %collective-permute-start.30 = (bf16[128,1408]{1,0:T(8,128)(2,1)S(1)}, bf16[128,1408]{1,0:T(8,128)(2,1)S(1)}, u32[]{:S(2)}, u32[]{:S(2)}) collective-permute-start(bf16[128,1408]{1,0:T(8,128)(2,1)S(1)} %get-tuple-element.73.refs_7_), channel_id=1, source_target_pairs={{0,1},{1,0},{2,3},{3,2},{4,5},{5,4},{6,7},{7,6},{8,9},{9,8},{10,11... | collective-permute-start | bytes 1081352 | tf_op jit(solution)/shard_map/ppermute | solution.py:54
  109.5 1.9 %collective-permute-start.39 = (bf16[128,1408]{1,0:T(8,128)(2,1)S(1)}, bf16[128,1408]{1,0:T(8,128)(2,1)S(1)}, u32[]{:S(2)}, u32[]{:S(2)}) collective-permute-start(bf16[128,1408]{1,0:T(8,128)(2,1)S(1)} %get-tuple-element.81), channel_id=1, source_target_pairs={{0,1},{1,0},{2,3},{3,2},{4,5},{5,4},{6,7},{7,6},{8,9},{9,8},{10,11... | collective-permute-start | bytes 1081352 | tf_op jit(solution)/shard_map/ppermute | solution.py:54
  110.2 10.1 %collective-permute-start.31 = (bf16[128,1408]{1,0:T(8,128)(2,1)S(1)}, bf16[128,1408]{1,0:T(8,128)(2,1)S(1)}, u32[]{:S(2)}, u32[]{:S(2)}) collective-permute-start(bf16[128,1408]{1,0:T(8,128)(2,1)S(1)} %shard_map.141.own_ref), channel_id=1, source_target_pairs={{0,2},{1,3},{2,0},{3,1},{4,6},{5,7},{6,4},{7,5},{8,10},{9,11},{10,... | collective-permute-start | bytes 1081352 | tf_op jit(solution)/shard_map/ppermute | solution.py:54
  111.4 16.5 %collective-permute-start.40 = (bf16[128,1408]{1,0:T(8,128)(2,1)S(1)}, bf16[128,1408]{1,0:T(8,128)(2,1)S(1)}, u32[]{:S(2)}, u32[]{:S(2)}) collective-permute-start(bf16[128,1408]{1,0:T(8,128)(2,1)S(1)} %shard_map.146.own_ref), channel_id=1, source_target_pairs={{0,2},{1,3},{2,0},{3,1},{4,6},{5,7},{6,4},{7,5},{8,10},{9,11},{10,... | collective-permute-start | bytes 1081352 | tf_op jit(solution)/shard_map/ppermute | solution.py:54
  120.4 10.8 %copy-start.10 = (f32[1408]{0:T(1024)S(1)}, f32[1408]{0:T(1024)}, u32[]{:S(2)}) copy-start(f32[1408]{0:T(1024)} %gain_ref.5) | copy-start | bytes 16900
  120.4 8.6 %collective-permute-start.32 = (bf16[128,1408]{1,0:T(8,128)(2,1)S(1)}, bf16[128,1408]{1,0:T(8,128)(2,1)S(1)}, u32[]{:S(2)}, u32[]{:S(2)}) collective-permute-start(bf16[128,1408]{1,0:T(8,128)(2,1)S(1)} %shard_map.142.own_ref), channel_id=1, source_target_pairs={{0,1},{1,0},{2,3},{3,2},{4,5},{5,4},{6,7},{7,6},{8,9},{9,8},{10,11... | collective-permute-start | bytes 1081352 | tf_op jit(solution)/shard_map/ppermute | solution.py:54
  128.1 3.0 %collective-permute-start.41 = (bf16[128,1408]{1,0:T(8,128)(2,1)S(1)}, bf16[128,1408]{1,0:T(8,128)(2,1)S(1)}, u32[]{:S(2)}, u32[]{:S(2)}) collective-permute-start(bf16[128,1408]{1,0:T(8,128)(2,1)S(1)} %shard_map.147.own_ref), channel_id=1, source_target_pairs={{0,1},{1,0},{2,3},{3,2},{4,5},{5,4},{6,7},{7,6},{8,9},{9,8},{10,11... | collective-permute-start | bytes 1081352 | tf_op jit(solution)/shard_map/ppermute | solution.py:54
  (12 other events, 50.7 us)
